TPU v7x, 512 devices: a whole 4x4x16 slice. The times are simulated.
512 devices in a mesh: dp: 64 (over y, z_lo, core), score: 8 (over z_hi, x).
Axes of the slice: x: 4, y: 4, z: 16 (z_hi: 2, z_lo: 8; z = z_hi * 8 + z_lo), core: 2. Of those that a mesh axis runs over, the one named last changes fastest.
Arguments:
- hidden_in: bfloat16 [65536, 8192], P(('score', 'dp')), may hold values from -30 to 30
- norm_gain: float32 [8192], replicated, may hold values from 0.1 to 1.9
- value_weight: bfloat16 [8192, 512], P('dp'), may hold values from -0.0625 to 0.0625
- input_proj: bfloat16 [8192, 64], P('dp'), may hold values from -0.0625 to 0.0625
- value_grad: bfloat16 [65536, 512], P(('score', 'dp')), may hold values from -6 to 6
- output_proj: bfloat16 [512, 64], replicated, may hold values from -0.25 to 0.25
- doc_ids: int32 [65536], P(('score', 'dp')), may hold values from 0 to 63, as said below
- queries: bfloat16 [8192, 4096], P(('dp', 'score')), may hold values from -0.0020599365 to 0.0020599365
Outputs:
- values_out: bfloat16 [65536, 512], P(('score', 'dp'))
- hidden_grad: bfloat16 [65536, 8192], P(('score', 'dp'))
- scores: float32 [64, 8192], P('score', 'dp')
Inputs may be any that keep to these rules, and one draw needn't show every extreme that they name: `doc_ids`: document numbers never fall along the tokens; every document holds 1 to 8192 tokens and one holds exactly 8192.
All inputs are finite; a program needn't handle non-finite values.
Results may differ from a plain program's by a relative error of at most 0.0049.
Values may be sent and summed in bfloat16 or wider, within the bound.
No kernel may reach another device: no remote copies, remote signals or barrier semaphores. Data moves between devices by JAX's collectives and lax.ppermute only.
A program may use at most 64 MiB of HBM per device.

v0:
```python
import jax
import jax.numpy as jnp
from jax import lax
from jax.sharding import PartitionSpec as P

EPSILON = 1e-05


def passed_along(value, axis, steps):
    count = lax.axis_size(axis)
    pairs = [(source, (source + steps) % count) for source in range(count)]
    return lax.ppermute(value, axis, pairs)


def contract_last(left_side, right_side):
    return lax.dot_general(
        left_side, right_side, (((1,), (1,)), ((), ())), preferred_element_type=jnp.float32
    )


def shards(
    hidden_in, norm_gain, value_weight, input_proj, value_grad, output_proj, doc_ids, queries
):
    row_count = hidden_in.shape[0]
    rank_size = input_proj.shape[1]
    wide_in = hidden_in.astype(jnp.float32)
    inv_rms = lax.rsqrt(jnp.mean(wide_in * wide_in, axis=1, keepdims=True) + EPSILON)
    normed = (wide_in * inv_rms * norm_gain).astype(jnp.bfloat16)
    w_piece = lax.all_gather(value_weight, "dp", axis=0, tiled=True)
    p_piece = lax.all_gather(input_proj, "dp", axis=0, tiled=True)
    values_acc = jnp.dot(normed, w_piece, preferred_element_type=jnp.float32)
    left_acc = jnp.dot(normed, p_piece, preferred_element_type=jnp.float32)
    values_acc, left_proj = (values_acc, left_acc)
    grad_normed = contract_last(value_grad, lax.all_gather(value_weight, "dp", axis=0, tiled=True))
    values_out = values_acc.astype(jnp.bfloat16)
    grad_normed = grad_normed * norm_gain
    inner_sum = jnp.mean(grad_normed * wide_in, axis=1, keepdims=True)
    cube = inv_rms * inv_rms * inv_rms
    hidden_grad = (inv_rms * grad_normed - wide_in * cube * inner_sum).astype(jnp.bfloat16)
    right_proj = jnp.dot(value_grad, output_proj, preferred_element_type=jnp.float32)
    group_size = lax.axis_size("score")
    doc_count = lax.axis_size("dp") * group_size // 8
    per_group = doc_count // group_size
    doc_range = jnp.arange(doc_count, dtype=jnp.int32)
    onehot = (doc_ids[:, None] == doc_range[None, :]).astype(jnp.float32)
    spread = (onehot[:, :, None] * left_proj[:, None, :]).reshape(row_count, doc_count * rank_size)
    doc_term = jnp.dot(spread.T, right_proj, precision=lax.Precision.HIGHEST).reshape(
        doc_count, rank_size * rank_size
    )
    group_index = lax.axis_index("score")
    totals = lax.psum(doc_term, ("dp", "score"))
    own_docs = lax.dynamic_slice_in_dim(totals, group_index * per_group, per_group, 0)
    doc_low = own_docs.astype(jnp.bfloat16)
    query_rows = queries.shape[0]
    scores = jnp.zeros((per_group, query_rows * group_size), jnp.float32)
    current = queries
    for rotation in range(group_size):
        anchor = (group_index - rotation) % group_size
        piece_scores = contract_last(doc_low, current)
        scores = lax.dynamic_update_slice_in_dim(scores, piece_scores, anchor * query_rows, 1)
        if rotation + 1 < group_size:
            current = passed_along(current, "score", 1)
    return (values_out, hidden_grad, scores)


def solution(mesh):
    placed = (
        P(("score", "dp"), None),
        P(),
        P("dp", None),
        P("dp", None),
        P(("score", "dp"), None),
        P(),
        P(("score", "dp")),
        P(("dp", "score"), None),
    )
    return jax.shard_map(
        shards,
        mesh=mesh,
        in_specs=placed,
        out_specs=(P(("score", "dp"), None), P(("score", "dp"), None), P("score", "dp")),
        check_vma=False,
    )
```

profile of v0, /device:TPU:1, one launch (start us, length us, event | category | flops | bytes accessed | tf_op | source)
XLA Modules:
  0.0 450.3 jit_solution(516351808430916587)
XLA Ops:
  8.0 4.0 collective-permute-start
  11.9 17.3 %collective-permute-done = bf16[16,4096]{1,0:T(8,128)(2,1)S(1)} collective-permute-done((bf16[16,4096]{1,0:T(8,128)(2,1)}, bf16[16,4096]{1,0:T(8,128)(2,1)S(1)}, u32[]{:S(2)}, u32[]{:S(2)}) %collective-permute-start) | collective-permute-done | bytes 131104 | tf_op jit(solution)/shard_map/ppermute | solution.py:12
  29.3 1.9 collective-permute-start.1
  31.2 15.6 %collective-permute-done.1 = bf16[16,4096]{1,0:T(8,128)(2,1)S(1)} collective-permute-done((bf16[16,4096]{1,0:T(8,128)(2,1)S(1)}, bf16[16,4096]{1,0:T(8,128)(2,1)S(1)}, u32[]{:S(2)}, u32[]{:S(2)}) %collective-permute-start.1) | collective-permute-done | bytes 131104 | tf_op jit(solution)/shard_map/ppermute | solution.py:12
  47.4 1.9 collective-permute-start.2
  49.4 22.3 %collective-permute-done.2 = bf16[16,4096]{1,0:T(8,128)(2,1)S(1)} collective-permute-done((bf16[16,4096]{1,0:T(8,128)(2,1)S(1)}, bf16[16,4096]{1,0:T(8,128)(2,1)S(1)}, u32[]{:S(2)}, u32[]{:S(2)}) %collective-permute-start.2) | collective-permute-done | bytes 131104 | tf_op jit(solution)/shard_map/ppermute | solution.py:12
  71.6 1.9 collective-permute-start.3
  73.7 16.9 %collective-permute-done.3 = bf16[16,4096]{1,0:T(8,128)(2,1)S(1)} collective-permute-done((bf16[16,4096]{1,0:T(8,128)(2,1)S(1)}, bf16[16,4096]{1,0:T(8,128)(2,1)S(1)}, u32[]{:S(2)}, u32[]{:S(2)}) %collective-permute-start.3) | collective-permute-done | bytes 131104 | tf_op jit(solution)/shard_map/ppermute | solution.py:12
  90.6 1.9 collective-permute-start.4
  92.5 1.0 fusion.11
  93.5 14.9 %collective-permute-done.4 = bf16[16,4096]{1,0:T(8,128)(2,1)S(1)} collective-permute-done((bf16[16,4096]{1,0:T(8,128)(2,1)S(1)}, bf16[16,4096]{1,0:T(8,128)(2,1)S(1)}, u32[]{:S(2)}, u32[]{:S(2)}) %collective-permute-start.4) | collective-permute-done | bytes 131104 | tf_op jit(solution)/shard_map/ppermute | solution.py:12
  108.4 1.9 collective-permute-start.5
  111.0 18.8 %collective-permute-done.5 = bf16[16,4096]{1,0:T(8,128)(2,1)} collective-permute-done((bf16[16,4096]{1,0:T(8,128)(2,1)S(1)}, bf16[16,4096]{1,0:T(8,128)(2,1)}, u32[]{:S(2)}, u32[]{:S(2)}) %collective-permute-start.5) | collective-permute-done | bytes 131104 | tf_op jit(solution)/shard_map/ppermute | solution.py:12
  129.8 1.9 collective-permute-start.6
  131.8 11.9 %all-gather.3.cloned.1.call-done = bf16[8192,512]{1,0:T(8,128)(2,1)} async-done(((bf16[128,512]{1,0:T(8,128)(2,1)}), bf16[8192,512]{1,0:T(8,128)(2,1)}) %all-gather.3.cloned.1.call-update) | async-done | bytes 8388624 | tf_op jit(solution)/shard_map/all_gather | solution.py:29
  143.6 8.9 %fusion.6 = (f32[128]{0:T(128)S(1)}, f32[128]{0:T(128)S(1)}, f32[128,8192]{1,0:T(8,128)}) fusion(bf16[128,8192]{1,0:T(8,128)(2,1)} %param.8, f32[8192]{0:T(1024)} %param.9, bf16[128,512]{1,0:T(8,128)(2,1)S(1)} %copy-done, bf16[8192,512]{1,0:T(8,128)(2,1)} %all-gather.3.cloned.1.call-done), kind=kOutput, calls=%fused_computation.11 | convolution fusion | flops 1080033024 | bytes 14844928 | tf_op jit(solution)/shard_map/dot_general | solution.py:16
  152.5 163.2 %all-gather.5.cloned.1.call-done = bf16[8192,64]{0,1:T(8,128)(2,1)} async-done(((bf16[128,64]{0,1:T(8,128)(2,1)}), bf16[8192,64]{0,1:T(8,128)(2,1)}) %all-gather.5.cloned.1.call-update) | async-done | bytes 1048592 | tf_op jit(solution)/shard_map/all_gather | solution.py:30
  315.8 2.1 fusion.7
  318.2 1.8 fusion.12
  320.6 107.7 %all-reduce.1 = bf16[64,4096]{1,0:T(8,128)(2,1)S(1)} all-reduce(f32[64,4096]{1,0:T(8,128)S(1)} %reshape.55), channel_id=1, replica_groups=mesh['dp'=64,'score'=8] {'dp','score'}, use_global_device_ids=true, to_apply=%region_2.0 | all-reduce | flops 262144 | bytes 1572864 | tf_op jit(solution)/shard_map/psum | solution.py:51
  428.6 5.3 %fusion.5 = bf16[128,8192]{1,0:T(8,128)(2,1)} fusion(bf16[128,8192]{1,0:T(8,128)(2,1)} %param.8, f32[128,8192]{1,0:T(8,128)} %get-tuple-element.7, f32[128]{0:T(128)S(1)} %broadcast_multiply_fusion.1, f32[128]{0:T(128)S(1)} %get-tuple-element.5, f32[128]{0:T(128)S(1)} %get-tuple-element.6), kind=kLoop, calls=%fused_computation.10 | loop fusion | flops 6291456 | bytes 8390144 | tf_op jit(solution)/shard_map/convert_element_type | solution.py:39
  435.6 1.1 fusion.19
  436.9 1.1 fusion.20
  438.1 5.3 %convolution_convert_fusion = bf16[128,512]{1,0:T(8,128)(2,1)} fusion(bf16[8192,512]{1,0:T(8,128)(2,1)} %all-gather.3.cloned.1.call-done, bf16[128,8192]{1,0:T(8,128)(2,1)S(1)} %copy-done.2, f32[8192]{0:T(1024)S(1)} %copy-done.13, f32[128]{0:T(128)S(1)} %get-tuple-element.6), kind=kOutput, calls=%fused_computation.12 | convolution fusion | flops 1078001664 | bytes 10650112 | tf_op jit(solution)/shard_map/dot_general | solution.py:31
  (56 shorter events, 5.3 us)
Async XLA Ops:
  7.2 85.3 %copy-start = (bf16[128,512]{1,0:T(8,128)(2,1)S(1)}, bf16[128,512]{1,0:T(8,128)(2,1)}, u32[]{:S(2)}) copy-start(bf16[128,512]{1,0:T(8,128)(2,1)} %param.12) | copy-start | bytes 393220
  7.2 136.5 %all-gather.3.cloned.1.call-start = ((), (), s32[]{:S(2)}) async-start(), calls=%async_computation | async-start | bytes 8519680 | tf_op jit(solution)/shard_map/all_gather | solution.py:29
  7.9 307.8 %all-gather.5.cloned.1.call-start = ((), (), s32[]{:S(2)}) async-start(), calls=%async_computation.1 | async-start | bytes 1064960 | tf_op jit(solution)/shard_map/all_gather | solution.py:30
  8.0 21.3 %collective-permute-start = (bf16[16,4096]{1,0:T(8,128)(2,1)}, bf16[16,4096]{1,0:T(8,128)(2,1)S(1)}, u32[]{:S(2)}, u32[]{:S(2)}) collective-permute-start(bf16[16,4096]{1,0:T(8,128)(2,1)} %param.15), channel_id=1, source_target_pairs={{0,1},{1,2},{2,3},{3,4},{4,5},{5,6},{6,7},{7,0},{8,9},{9,10},{10,1... | collective-permute-start | bytes 393224 | tf_op jit(solution)/shard_map/ppermute | solution.py:12
  29.3 17.5 %collective-permute-start.1 = (bf16[16,4096]{1,0:T(8,128)(2,1)S(1)}, bf16[16,4096]{1,0:T(8,128)(2,1)S(1)}, u32[]{:S(2)}, u32[]{:S(2)}) collective-permute-start(bf16[16,4096]{1,0:T(8,128)(2,1)S(1)} %collective-permute-done), channel_id=1, source_target_pairs={{0,1},{1,2},{2,3},{3,4},{4,5},{5,6},{6,7},{7,0},{8,9},{9,10},{10,1... | collective-permute-start | bytes 393224 | tf_op jit(solution)/shard_map/ppermute | solution.py:12
  46.8 0.7 copy-start.4
  47.4 24.2 %collective-permute-start.2 = (bf16[16,4096]{1,0:T(8,128)(2,1)S(1)}, bf16[16,4096]{1,0:T(8,128)(2,1)S(1)}, u32[]{:S(2)}, u32[]{:S(2)}) collective-permute-start(bf16[16,4096]{1,0:T(8,128)(2,1)S(1)} %collective-permute-done.1), channel_id=1, source_target_pairs={{0,1},{1,2},{2,3},{3,4},{4,5},{5,6},{6,7},{7,0},{8,9},{9,10},{10,1... | collective-permute-start | bytes 393224 | tf_op jit(solution)/shard_map/ppermute | solution.py:12
  71.6 38.7 %copy-start.6 = (bf16[16,4096]{1,0:T(8,128)(2,1)}, bf16[16,4096]{1,0:T(8,128)(2,1)S(1)}, u32[]{:S(2)}) copy-start(bf16[16,4096]{1,0:T(8,128)(2,1)S(1)} %collective-permute-done.2) | copy-start | bytes 393220
  71.6 19.0 %collective-permute-start.3 = (bf16[16,4096]{1,0:T(8,128)(2,1)S(1)}, bf16[16,4096]{1,0:T(8,128)(2,1)S(1)}, u32[]{:S(2)}, u32[]{:S(2)}) collective-permute-start(bf16[16,4096]{1,0:T(8,128)(2,1)S(1)} %collective-permute-done.2), channel_id=1, source_target_pairs={{0,1},{1,2},{2,3},{3,4},{4,5},{5,6},{6,7},{7,0},{8,9},{9,10},{10,1... | collective-permute-start | bytes 393224 | tf_op jit(solution)/shard_map/ppermute | solution.py:12
  90.6 17.8 %copy-start.8 = (bf16[16,4096]{1,0:T(8,128)(2,1)}, bf16[16,4096]{1,0:T(8,128)(2,1)S(1)}, u32[]{:S(2)}) copy-start(bf16[16,4096]{1,0:T(8,128)(2,1)S(1)} %collective-permute-done.3) | copy-start | bytes 393220
  90.6 17.8 %collective-permute-start.4 = (bf16[16,4096]{1,0:T(8,128)(2,1)S(1)}, bf16[16,4096]{1,0:T(8,128)(2,1)S(1)}, u32[]{:S(2)}, u32[]{:S(2)}) collective-permute-start(bf16[16,4096]{1,0:T(8,128)(2,1)S(1)} %collective-permute-done.3), channel_id=1, source_target_pairs={{0,1},{1,2},{2,3},{3,4},{4,5},{5,6},{6,7},{7,0},{8,9},{9,10},{10,1... | collective-permute-start | bytes 393224 | tf_op jit(solution)/shard_map/ppermute | solution.py:12
  108.4 44.1 %copy-start.10 = (bf16[16,4096]{1,0:T(8,128)(2,1)}, bf16[16,4096]{1,0:T(8,128)(2,1)S(1)}, u32[]{:S(2)}) copy-start(bf16[16,4096]{1,0:T(8,128)(2,1)S(1)} %collective-permute-done.4) | copy-start | bytes 393220
  108.4 21.4 %collective-permute-start.5 = (bf16[16,4096]{1,0:T(8,128)(2,1)S(1)}, bf16[16,4096]{1,0:T(8,128)(2,1)}, u32[]{:S(2)}, u32[]{:S(2)}) collective-permute-start(bf16[16,4096]{1,0:T(8,128)(2,1)S(1)} %collective-permute-done.4), channel_id=1, source_target_pairs={{0,1},{1,2},{2,3},{3,4},{4,5},{5,6},{6,7},{7,0},{8,9},{9,10},{10,1... | collective-permute-start | bytes 393224 | tf_op jit(solution)/shard_map/ppermute | solution.py:12
  111.0 204.8 %copy-start.1 = (bf16[128,8192]{1,0:T(8,128)(2,1)S(1)}, bf16[128,8192]{1,0:T(8,128)(2,1)}, u32[]{:S(2)}) copy-start(bf16[128,8192]{1,0:T(8,128)(2,1)} %param.8) | copy-start | bytes 6291460
  111.0 204.8 %copy-start.12 = (f32[8192]{0:T(1024)S(1)}, f32[8192]{0:T(1024)}, u32[]{:S(2)}) copy-start(f32[8192]{0:T(1024)} %param.9) | copy-start | bytes 98308
  129.8 307.0 %collective-permute-start.6 = (bf16[16,4096]{1,0:T(8,128)(2,1)}, bf16[16,4096]{1,0:T(8,128)(2,1)}, u32[]{:S(2)}, u32[]{:S(2)}) collective-permute-start(bf16[16,4096]{1,0:T(8,128)(2,1)} %collective-permute-done.5), channel_id=1, source_target_pairs={{0,1},{1,2},{2,3},{3,4},{4,5},{5,6},{6,7},{7,0},{8,9},{9,10},{10,1... | collective-permute-start | bytes 393224 | tf_op jit(solution)/shard_map/ppermute | solution.py:12
  318.2 110.2 %copy-start.3 = (bf16[16,4096]{1,0:T(8,128)(2,1)S(1)}, bf16[16,4096]{1,0:T(8,128)(2,1)}, u32[]{:S(2)}) copy-start(bf16[16,4096]{1,0:T(8,128)(2,1)} %param.15) | copy-start | bytes 393220
  428.5 5.8 %copy-start.5 = (bf16[16,4096]{1,0:T(8,128)(2,1)S(1)}, bf16[16,4096]{1,0:T(8,128)(2,1)}, u32[]{:S(2)}) copy-start(bf16[16,4096]{1,0:T(8,128)(2,1)} %copy-done.4) | copy-start | bytes 393220
  428.5 6.1 %copy-start.7 = (bf16[16,4096]{1,0:T(8,128)(2,1)S(1)}, bf16[16,4096]{1,0:T(8,128)(2,1)}, u32[]{:S(2)}) copy-start(bf16[16,4096]{1,0:T(8,128)(2,1)} %copy-done.6) | copy-start | bytes 393220
  428.5 6.4 %copy-start.9 = (bf16[16,4096]{1,0:T(8,128)(2,1)S(1)}, bf16[16,4096]{1,0:T(8,128)(2,1)}, u32[]{:S(2)}) copy-start(bf16[16,4096]{1,0:T(8,128)(2,1)} %copy-done.8) | copy-start | bytes 393220
  428.5 6.8 %copy-start.11 = (bf16[16,4096]{1,0:T(8,128)(2,1)S(1)}, bf16[16,4096]{1,0:T(8,128)(2,1)}, u32[]{:S(2)}) copy-start(bf16[16,4096]{1,0:T(8,128)(2,1)} %copy-done.10) | copy-start | bytes 393220
  428.5 9.6 %copy-start.2 = (bf16[128,8192]{1,0:T(8,128)(2,1)S(1)}, bf16[128,8192]{1,0:T(8,128)(2,1)}, u32[]{:S(2)}) copy-start(bf16[128,8192]{1,0:T(8,128)(2,1)} %param.8) | copy-start | bytes 6291460
  428.6 9.6 %copy-start.13 = (f32[8192]{0:T(1024)S(1)}, f32[8192]{0:T(1024)}, u32[]{:S(2)}) copy-start(f32[8192]{0:T(1024)} %param.9) | copy-start | bytes 98308
  438.1 5.4 %copy-start.14 = (f32[8,128]{1,0:T(8,128)}, f32[8,128]{1,0:T(8,128)S(1)}, u32[]{:S(2)}) copy-start(f32[8,128]{1,0:T(8,128)S(1)} %dynamic_update_slice.31) | copy-start | bytes 12292
Sparse Core Ops, SparseCore 0:
  10.2 133.4 all-gather.2
  145.7 170.0 all-gather.4
where the time goes:
time: 451 us; the launch traced here: 450 us
  waiting for transfers between devices  282 us (63%)
  blocking collectives  108 us (24%)
  matrix products  22.1 us (5%)
  starting transfers between devices  15.5 us (3%)
  between operations  14.4 us (3%)
  other arithmetic  6.24 us (1%)
    all_gather x1, waiting for transfers between devices, shards(): p_piece = lax.all_gather(input_proj, 'dp', axis=0, tiled=True)  163 us
    psum x1, blocking collectives, shards(): totals = lax.psum(doc_term, ('dp', 'score'))  108 us
    ppermute x7, waiting for transfers between devices, passed_along(): return lax.ppermute(value, axis, pairs)  106 us
    ppermute x7, starting transfers between devices, passed_along(): return lax.ppermute(value, axis, pairs)  15.4 us
    all_gather x1, waiting for transfers between devices, shards(): w_piece = lax.all_gather(value_weight, 'dp', axis=0, tiled=True)  11.9 us
    dot_general x9, matrix products, contract_last(): lax.dot_general(left_side, right_side, (((1,), (1,)), ((), ())), preferre...  11.9 us
  transfers between devices with their start and end apart: 9, of which 8 were waited for; matrix products, arithmetic and copies ran while one was open for 5% of the time, Pallas kernels for 0%

commit v1 on v0

v1 whole, which is shorter than its diff:
```python
import jax
import jax.numpy as jnp
from jax import lax
from jax.sharding import Mesh
from jax.sharding import PartitionSpec as P

EPSILON = 1e-05
DP = ("y", "zl", "core")
SCORE = ("zh", "x")


def spread_to_all(value, axes):
    count = lax.axis_size(axes)
    copies = jnp.broadcast_to(value[None], (count,) + value.shape)
    return lax.all_to_all(copies, axes, 0, 0, tiled=True)


def swapped(value, axis):
    return lax.ppermute(value, axis, [(0, 1), (1, 0)])


def contract_last(left_side, right_side):
    return lax.dot_general(
        left_side, right_side, (((1,), (1,)), ((), ())), preferred_element_type=jnp.float32
    )


def ordered(first, own, other):
    return jnp.where(first, own, other), jnp.where(first, other, own)


def shards(
    hidden_in, norm_gain, value_weight, input_proj, value_grad, output_proj, doc_ids, queries
):
    rows, width = hidden_in.shape
    kv = value_weight.shape[1]
    rank = input_proj.shape[1]
    core = lax.axis_index("core")
    x_index = lax.axis_index("x")
    on_first = core == 0

    p_own = spread_to_all(spread_to_all(input_proj.T, "zl"), "y")
    p_other = swapped(p_own, "core")

    q_pair = jnp.stack([queries, swapped(queries, "zh")])
    q_all = spread_to_all(q_pair, "x")

    quarter = lax.dynamic_slice_in_dim(value_weight, x_index * (kv // 4), kv // 4, 1)
    w_z = spread_to_all(quarter, "zl")
    half = w_z.shape[0] // 2
    wa = spread_to_all(w_z[:half], "x").transpose(1, 2, 0, 3).reshape(half, -1, kv)
    wa = spread_to_all(wa, "y").reshape(-1, kv)
    wb = spread_to_all(spread_to_all(w_z[half:], "y"), "x")
    wb = wb.transpose(1, 2, 3, 0, 4).reshape(-1, kv)
    w_parts = (wa, wb, swapped(wa, "core"), swapped(wb, "core"))

    def cut(array):
        blocks = array.reshape(array.shape[0], 4, 2, half, 2, 128)
        parts = []
        for side in (core, 1 - core):
            mine = lax.dynamic_index_in_dim(blocks, side, 4, keepdims=False)
            for zone in range(2):
                parts.append(mine[:, :, zone].reshape(array.shape[0], -1))
        return parts

    wide_in = hidden_in.astype(jnp.float32)
    inv_rms = lax.rsqrt(jnp.mean(wide_in * wide_in, axis=1, keepdims=True) + EPSILON)
    normed = (wide_in * inv_rms * norm_gain).astype(jnp.bfloat16)

    right_t = lax.dot_general(
        output_proj, value_grad, (((0,), (1,)), ((), ())), preferred_element_type=jnp.float32
    )
    ids_row = jnp.broadcast_to(doc_ids.astype(jnp.float32)[None], (8, rows))
    right_all = spread_to_all(jnp.concatenate([right_t, ids_row], 0), ("y", "core"))
    p_first, p_second = ordered(on_first, p_own, p_other)
    p_full = jnp.stack([p_first, p_second], 2).reshape(64, rank, 128)
    p_full = p_full.transpose(1, 0, 2).reshape(rank, width)
    left_t = contract_last(p_full, normed)
    left_blocks = left_t.reshape(4, 8, 2, rows).transpose(0, 2, 1, 3).reshape(8, 8, rows)
    left_all = lax.all_to_all(left_blocks, ("y", "core"), 0, 0, tiled=True)

    doc_count = 64
    ids_all = right_all[:, rank].reshape(1, -1)
    right_flat = right_all[:, :rank].transpose(1, 0, 2).reshape(rank, -1)
    left_flat = left_all.transpose(1, 0, 2).reshape(8, 1, -1)
    doc_range = jnp.arange(doc_count, dtype=jnp.float32)[:, None]
    onehot = (ids_all == doc_range).astype(jnp.float32)
    spread = (onehot[None] * left_flat).reshape(8 * doc_count, -1)
    doc_term = lax.dot_general(
        spread, right_flat, (((1,), (1,)), ((), ())), precision=lax.Precision.HIGHEST
    )
    doc_term = doc_term.reshape(16, 2, 16, rank)
    doc_term = jnp.concatenate([doc_term[:, 0], doc_term[:, 1]], -1)
    z_parts = lax.all_to_all(doc_term, ("zl", "zh"), 0, 0, tiled=True)
    z_sum = jnp.sum(z_parts, 0)
    z_sum = jnp.concatenate([z_sum[:, :rank], z_sum[:, rank:]], 0).reshape(4, 8, rank)
    x_parts = lax.all_to_all(z_sum, "x", 0, 0, tiled=True)
    own_docs = jnp.sum(x_parts, 0).astype(jnp.bfloat16)
    doc_low = spread_to_all(own_docs, DP)
    doc_low = doc_low.transpose(1, 0, 2).reshape(8, -1)
    q_flat = q_all.reshape(-1, q_all.shape[-1])
    piece = contract_last(doc_low, q_flat).reshape(8, 4, 2, -1)
    first, second = ordered(lax.axis_index("zh") == 0, piece[:, :, 0], piece[:, :, 1])
    scores = jnp.concatenate([first.reshape(8, -1), second.reshape(8, -1)], 1)

    values_acc = jnp.zeros((rows, kv), jnp.float32)
    grads = []
    for normed_part, w_part in zip(cut(normed), w_parts):
        values_acc += jnp.dot(normed_part, w_part, preferred_element_type=jnp.float32)
        grads.append(contract_last(value_grad, w_part))
    values_out = values_acc.astype(jnp.bfloat16)
    along = jnp.sum(values_acc * value_grad.astype(jnp.float32), axis=1, keepdims=True)
    scale = inv_rms * inv_rms * along / width
    shape = (rows, 4, half, 128)
    own = jnp.stack([grads[0].reshape(shape), grads[1].reshape(shape)], 2)
    other = jnp.stack([grads[2].reshape(shape), grads[3].reshape(shape)], 2)
    grad_normed = jnp.stack(ordered(on_first, own, other), 4).reshape(rows, width) * norm_gain
    hidden_grad = (inv_rms * grad_normed - wide_in * scale).astype(jnp.bfloat16)
    return (values_out, hidden_grad, scores)


def solution(mesh):
    fine = Mesh(mesh.devices.reshape(4, 8, 2, 2, 4), DP + SCORE)
    tokens = SCORE + DP
    placed = (
        P(tokens, None),
        P(),
        P(DP, None),
        P(DP, None),
        P(tokens, None),
        P(),
        P(tokens),
        P(DP + SCORE, None),
    )
    return jax.shard_map(
        shards,
        mesh=fine,
        in_specs=placed,
        out_specs=(P(tokens, None), P(tokens, None), P(SCORE, DP)),
        check_vma=False,
    )
```

time: 451 us -> 290 us (0.64)
  waiting for transfers between devices: 282 us -> 81.7 us
  blocking collectives: 108 us -> 29.3 us
  starting transfers between devices: 15.5 us -> 93 us
  local copies, waits for them, and re-layouts: 2.75 us -> 47.5 us
  between operations: 14.4 us -> 1.18 us
  other arithmetic: 6.24 us -> 14.6 us
    all_gather x2 -> x0, waiting for transfers between devices: 175 us -> none  [the longest x1 163 us: shards(): p_piece = lax.all_gather(input_proj, 'dp', axis=0, tiled=True)]
    psum x1 -> x0, blocking collectives: 108 us -> none  [shards(): totals = lax.psum(doc_term, ('dp', 'score'))]
    ppermute x7 -> x4, waiting for transfers between devices: 106 us -> 15.1 us  [swapped(): return lax.ppermute(value, axis, [(0, 1), (1, 0)])]
    all_to_all x0 -> x12, starting transfers between devices: none -> 76.4 us  [the longest x9 59.3 us: spread_to_all(): return lax.all_to_all(copies, axes, 0, 0, tiled=True)]
    all_to_all x0 -> x12, waiting for transfers between devices: none -> 66.6 us  [the longest x9 45.2 us: spread_to_all(): return lax.all_to_all(copies, axes, 0, 0, tiled=True)]
    all_to_all x0 -> x1, blocking collectives: none -> 29.3 us  [spread_to_all(): return lax.all_to_all(copies, axes, 0, 0, tiled=True)]
    unnamed x30 -> x39, local copies, waits for them, and re-layouts: 0.74 us -> 12.6 us
    broadcast_in_dim x1 -> x12, local copies, waits for them, and re-layouts: 0.01 us -> 10.1 us  [the longest x11 10.1 us: spread_to_all(): copies = jnp.broadcast_to(value[None], (count,) + value.shape)]
  transfers between devices with their start and end apart: 9 -> 16, of which waited for: 8 -> 12; matrix products, arithmetic and copies ran while one was open for 5% -> 17% of each run, Pallas kernels for 0% -> 0%
where the time goes in v1:
time: 290 us; the launch traced here: 289 us
  starting transfers between devices  93 us (32%)
  waiting for transfers between devices  81.7 us (28%)
  local copies, waits for them, and re-layouts  47.5 us (16%)
  blocking collectives  29.3 us (10%)
  matrix products  21.3 us (7%)
  other arithmetic  14.6 us (5%)
    all_to_all x9, starting transfers between devices, spread_to_all(): return lax.all_to_all(copies, axes, 0, 0, tiled=True)  59.3 us
    all_to_all x9, waiting for transfers between devices, spread_to_all(): return lax.all_to_all(copies, axes, 0, 0, tiled=True)  45.2 us
    all_to_all x1, blocking collectives, spread_to_all(): return lax.all_to_all(copies, axes, 0, 0, tiled=True)  29.3 us
    ppermute x4, starting transfers between devices, swapped(): return lax.ppermute(value, axis, [(0, 1), (1, 0)])  16.6 us
    ppermute x4, waiting for transfers between devices, swapped(): return lax.ppermute(value, axis, [(0, 1), (1, 0)])  15.1 us
    all_to_all x1, waiting for transfers between devices, shards(): z_parts = lax.all_to_all(doc_term, ('zl', 'zh'), 0, 0, tiled=True)  12.9 us
    unnamed x39, local copies, waits for them, and re-layouts  12.6 us
    dot_general x6, matrix products, contract_last(): lax.dot_general(left_side, right_side, (((1,), (1,)), ((), ())), preferre...  11.9 us
  transfers between devices with their start and end apart: 16, of which 12 were waited for; matrix products, arithmetic and copies ran while one was open for 17% of the time, Pallas kernels for 0%

profile of v1, /device:TPU:1, one launch (start us, length us, event | category | flops | bytes accessed | tf_op | source)
XLA Modules:
  0.0 288.5 jit_solution(5183446104317644672)
XLA Ops:
  2.1 13.1 %all-to-all-start.6 = ((bf16[8,64,128]{2,1,0:T(8,128)(2,1)}), bf16[8,64,128]{2,1,0:T(8,128)(2,1)S(1)}, u32[]{:S(2)}, u32[]{:S(2)}) async-start(bf16[8,64,128]{2,1,0:T(8,128)(2,1)} %broadcast_in_dim.32), calls=%async_computation.6 | async-start | bytes 262144 | tf_op jit(solution)/shard_map/all_to_all | solution.py:15
  19.5 6.0 %all-to-all-done.6 = bf16[8,64,128]{2,1,0:T(8,128)(2,1)S(1)} async-done(((bf16[8,64,128]{2,1,0:T(8,128)(2,1)}), bf16[8,64,128]{2,1,0:T(8,128)(2,1)S(1)}, u32[]{:S(2)}, u32[]{:S(2)}) %all-to-all-start.6) | async-done | bytes 131104 | tf_op jit(solution)/shard_map/all_to_all | solution.py:15
  26.4 4.2 %all-to-all-start.7 = ((bf16[4,8,64,128]{3,2,1,0:T(8,128)(2,1)}), bf16[4,8,64,128]{3,2,1,0:T(8,128)(2,1)S(1)}, u32[]{:S(2)}, u32[]{:S(2)}) async-start(bf16[4,8,64,128]{3,2,1,0:T(8,128)(2,1)} %broadcast_in_dim.33), calls=%async_computation.7 | async-start | bytes 1048576 | tf_op jit(solution)/shard_map/all_to_all | solution.py:15
  30.8 6.7 %all-to-all-done.7 = bf16[4,8,64,128]{3,2,1,0:T(8,128)(2,1)S(1)} async-done(((bf16[4,8,64,128]{3,2,1,0:T(8,128)(2,1)}), bf16[4,8,64,128]{3,2,1,0:T(8,128)(2,1)S(1)}, u32[]{:S(2)}, u32[]{:S(2)}) %all-to-all-start.7) | async-done | bytes 524320 | tf_op jit(solution)/shard_map/all_to_all | solution.py:15
  38.3 7.3 %all-to-all-start.5 = ((f32[8,72,128]{2,1,0:T(8,128)}), f32[8,72,128]{2,1,0:T(8,128)S(1)}, u32[]{:S(2)}, u32[]{:S(2)}) async-start(f32[8,72,128]{2,1,0:T(8,128)} %broadcast_in_dim.31), calls=%async_computation.5 | async-start | bytes 589824 | tf_op jit(solution)/shard_map/all_to_all | solution.py:15
  47.6 4.3 %fusion.2 = bf16[128,8192]{0,1:T(8,128)(2,1)} fusion(bf16[128,8192]{0,1:T(8,128)(2,1)S(1)} %copy.65, f32[8192]{0:T(1024)S(1)} %copy-done.11, f32[128]{0:T(128)S(1)} %add_rsqrt_fusion), kind=kLoop, calls=%fused_computation.5 | loop fusion | flops 4194304 | bytes 4227584 | tf_op jit(solution)/shard_map/convert_element_type | solution.py:68
  59.5 4.6 %all-to-all-start.8 = ((f32[8,8,128]{2,1,0:T(8,128)}), f32[8,8,128]{2,1,0:T(8,128)S(1)}, u32[]{:S(2)}, u32[]{:S(2)}) async-start(f32[8,8,128]{2,1,0:T(8,128)} %bitcast.29), calls=%async_computation.8 | async-start | bytes 65536 | tf_op jit(solution)/shard_map/all_to_all | solution.py:80
  64.3 4.5 %all-to-all-done.8 = f32[8,8,128]{2,1,0:T(8,128)S(1)} async-done(((f32[8,8,128]{2,1,0:T(8,128)}), f32[8,8,128]{2,1,0:T(8,128)S(1)}, u32[]{:S(2)}, u32[]{:S(2)}) %all-to-all-start.8) | async-done | bytes 32800 | tf_op jit(solution)/shard_map/all_to_all | solution.py:80
  69.5 5.1 %all-to-all-start = ((bf16[8,128,128]{1,2,0:T(8,128)(2,1)}), bf16[8,128,128]{1,2,0:T(8,128)(2,1)S(1)}, u32[]{:S(2)}, u32[]{:S(2)}) async-start(bf16[8,128,128]{1,2,0:T(8,128)(2,1)} %broadcast_in_dim.24), calls=%async_computation | async-start | bytes 524288 | tf_op jit(solution)/shard_map/all_to_all | solution.py:15
  77.9 8.9 %all-to-all-done = bf16[8,128,128]{1,2,0:T(8,128)(2,1)S(1)} async-done(((bf16[8,128,128]{1,2,0:T(8,128)(2,1)}), bf16[8,128,128]{1,2,0:T(8,128)(2,1)S(1)}, u32[]{:S(2)}, u32[]{:S(2)}) %all-to-all-start) | async-done | bytes 262176 | tf_op jit(solution)/shard_map/all_to_all | solution.py:15
  86.8 9.3 %all-to-all-start.9 = ((f32[16,16,128]{2,1,0:T(8,128)}), f32[16,16,128]{2,1,0:T(8,128)S(1)}, u32[]{:S(2)}, u32[]{:S(2)}) async-start(f32[16,16,128]{2,1,0:T(8,128)} %pad_maximum_fusion.5), calls=%async_computation.9 | async-start | bytes 262144 | tf_op jit(solution)/shard_map/all_to_all | solution.py:94
  96.1 12.9 %all-to-all-done.9 = f32[16,16,128]{2,1,0:T(8,128)S(1)} async-done(((f32[16,16,128]{2,1,0:T(8,128)}), f32[16,16,128]{2,1,0:T(8,128)S(1)}, u32[]{:S(2)}, u32[]{:S(2)}) %all-to-all-start.9) | async-done | bytes 131104 | tf_op jit(solution)/shard_map/all_to_all | solution.py:94
  114.7 6.1 %all-to-all-done.1 = bf16[4,4,128,128]{2,3,1,0:T(8,128)(2,1)S(1)} async-done(((bf16[4,4,128,128]{2,3,1,0:T(8,128)(2,1)}), bf16[4,4,128,128]{2,3,1,0:T(8,128)(2,1)S(1)}, u32[]{:S(2)}, u32[]{:S(2)}) %all-to-all-start.1) | async-done | bytes 524320 | tf_op jit(solution)/shard_map/all_to_all | solution.py:15
  134.7 4.8 %all-to-all-done.3 = bf16[4,4,128,128]{3,2,1,0:T(8,128)(2,1)S(1)} async-done(((bf16[4,4,128,128]{3,2,1,0:T(8,128)(2,1)}), bf16[4,4,128,128]{3,2,1,0:T(8,128)(2,1)S(1)}, u32[]{:S(2)}, u32[]{:S(2)}) %all-to-all-start.3) | async-done | bytes 524320 | tf_op jit(solution)/shard_map/all_to_all | solution.py:15
  139.5 13.1 %all-to-all-start.11 = ((bf16[64,2,256]{2,1,0:T(2,128)(2,1)}), bf16[64,2,256]{2,1,0:T(2,128)(2,1)S(1)}, u32[]{:S(2)}, u32[]{:S(2)}) async-start(bf16[64,2,256]{2,1,0:T(2,128)(2,1)} %reshape.263), calls=%async_computation.11 | async-start | bytes 131072 | tf_op jit(solution)/shard_map/all_to_all | solution.py:15
  154.7 10.9 %all-to-all-done.11 = bf16[64,2,256]{2,1,0:T(2,128)(2,1)S(1)} async-done(((bf16[64,2,256]{2,1,0:T(2,128)(2,1)}), bf16[64,2,256]{2,1,0:T(2,128)(2,1)S(1)}, u32[]{:S(2)}, u32[]{:S(2)}) %all-to-all-start.11) | async-done | bytes 65568 | tf_op jit(solution)/shard_map/all_to_all | solution.py:15
  165.8 29.3 %all_to_all.65 = bf16[4,4,128,512]{3,2,1,0:T(8,128)(2,1)} all-to-all(bf16[4,4,128,512]{3,2,1,0:T(8,128)(2,1)S(1)} %broadcast_in_dim.27), channel_id=1, replica_groups=mesh['y'=4,'zl'=8,'core'=2,'zh'=2,'x'=4] {'y'}, dimensions={0} | all-to-all | bytes 4194304 | tf_op jit(solution)/shard_map/all_to_all | solution.py:15
  197.0 4.6 %all-to-all-start.4 = ((bf16[4,4,4,128,128]{4,3,2,1,0:T(8,128)(2,1)}), bf16[4,4,4,128,128]{4,3,2,1,0:T(8,128)(2,1)}, u32[]{:S(2)}, u32[]{:S(2)}) async-start(bf16[4,4,4,128,128]{4,3,2,1,0:T(8,128)(2,1)} %broadcast_in_dim.29), calls=%async_computation.4 | async-start | bytes 4194304 | tf_op jit(solution)/shard_map/all_to_all | solution.py:15
  201.6 8.6 %collective-permute-start.3 = (bf16[16,4096]{1,0:T(8,128)(2,1)S(1)}, bf16[16,4096]{1,0:T(8,128)(2,1)S(1)}, u32[]{:S(2)}, u32[]{:S(2)}) collective-permute-start(bf16[16,4096]{1,0:T(8,128)(2,1)S(1)} %copy-done.13), channel_id=1, source_target_pairs={{0,4},{4,0},{1,5},{5,1},{2,6},{6,2},{3,7},{7,3},{8,12},{12,8},{9,1... | collective-permute-start | bytes 393224 | tf_op jit(solution)/shard_map/ppermute | solution.py:19
  210.2 15.1 %collective-permute-done.3 = bf16[16,4096]{1,0:T(8,128)(2,1)S(1)} collective-permute-done((bf16[16,4096]{1,0:T(8,128)(2,1)S(1)}, bf16[16,4096]{1,0:T(8,128)(2,1)S(1)}, u32[]{:S(2)}, u32[]{:S(2)}) %collective-permute-start.3) | collective-permute-done | bytes 131104 | tf_op jit(solution)/shard_map/ppermute | solution.py:19
  227.9 4.4 %all-to-all-start.12 = ((bf16[4,2,16,4096]{3,2,1,0:T(8,128)(2,1)}), bf16[4,2,16,4096]{3,2,1,0:T(8,128)(2,1)}, u32[]{:S(2)}, u32[]{:S(2)}) async-start(bf16[4,2,16,4096]{3,2,1,0:T(8,128)(2,1)} %broadcast_in_dim.35), calls=%async_computation.12 | async-start | bytes 2097152 | tf_op jit(solution)/shard_map/all_to_all | solution.py:15
  242.8 4.0 %collective-permute-start.1 = (bf16[2048,512]{1,0:T(8,128)(2,1)}, bf16[2048,512]{1,0:T(8,128)(2,1)}, u32[]{:S(2)}, u32[]{:S(2)}) collective-permute-start(bf16[2048,512]{1,0:T(8,128)(2,1)} %bitcast.99), channel_id=1, source_target_pairs={{0,8},{8,0},{1,9},{9,1},{2,10},{10,2},{3,11},{11,3},{4,12},{12,4},... | collective-permute-start | bytes 6291464 | tf_op jit(solution)/shard_map/ppermute | solution.py:19
  280.1 4.4 %fusion.4 = bf16[128,8192]{0,1:T(8,128)(2,1)} fusion(bf16[128,8192]{0,1:T(8,128)(2,1)S(1)} %copy.65, f32[128,4,2,4,2,128]{0,5,4,3,2,1:T(8,128)S(1)} %copy.77, f32[128]{0:T(128)S(1)} %multiply_multiply_fusion, f32[8192]{0:T(1024)S(1)} %copy-done.12, f32[128]{0:T(128)S(1)} %add_rsqrt_fusion), kind=kLoop, calls=%fused_computation.7 | loop fusion | flops 6291456 | bytes 8422400 | tf_op jit(solution)/shard_map/convert_element_type | solution.py:118
  284.5 4.1 %copy.87 = bf16[128,8192]{1,0:T(8,128)(2,1)} copy(bf16[128,8192]{0,1:T(8,128)(2,1)} %fusion.4) | data formatting | bytes 4194304
  (127 shorter events, 91.0 us)
Async XLA Ops:
  0.6 51.3 %copy-start = (bf16[128,512]{1,0:T(8,128)(2,1)S(1)}, bf16[128,512]{1,0:T(8,128)(2,1)}, u32[]{:S(2)}) copy-start(bf16[128,512]{1,0:T(8,128)(2,1)} %param.10) | copy-start | bytes 393220
  2.1 23.4 %all-to-all-start.6 = ((bf16[8,64,128]{2,1,0:T(8,128)(2,1)}), bf16[8,64,128]{2,1,0:T(8,128)(2,1)S(1)}, u32[]{:S(2)}, u32[]{:S(2)}) async-start(bf16[8,64,128]{2,1,0:T(8,128)(2,1)} %broadcast_in_dim.32), calls=%async_computation.6 | async-start | bytes 262144 | tf_op jit(solution)/shard_map/all_to_all | solution.py:15
  18.4 12.2 %copy-start.6 = (bf16[128,512]{1,0:T(8,128)(2,1)S(1)}, bf16[128,512]{1,0:T(8,128)(2,1)}, u32[]{:S(2)}) copy-start(bf16[128,512]{1,0:T(8,128)(2,1)} %param.12) | copy-start | bytes 393220
  18.4 12.2 %copy-start.14 = (bf16[512,64]{0,1:T(8,128)(2,1)S(1)}, bf16[512,64]{0,1:T(8,128)(2,1)}, u32[]{:S(2)}) copy-start(bf16[512,64]{0,1:T(8,128)(2,1)} %param.13) | copy-start | bytes 196612
  18.4 12.3 %copy-start.15 = (s32[128]{0:T(128)S(1)}, s32[128]{0:T(128)}, u32[]{:S(2)}) copy-start(s32[128]{0:T(128)} %param.14) | copy-start | bytes 1540
  18.4 29.2 %copy-start.11 = (f32[8192]{0:T(1024)S(1)}, f32[8192]{0:T(1024)}, u32[]{:S(2)}) copy-start(f32[8192]{0:T(1024)} %param.9) | copy-start | bytes 98308
  26.4 11.1 %all-to-all-start.7 = ((bf16[4,8,64,128]{3,2,1,0:T(8,128)(2,1)}), bf16[4,8,64,128]{3,2,1,0:T(8,128)(2,1)S(1)}, u32[]{:S(2)}, u32[]{:S(2)}) async-start(bf16[4,8,64,128]{3,2,1,0:T(8,128)(2,1)} %broadcast_in_dim.33), calls=%async_computation.7 | async-start | bytes 1048576 | tf_op jit(solution)/shard_map/all_to_all | solution.py:15
  38.3 14.1 %all-to-all-start.5 = ((f32[8,72,128]{2,1,0:T(8,128)}), f32[8,72,128]{2,1,0:T(8,128)S(1)}, u32[]{:S(2)}, u32[]{:S(2)}) async-start(f32[8,72,128]{2,1,0:T(8,128)} %broadcast_in_dim.31), calls=%async_computation.5 | async-start | bytes 589824 | tf_op jit(solution)/shard_map/all_to_all | solution.py:15
  45.6 7.5 %collective-permute-start.2 = (bf16[4,8,64,128]{3,2,1,0:T(8,128)(2,1)S(1)}, bf16[4,8,64,128]{3,2,1,0:T(8,128)(2,1)}, u32[]{:S(2)}, u32[]{:S(2)}) collective-permute-start(bf16[4,8,64,128]{3,2,1,0:T(8,128)(2,1)S(1)} %all-to-all-done.7), channel_id=1, source_target_pairs={{0,8},{8,0},{1,9},{9,1},{2,10},{10,2},{3,11},{11,3},{4,12},{12,4},... | collective-permute-start | bytes 1572872 | tf_op jit(solution)/shard_map/ppermute | solution.py:19
  56.1 7.9 %copy-start.10 = (f32[64,8,128]{2,0,1:T(8,128)S(1)}, f32[64,8,128]{2,0,1:T(8,128)}, u32[]{:S(2)}) copy-start(f32[64,8,128]{2,0,1:T(8,128)} %slice_bitcast_fusion) | copy-start | bytes 786436
  59.5 9.3 %all-to-all-start.8 = ((f32[8,8,128]{2,1,0:T(8,128)}), f32[8,8,128]{2,1,0:T(8,128)S(1)}, u32[]{:S(2)}, u32[]{:S(2)}) async-start(f32[8,8,128]{2,1,0:T(8,128)} %bitcast.29), calls=%async_computation.8 | async-start | bytes 65536 | tf_op jit(solution)/shard_map/all_to_all | solution.py:80
  69.5 17.3 %all-to-all-start = ((bf16[8,128,128]{1,2,0:T(8,128)(2,1)}), bf16[8,128,128]{1,2,0:T(8,128)(2,1)S(1)}, u32[]{:S(2)}, u32[]{:S(2)}) async-start(bf16[8,128,128]{1,2,0:T(8,128)(2,1)} %broadcast_in_dim.24), calls=%async_computation | async-start | bytes 524288 | tf_op jit(solution)/shard_map/all_to_all | solution.py:15
  86.8 22.2 %all-to-all-start.9 = ((f32[16,16,128]{2,1,0:T(8,128)}), f32[16,16,128]{2,1,0:T(8,128)S(1)}, u32[]{:S(2)}, u32[]{:S(2)}) async-start(f32[16,16,128]{2,1,0:T(8,128)} %pad_maximum_fusion.5), calls=%async_computation.9 | async-start | bytes 262144 | tf_op jit(solution)/shard_map/all_to_all | solution.py:94
  109.9 10.9 %all-to-all-start.1 = ((bf16[4,4,128,128]{2,3,1,0:T(8,128)(2,1)}), bf16[4,4,128,128]{2,3,1,0:T(8,128)(2,1)S(1)}, u32[]{:S(2)}, u32[]{:S(2)}) async-start(bf16[4,4,128,128]{2,3,1,0:T(8,128)(2,1)} %broadcast_in_dim.25), calls=%async_computation.1 | async-start | bytes 1048576 | tf_op jit(solution)/shard_map/all_to_all | solution.py:15
  120.9 7.4 %all-to-all-start.10 = ((f32[4,1,512]{2,1,0:T(1,128)}), f32[4,1,512]{2,1,0:T(1,128)S(1)}, u32[]{:S(2)}, u32[]{:S(2)}) async-start(f32[4,1,512]{2,1,0:T(1,128)} %reshape.261), calls=%async_computation.10 | async-start | bytes 16384 | tf_op jit(solution)/shard_map/all_to_all | solution.py:97
  129.2 10.4 %all-to-all-start.3 = ((bf16[4,4,128,128]{3,2,1,0:T(8,128)(2,1)}), bf16[4,4,128,128]{3,2,1,0:T(8,128)(2,1)S(1)}, u32[]{:S(2)}, u32[]{:S(2)}) async-start(bf16[4,4,128,128]{3,2,1,0:T(8,128)(2,1)} %broadcast_in_dim.28), calls=%async_computation.3 | async-start | bytes 1048576 | tf_op jit(solution)/shard_map/all_to_all | solution.py:15
  139.5 26.0 %all-to-all-start.11 = ((bf16[64,2,256]{2,1,0:T(2,128)(2,1)}), bf16[64,2,256]{2,1,0:T(2,128)(2,1)S(1)}, u32[]{:S(2)}, u32[]{:S(2)}) async-start(bf16[64,2,256]{2,1,0:T(2,128)(2,1)} %reshape.263), calls=%async_computation.11 | async-start | bytes 131072 | tf_op jit(solution)/shard_map/all_to_all | solution.py:15
  197.0 29.8 %all-to-all-start.4 = ((bf16[4,4,4,128,128]{4,3,2,1,0:T(8,128)(2,1)}), bf16[4,4,4,128,128]{4,3,2,1,0:T(8,128)(2,1)}, u32[]{:S(2)}, u32[]{:S(2)}) async-start(bf16[4,4,4,128,128]{4,3,2,1,0:T(8,128)(2,1)} %broadcast_in_dim.29), calls=%async_computation.4 | async-start | bytes 4194304 | tf_op jit(solution)/shard_map/all_to_all | solution.py:15
  201.6 23.7 %collective-permute-start.3 = (bf16[16,4096]{1,0:T(8,128)(2,1)S(1)}, bf16[16,4096]{1,0:T(8,128)(2,1)S(1)}, u32[]{:S(2)}, u32[]{:S(2)}) collective-permute-start(bf16[16,4096]{1,0:T(8,128)(2,1)S(1)} %copy-done.13), channel_id=1, source_target_pairs={{0,4},{4,0},{1,5},{5,1},{2,6},{6,2},{3,7},{7,3},{8,12},{12,8},{9,1... | collective-permute-start | bytes 393224 | tf_op jit(solution)/shard_map/ppermute | solution.py:19
  227.9 32.2 %all-to-all-start.12 = ((bf16[4,2,16,4096]{3,2,1,0:T(8,128)(2,1)}), bf16[4,2,16,4096]{3,2,1,0:T(8,128)(2,1)}, u32[]{:S(2)}, u32[]{:S(2)}) async-start(bf16[4,2,16,4096]{3,2,1,0:T(8,128)(2,1)} %broadcast_in_dim.35), calls=%async_computation.12 | async-start | bytes 2097152 | tf_op jit(solution)/shard_map/all_to_all | solution.py:15
  242.8 25.6 %collective-permute-start.1 = (bf16[2048,512]{1,0:T(8,128)(2,1)}, bf16[2048,512]{1,0:T(8,128)(2,1)}, u32[]{:S(2)}, u32[]{:S(2)}) collective-permute-start(bf16[2048,512]{1,0:T(8,128)(2,1)} %bitcast.99), channel_id=1, source_target_pairs={{0,8},{8,0},{1,9},{9,1},{2,10},{10,2},{3,11},{11,3},{4,12},{12,4},... | collective-permute-start | bytes 6291464 | tf_op jit(solution)/shard_map/ppermute | solution.py:19
  255.4 8.1 %copy-start.7 = (bf16[128,4,1,4,128]{0,4,3,1,2:T(8,128)(2,1)S(1)}, bf16[128,4,1,4,128]{0,4,3,1,2:T(8,128)(2,1)}, u32[]{:S(2)}) copy-start(bf16[128,4,1,4,128]{0,4,3,1,2:T(8,128)(2,1)} %copy.67) | copy-start | bytes 1572868
  258.1 12.7 %collective-permute-start = (bf16[2048,512]{1,0:T(8,128)(2,1)}, bf16[2048,512]{1,0:T(8,128)(2,1)}, u32[]{:S(2)}, u32[]{:S(2)}) collective-permute-start(bf16[2048,512]{1,0:T(8,128)(2,1)} %bitcast.100), channel_id=1, source_target_pairs={{0,8},{8,0},{1,9},{9,1},{2,10},{10,2},{3,11},{11,3},{4,12},{12,4},... | collective-permute-start | bytes 6291464 | tf_op jit(solution)/shard_map/ppermute | solution.py:19
  280.1 8.4 %copy-start.1 = (bf16[128,512]{1,0:T(8,128)(2,1)S(1)}, bf16[128,512]{1,0:T(8,128)(2,1)}, u32[]{:S(2)}) copy-start(bf16[128,512]{1,0:T(8,128)(2,1)} %param.10) | copy-start | bytes 393220
  (8 other events, 21.9 us)

commit v2 on v1

v2 whole, which is shorter than its diff:
```python
import jax
import jax.numpy as jnp
from jax import lax
from jax.experimental import pallas as pl
from jax.experimental.pallas import tpu as pltpu
from jax.sharding import Mesh
from jax.sharding import PartitionSpec as P

EPSILON = 1e-05
DP = ("y", "zl", "core")
SCORE = ("zh", "x")
Y_STEPS = (0, 1, -1, 2)
Z_STEPS = (-1, 0, 1, 2, 3, 4, -3, -2)
BLOCK = 128
LIMIT = 48 * 1024 * 1024


def spread_to_all(value, axes):
    count = lax.axis_size(axes)
    copies = jnp.broadcast_to(value[None], (count,) + value.shape)
    return lax.all_to_all(copies, axes, 0, 0, tiled=True)


def swapped(value, axis):
    return lax.ppermute(value, axis, [(0, 1), (1, 0)])


def from_y(value, step):
    return lax.ppermute(value, "y", [((y + step) % 4, y) for y in range(4)])


def from_z(value, step):
    def place(z):
        return (z % 8) * 2 + z // 8

    return lax.ppermute(
        value, ("zl", "zh"), [(place((z + step) % 16), place(z)) for z in range(16)]
    )


def contract_last(left_side, right_side):
    return lax.dot_general(
        left_side, right_side, (((1,), (1,)), ((), ())), preferred_element_type=jnp.float32
    )


def ordered(first, own, other):
    return jnp.where(first, own, other), jnp.where(first, other, own)


def after(value, earlier):
    return lax.optimization_barrier((value, earlier))[0]


def left_kernel(core_ref, normed_ref, own_ref, other_ref, left_ref):
    first = core_ref[0] == 0
    rank = left_ref.shape[0]
    total = jnp.zeros(left_ref.shape, jnp.float32)
    for pair in range(32):
        y, z = divmod(pair, 8)
        own = own_ref[y, z * rank : (z + 1) * rank]
        other = other_ref[y, z * rank : (z + 1) * rank]
        factor = jnp.concatenate(ordered(first, own, other), 1)
        total += contract_last(factor, normed_ref[:, pair * 256 : (pair + 1) * 256])
    left_ref[...] = total


def layer_kernel(
    core_ref, place_ref, normed_ref, hidden_ref, gain_ref, scale_ref, grad_ref, own_ref, other_ref,
    values_ref, hidden_grad_ref,
):
    first = core_ref[0] == 0
    width = normed_ref.shape[1]
    grad = grad_ref[...]
    inv_rms = scale_ref[...]

    def weights(pair):
        rows = slice(pair * BLOCK, (pair + 1) * BLOCK)
        return jnp.concatenate(ordered(first, own_ref[rows], other_ref[rows]), 0)

    def columns(pair):
        return pl.ds(pl.multiple_of(place_ref[pair] * 256, 256), 256)

    total = jnp.zeros(values_ref.shape, jnp.float32)
    for pair in range(32):
        total += jnp.dot(
            normed_ref[:, columns(pair)], weights(pair), preferred_element_type=jnp.float32
        )
    values_ref[...] = total.astype(jnp.bfloat16)
    along = jnp.sum(total * grad.astype(jnp.float32), axis=1, keepdims=True)
    pull = inv_rms * inv_rms * along / width
    for pair in range(32):
        where = columns(pair)
        back = contract_last(grad, weights(pair)) * gain_ref[:, where]
        wide = hidden_ref[:, where].astype(jnp.float32)
        hidden_grad_ref[:, where] = (inv_rms * back - wide * pull).astype(jnp.bfloat16)


def shards(
    hidden_in, norm_gain, value_weight, input_proj, value_grad, output_proj, doc_ids, queries
):
    rows, width = hidden_in.shape
    kv = value_weight.shape[1]
    rank = input_proj.shape[1]
    core = lax.axis_index("core")
    core_row = core.astype(jnp.int32).reshape(1)
    on_first = core == 0
    smem = pl.BlockSpec(memory_space=pltpu.SMEM)
    vmem = pl.BlockSpec(memory_space=pltpu.VMEM)
    params = pltpu.CompilerParams(vmem_limit_bytes=LIMIT)

    factor = input_proj.T.reshape(4, 8, 2, BLOCK).transpose(0, 2, 1, 3).reshape(rank, BLOCK)
    right_t = lax.dot_general(
        output_proj, value_grad, (((0,), (1,)), ((), ())), preferred_element_type=jnp.float32
    )
    right_high = right_t.astype(jnp.bfloat16)
    right_low = (right_t - right_high.astype(jnp.float32)).astype(jnp.bfloat16)
    ids_rows = jnp.broadcast_to(doc_ids.astype(jnp.bfloat16)[None], (16, rows))
    factor_z = spread_to_all(factor, "zl").reshape(-1, BLOCK)
    packed = jnp.concatenate([factor_z, right_high, right_low, ids_rows], 0)
    packed = spread_to_all(packed, "y")
    packed_other = swapped(packed, "core")

    ahead, behind = from_z(value_weight, 1), from_z(value_weight, -1)
    near = after(jnp.concatenate([behind, value_weight, ahead], 0), factor_z)
    far_ahead, far_behind = from_z(near, 3), from_z(near[BLOCK:], -3)
    w_z = after(jnp.concatenate([near, far_ahead, far_behind], 0), packed)
    half = w_z.shape[0] // 2
    y_ahead, y_behind = from_y(w_z, 1), from_y(w_z, -1)

    q_all = lax.all_gather(queries, SCORE, axis=0, tiled=True)

    wide_in = hidden_in.astype(jnp.float32)
    inv_rms = lax.rsqrt(jnp.mean(wide_in * wide_in, axis=1, keepdims=True) + EPSILON)
    normed = (wide_in * inv_rms * norm_gain).astype(jnp.bfloat16)

    left_t = pl.pallas_call(
        left_kernel,
        out_shape=jax.ShapeDtypeStruct((rank, rows), jnp.float32),
        in_specs=[smem, vmem, vmem, vmem],
        out_specs=vmem,
        compiler_params=params,
        name="left_factor",
    )(core_row, normed, packed, packed_other)
    left_all = lax.all_to_all(
        left_t.reshape(8, rank // 8, rows), ("y", "core"), 0, 0, tiled=True
    )
    base = 8 * rank
    tail = jnp.stack(ordered(on_first, packed[:, base:], packed_other[:, base:]), 1)
    tail = tail.reshape(8, -1, rows).astype(jnp.float32)
    right_all = tail[:, :rank] + tail[:, rank : 2 * rank]
    ids_all = tail[:, 2 * rank].reshape(1, -1)
    right_flat = right_all.transpose(1, 0, 2).reshape(rank, -1)
    left_flat = left_all.transpose(1, 0, 2).reshape(8, 1, -1)
    doc_count = 64
    doc_range = jnp.arange(doc_count, dtype=jnp.float32)[:, None]
    onehot = (ids_all == doc_range).astype(jnp.float32)
    spread = (onehot[None] * left_flat).reshape(8 * doc_count, -1)
    doc_term = lax.dot_general(
        spread, right_flat, (((1,), (1,)), ((), ())), precision=lax.Precision.HIGHEST
    )
    doc_term, q_all = lax.optimization_barrier((doc_term, q_all))
    halves = after((y_ahead[:half], y_behind[half:]), doc_term)
    y_far = (from_y(halves[0], 1), from_y(halves[1], -1))
    doc_parts = lax.all_to_all(
        doc_term.reshape(64, 8, rank), ("zl", "zh", "x"), 0, 0, tiled=True
    )
    w_own = jnp.concatenate([w_z, y_ahead, y_behind, *after(y_far, doc_parts)], 0)
    w_other = swapped(w_own, "core")
    own_docs = jnp.sum(doc_parts, 0).astype(jnp.bfloat16)
    doc_low = spread_to_all(own_docs, DP)
    doc_low = doc_low.transpose(1, 0, 2).reshape(8, -1)
    scores = contract_last(doc_low, q_all)

    y_index, z_index = lax.axis_index("y"), lax.axis_index("zl")
    y_place = (y_index + jnp.array(Y_STEPS, jnp.int32)) % 4
    z_place = (z_index + jnp.array(Z_STEPS, jnp.int32)) % 8
    place = (y_place[:, None] * 8 + z_place[None, :]).reshape(32).astype(jnp.int32)
    values_out, hidden_grad = pl.pallas_call(
        layer_kernel,
        out_shape=(
            jax.ShapeDtypeStruct((rows, kv), jnp.bfloat16),
            jax.ShapeDtypeStruct((rows, width), jnp.bfloat16),
        ),
        in_specs=[smem, smem] + [vmem] * 7,
        out_specs=(vmem, vmem),
        compiler_params=params,
        name="layer",
    )(
        core_row, place, normed, hidden_in, norm_gain.reshape(1, width), inv_rms, value_grad,
        w_own, w_other,
    )
    return (values_out, hidden_grad, scores)


def solution(mesh):
    fine = Mesh(mesh.devices.reshape(4, 8, 2, 2, 4), DP + SCORE)
    tokens = SCORE + DP
    placed = (
        P(tokens, None),
        P(),
        P(DP, None),
        P(DP, None),
        P(tokens, None),
        P(),
        P(tokens),
        P(DP + SCORE, None),
    )
    return jax.shard_map(
        shards,
        mesh=fine,
        in_specs=placed,
        out_specs=(P(tokens, None), P(tokens, None), P(SCORE, DP)),
        check_vma=False,
    )
```

time: 290 us -> 214 us (0.74)
  blocking collectives: 29.3 us -> 0 us
  local copies, waits for them, and re-layouts: 47.5 us -> 28.4 us
  starting transfers between devices: 93 us -> 75.8 us
  matrix products: 21.3 us -> 5.22 us
  between operations: 1.18 us -> 14.4 us
  waiting for transfers between devices: 81.7 us -> 70.1 us
  Pallas kernels: 0 us -> 9.9 us
  other arithmetic: 14.6 us -> 9.4 us
    all_to_all x9 -> x3, starting transfers between devices: 59.3 us -> 23.6 us  [spread_to_all(): return lax.all_to_all(copies, axes, 0, 0, tiled=True)]
    all_to_all x9 -> x3, waiting for transfers between devices: 45.2 us -> 12.5 us  [spread_to_all(): return lax.all_to_all(copies, axes, 0, 0, tiled=True)]
    ppermute x0 -> x8, starting transfers between devices: none -> 30.3 us  [the longest x4 17.2 us: from_z(): lax.ppermute(value, ('zl', 'zh'), [(place((z + step) % 16), place(z)) for...]
    all_to_all x1 -> x0, blocking collectives: 29.3 us -> none  [spread_to_all(): return lax.all_to_all(copies, axes, 0, 0, tiled=True)]
    ppermute x0 -> x8, waiting for transfers between devices: none -> 21 us  [the longest x4 20.9 us: from_z(): lax.ppermute(value, ('zl', 'zh'), [(place((z + step) % 16), place(z)) for...]
    ppermute x4 -> x2, waiting for transfers between devices: 15.1 us -> 0.01 us  [swapped(): return lax.ppermute(value, axis, [(0, 1), (1, 0)])]
    all_gather x0 -> x1, waiting for transfers between devices: none -> 11 us  [shards(): q_all = lax.all_gather(queries, SCORE, axis=0, tiled=True)]
    dot_general x6 -> x1, matrix products: 11.9 us -> 0.98 us  [contract_last(): lax.dot_general(left_side, right_side, (((1,), (1,)), ((), ())), preferre...]
  transfers between devices with their start and end apart: 16 -> 16, of which waited for: 12 -> 6; matrix products, arithmetic and copies ran while one was open for 17% -> 15% of each run, Pallas kernels for 0% -> 0%
where the time goes in v2:
time: 214 us; the launch traced here: 213 us
  starting transfers between devices  75.8 us (35%)
  waiting for transfers between devices  70.1 us (33%)
  local copies, waits for them, and re-layouts  28.4 us (13%)
  between operations  14.4 us (7%)
  Pallas kernels  9.9 us (5%)
  other arithmetic  9.4 us (4%)
  matrix products  5.22 us (2%)
    all_to_all x3, starting transfers between devices, spread_to_all(): return lax.all_to_all(copies, axes, 0, 0, tiled=True)  23.6 us
    ppermute x4, waiting for transfers between devices, from_z(): lax.ppermute(value, ('zl', 'zh'), [(place((z + step) % 16), place(z)) for...  20.9 us
    all_to_all x1, waiting for transfers between devices, shards(): lax.all_to_all(left_t.reshape(8, rank // 8, rows), ('y', 'core'), 0, 0, t...  18.1 us
    ppermute x4, starting transfers between devices, from_z(): lax.ppermute(value, ('zl', 'zh'), [(place((z + step) % 16), place(z)) for...  17.2 us
    unnamed x34, local copies, waits for them, and re-layouts  15 us
    ppermute x4, starting transfers between devices, from_y(): return lax.ppermute(value, 'y', [((y + step) % 4, y) for y in range(4)])  13.1 us
    all_to_all x3, waiting for transfers between devices, spread_to_all(): return lax.all_to_all(copies, axes, 0, 0, tiled=True)  12.5 us
    all_gather x1, waiting for transfers between devices, shards(): q_all = lax.all_gather(queries, SCORE, axis=0, tiled=True)  11 us
  transfers between devices with their start and end apart: 16, of which 6 were waited for; matrix products, arithmetic and copies ran while one was open for 15% of the time, Pallas kernels for 0%

profile of v2, /device:TPU:1, one launch (start us, length us, event | category | flops | bytes accessed | tf_op | source)
XLA Modules:
  0.0 213.2 jit_solution(8003164795513785321)
XLA Ops:
  8.8 13.1 %all-to-all-start = ((bf16[8,64,128]{2,1,0:T(8,128)(2,1)}), bf16[8,64,128]{2,1,0:T(8,128)(2,1)S(1)}, u32[]{:S(2)}, u32[]{:S(2)}) async-start(bf16[8,64,128]{2,1,0:T(8,128)(2,1)} %broadcast_in_dim.14), calls=%async_computation | async-start | bytes 262144 | tf_op jit(solution)/shard_map/all_to_all | solution.py:21
  21.9 3.3 %collective-permute-start = (bf16[128,512]{1,0:T(8,128)(2,1)}, bf16[128,512]{1,0:T(8,128)(2,1)S(1)}, u32[]{:S(2)}, u32[]{:S(2)}) collective-permute-start(bf16[128,512]{1,0:T(8,128)(2,1)} %param.12), channel_id=1, source_target_pairs={{116,0},{0,16},{16,32},{32,48},{48,64},{64,80},{80,96},{96,112},{1... | collective-permute-start | bytes 393224 | tf_op jit(solution)/shard_map/ppermute | solution.py:36
  25.2 6.8 %collective-permute-start.1 = (bf16[128,512]{1,0:T(8,128)(2,1)}, bf16[128,512]{1,0:T(8,128)(2,1)S(1)}, u32[]{:S(2)}, u32[]{:S(2)}) collective-permute-start(bf16[128,512]{1,0:T(8,128)(2,1)} %param.12), channel_id=1, source_target_pairs={{16,0},{32,16},{48,32},{64,48},{80,64},{96,80},{112,96},{4,112},{2... | collective-permute-start | bytes 393224 | tf_op jit(solution)/shard_map/ppermute | solution.py:36
  34.7 4.2 %all-to-all-start.1 = ((bf16[4,656,128]{2,1,0:T(8,128)(2,1)}), bf16[4,656,128]{2,1,0:T(8,128)(2,1)S(1)}, u32[]{:S(2)}, u32[]{:S(2)}) async-start(bf16[4,656,128]{2,1,0:T(8,128)(2,1)} %broadcast_in_dim.16), calls=%async_computation.1 | async-start | bytes 1343488 | tf_op jit(solution)/shard_map/all_to_all | solution.py:21
  41.9 3.4 %collective-permute-start.2 = (bf16[384,512]{1,0:T(8,128)(2,1)}, bf16[384,512]{1,0:T(8,128)(2,1)}, u32[]{:S(2)}, u32[]{:S(2)}) collective-permute-start(bf16[384,512]{1,0:T(8,128)(2,1)} %pad_maximum_fusion.1), channel_id=1, source_target_pairs={{48,0},{64,16},{80,32},{96,48},{112,64},{4,80},{20,96},{36,112},{5... | collective-permute-start | bytes 1179656 | tf_op jit(solution)/shard_map/ppermute | solution.py:36
  45.2 3.7 %collective-permute-start.3 = (bf16[256,512]{1,0:T(8,128)(2,1)}, bf16[256,512]{1,0:T(8,128)(2,1)}, u32[]{:S(2)}, u32[]{:S(2)}) collective-permute-start(bf16[256,512]{1,0:T(8,128)(2,1)} %slice.24), channel_id=1, source_target_pairs={{84,0},{100,16},{116,32},{0,48},{16,64},{32,80},{48,96},{64,112},{... | collective-permute-start | bytes 786440 | tf_op jit(solution)/shard_map/ppermute | solution.py:36
  49.0 4.3 %collective-permute-start.6 = (bf16[4,656,128]{2,1,0:T(8,128)(2,1)S(1)}, bf16[4,656,128]{2,1,0:T(8,128)(2,1)S(1)}, u32[]{:S(2)}, u32[]{:S(2)}) collective-permute-start(bf16[4,656,128]{2,1,0:T(8,128)(2,1)S(1)} %all-to-all-done.1.own_ref), channel_id=1, source_target_pairs={{0,8},{8,0},{1,9},{9,1},{2,10},{10,2},{3,11},{11,3},{4,12},{12,4},... | collective-permute-start | bytes 2015240 | tf_op jit(solution)/shard_map/ppermute | solution.py:25
  55.1 15.4 %collective-permute-done.3 = bf16[256,512]{1,0:T(8,128)(2,1)} collective-permute-done((bf16[256,512]{1,0:T(8,128)(2,1)}, bf16[256,512]{1,0:T(8,128)(2,1)}, u32[]{:S(2)}, u32[]{:S(2)}) %collective-permute-start.3) | collective-permute-done | bytes 262176 | tf_op jit(solution)/shard_map/ppermute | solution.py:36
  70.5 5.6 %collective-permute-done.2 = bf16[384,512]{1,0:T(8,128)(2,1)} collective-permute-done((bf16[384,512]{1,0:T(8,128)(2,1)}, bf16[384,512]{1,0:T(8,128)(2,1)}, u32[]{:S(2)}, u32[]{:S(2)}) %collective-permute-start.2) | collective-permute-done | bytes 393248 | tf_op jit(solution)/shard_map/ppermute | solution.py:36
  78.3 5.0 %collective-permute-start.4 = (bf16[1024,512]{1,0:T(8,128)(2,1)}, bf16[1024,512]{1,0:T(8,128)(2,1)}, u32[]{:S(2)}, u32[]{:S(2)}) collective-permute-start(bf16[1024,512]{1,0:T(8,128)(2,1)} %pad_maximum_fusion), channel_id=1, source_target_pairs={{128,0},{256,128},{384,256},{0,384},{129,1},{257,129},{385,257},{1... | collective-permute-start | bytes 3145736 | tf_op jit(solution)/shard_map/ppermute | solution.py:29
  86.9 7.2 %all-to-all-start.2 = ((f32[8,8,128]{2,1,0:T(8,128)}), f32[8,8,128]{2,1,0:T(8,128)S(1)}, u32[]{:S(2)}, u32[]{:S(2)}) async-start(f32[8,8,128]{2,1,0:T(8,128)} %bitcast.38), calls=%async_computation.2 | async-start | bytes 65536 | tf_op jit(solution)/shard_map/all_to_all | solution.py:145
  94.1 18.1 %all-to-all-done.2 = f32[8,8,128]{2,1,0:T(8,128)S(1)} async-done(((f32[8,8,128]{2,1,0:T(8,128)}), f32[8,8,128]{2,1,0:T(8,128)S(1)}, u32[]{:S(2)}, u32[]{:S(2)}) %all-to-all-start.2) | async-done | bytes 32800 | tf_op jit(solution)/shard_map/all_to_all | solution.py:145
  112.5 3.2 %fusion.3 = f32[512,64]{0,1:T(8,128)S(1)} fusion(f32[512,1024]{1,0:T(8,128)S(1)} %bitcast.39, f32[8,144,128]{2,1,0:T(8,128)} %bitcast.41), kind=kOutput, calls=%fused_computation.9 | convolution fusion | flops 402718720 | bytes 2752512 | tf_op jit(solution)/shard_map/dot_general | solution.py:159
  115.6 11.0 %all-gather.2.cloned.1.call-done = bf16[128,4096]{1,0:T(8,128)(2,1)} async-done(((bf16[16,4096]{1,0:T(8,128)(2,1)}), bf16[128,4096]{1,0:T(8,128)(2,1)}) %all-gather.2.cloned.1.call-update) | async-done | bytes 1048592 | tf_op jit(solution)/shard_map/all_gather | solution.py:131
  130.4 4.4 %collective-permute-start.7 = (bf16[512,512]{1,0:T(8,128)(2,1)}, bf16[512,512]{1,0:T(8,128)(2,1)}, u32[]{:S(2)}, u32[]{:S(2)}) collective-permute-start(bf16[512,512]{1,0:T(8,128)(2,1)} %slice.32), channel_id=1, source_target_pairs={{128,0},{256,128},{384,256},{0,384},{129,1},{257,129},{385,257},{1... | collective-permute-start | bytes 1572872 | tf_op jit(solution)/shard_map/ppermute | solution.py:29
  137.6 4.6 %all-to-all-start.3 = ((f32[64,1,512]{2,1,0:T(1,128)}), f32[64,1,512]{2,1,0:T(1,128)S(1)}, u32[]{:S(2)}, u32[]{:S(2)}) async-start(f32[64,1,512]{2,1,0:T(1,128)} %reshape.114), calls=%async_computation.3 | async-start | bytes 262144 | tf_op jit(solution)/shard_map/all_to_all | solution.py:165
  142.3 2.3 %constant_dynamic-update-slice_fusion.4 = bf16[4096,512]{1,0:T(8,128)(2,1)} fusion(bf16[1024,512]{1,0:T(8,128)(2,1)} %pad_maximum_fusion), kind=kLoop, calls=%fused_computation.24 | loop fusion | bytes 2097152
  144.6 2.4 %constant_dynamic-update-slice_fusion.3 = bf16[4096,512]{1,0:T(8,128)(2,1)} fusion(bf16[4096,512]{1,0:T(8,128)(2,1)} %constant_dynamic-update-slice_fusion.4, bf16[1024,512]{1,0:T(8,128)(2,1)} %collective-permute-done.4), kind=kLoop, calls=%fused_computation.23 | loop fusion | bytes 2097152
  147.0 2.3 %constant_dynamic-update-slice_fusion.2 = bf16[4096,512]{1,0:T(8,128)(2,1)} fusion(bf16[4096,512]{1,0:T(8,128)(2,1)} %constant_dynamic-update-slice_fusion.3, bf16[1024,512]{1,0:T(8,128)(2,1)} %collective-permute-done.5), kind=kLoop, calls=%fused_computation.22 | loop fusion | bytes 2097152
  149.3 7.5 %all-to-all-done.3 = f32[64,1,512]{2,1,0:T(1,128)S(1)} async-done(((f32[64,1,512]{2,1,0:T(1,128)}), f32[64,1,512]{2,1,0:T(1,128)S(1)}, u32[]{:S(2)}, u32[]{:S(2)}) %all-to-all-start.3) | async-done | bytes 131104 | tf_op jit(solution)/shard_map/all_to_all | solution.py:165
  164.4 5.8 %collective-permute-start.9 = (bf16[4096,512]{1,0:T(8,128)(2,1)}, bf16[4096,512]{1,0:T(8,128)(2,1)}, u32[]{:S(2)}, u32[]{:S(2)}) collective-permute-start(bf16[4096,512]{1,0:T(8,128)(2,1)} %constant_dynamic-update-slice_fusion.own_ref), channel_id=1, source_target_pairs={{0,8},{8,0},{1,9},{9,1},{2,10},{10,2},{3,11},{11,3},{4,12},{12,4},... | collective-permute-start | bytes 12582920 | tf_op jit(solution)/shard_map/ppermute | solution.py:25
  172.1 6.3 %all-to-all-start.4 = ((bf16[64,2,256]{2,1,0:T(2,128)(2,1)}), bf16[64,2,256]{2,1,0:T(2,128)(2,1)S(1)}, u32[]{:S(2)}, u32[]{:S(2)}) async-start(bf16[64,2,256]{2,1,0:T(2,128)(2,1)} %reshape.116), calls=%async_computation.4 | async-start | bytes 131072 | tf_op jit(solution)/shard_map/all_to_all | solution.py:21
  178.7 12.5 %all-to-all-done.4 = bf16[64,2,256]{2,1,0:T(2,128)(2,1)S(1)} async-done(((bf16[64,2,256]{2,1,0:T(2,128)(2,1)}), bf16[64,2,256]{2,1,0:T(2,128)(2,1)S(1)}, u32[]{:S(2)}, u32[]{:S(2)}) %all-to-all-start.4) | async-done | bytes 65568 | tf_op jit(solution)/shard_map/all_to_all | solution.py:21
  197.3 9.1 %layer.1 = (bf16[128,512]{1,0:T(8,128)(2,1)}, bf16[128,8192]{1,0:T(8,128)(2,1)}) custom-call(s32[1]{0:T(128)} %bitcast.core_ref, s32[32]{0:T(128)S(1)} %add.69.place_ref, bf16[128,8192]{1,0:T(8,128)(2,1)S(1)} %copy-done.3, bf16[128,8192]{1,0:T(8,128)(2,1)S(1)} %copy-done.1, f32[1,8192]{1,0:T(1,128)S(1)} %bitcast.37, f32[128,1]{1,0:T(8,128)S(1)} %copy.27.scale_ref, ...), custom_call_target="tpu_custom_call" | custom-call | tf_op jit(solution)/shard_map/layer/pallas_call | solution.py:179
  (81 shorter events, 37.6 us)
Async XLA Ops:
  7.2 32.2 %copy-start.10 = (bf16[128,512]{1,0:T(8,128)(2,1)S(1)}, bf16[128,512]{1,0:T(8,128)(2,1)}, u32[]{:S(2)}) copy-start(bf16[128,512]{1,0:T(8,128)(2,1)} %param.12) | copy-start | bytes 393220
  7.2 31.7 %copy-start.1 = (bf16[128,8192]{1,0:T(8,128)(2,1)S(1)}, bf16[128,8192]{1,0:T(8,128)(2,1)}, u32[]{:S(2)}) copy-start(bf16[128,8192]{1,0:T(8,128)(2,1)} %hidden_ref.1) | copy-start | bytes 6291460
  7.2 46.0 %copy-start.5 = (f32[8192]{0:T(1024)S(1)}, f32[8192]{0:T(1024)}, u32[]{:S(2)}) copy-start(f32[8192]{0:T(1024)} %param.11) | copy-start | bytes 98308
  8.8 25.0 %all-to-all-start = ((bf16[8,64,128]{2,1,0:T(8,128)(2,1)}), bf16[8,64,128]{2,1,0:T(8,128)(2,1)S(1)}, u32[]{:S(2)}, u32[]{:S(2)}) async-start(bf16[8,64,128]{2,1,0:T(8,128)(2,1)} %broadcast_in_dim.14), calls=%async_computation | async-start | bytes 262144 | tf_op jit(solution)/shard_map/all_to_all | solution.py:21
  21.8 104.8 %all-gather.2.cloned.1.call-start = ((), (), s32[]{:S(2)}) async-start(), calls=%async_computation.5 | async-start | bytes 1179648 | tf_op jit(solution)/shard_map/all_gather | solution.py:131
  21.9 17.5 %collective-permute-start = (bf16[128,512]{1,0:T(8,128)(2,1)}, bf16[128,512]{1,0:T(8,128)(2,1)S(1)}, u32[]{:S(2)}, u32[]{:S(2)}) collective-permute-start(bf16[128,512]{1,0:T(8,128)(2,1)} %param.12), channel_id=1, source_target_pairs={{116,0},{0,16},{16,32},{32,48},{48,64},{64,80},{80,96},{96,112},{1... | collective-permute-start | bytes 393224 | tf_op jit(solution)/shard_map/ppermute | solution.py:36
  25.2 14.2 %collective-permute-start.1 = (bf16[128,512]{1,0:T(8,128)(2,1)}, bf16[128,512]{1,0:T(8,128)(2,1)S(1)}, u32[]{:S(2)}, u32[]{:S(2)}) collective-permute-start(bf16[128,512]{1,0:T(8,128)(2,1)} %param.12), channel_id=1, source_target_pairs={{16,0},{32,16},{48,32},{64,48},{80,64},{96,80},{112,96},{4,112},{2... | collective-permute-start | bytes 393224 | tf_op jit(solution)/shard_map/ppermute | solution.py:36
  34.7 14.2 %all-to-all-start.1 = ((bf16[4,656,128]{2,1,0:T(8,128)(2,1)}), bf16[4,656,128]{2,1,0:T(8,128)(2,1)S(1)}, u32[]{:S(2)}, u32[]{:S(2)}) async-start(bf16[4,656,128]{2,1,0:T(8,128)(2,1)} %broadcast_in_dim.16), calls=%async_computation.1 | async-start | bytes 1343488 | tf_op jit(solution)/shard_map/all_to_all | solution.py:21
  41.9 34.2 %collective-permute-start.2 = (bf16[384,512]{1,0:T(8,128)(2,1)}, bf16[384,512]{1,0:T(8,128)(2,1)}, u32[]{:S(2)}, u32[]{:S(2)}) collective-permute-start(bf16[384,512]{1,0:T(8,128)(2,1)} %pad_maximum_fusion.1), channel_id=1, source_target_pairs={{48,0},{64,16},{80,32},{96,48},{112,64},{4,80},{20,96},{36,112},{5... | collective-permute-start | bytes 1179656 | tf_op jit(solution)/shard_map/ppermute | solution.py:36
  45.2 25.3 %collective-permute-start.3 = (bf16[256,512]{1,0:T(8,128)(2,1)}, bf16[256,512]{1,0:T(8,128)(2,1)}, u32[]{:S(2)}, u32[]{:S(2)}) collective-permute-start(bf16[256,512]{1,0:T(8,128)(2,1)} %slice.24), channel_id=1, source_target_pairs={{84,0},{100,16},{116,32},{0,48},{16,64},{32,80},{48,96},{64,112},{... | collective-permute-start | bytes 786440 | tf_op jit(solution)/shard_map/ppermute | solution.py:36
  49.0 36.3 %collective-permute-start.6 = (bf16[4,656,128]{2,1,0:T(8,128)(2,1)S(1)}, bf16[4,656,128]{2,1,0:T(8,128)(2,1)S(1)}, u32[]{:S(2)}, u32[]{:S(2)}) collective-permute-start(bf16[4,656,128]{2,1,0:T(8,128)(2,1)S(1)} %all-to-all-done.1.own_ref), channel_id=1, source_target_pairs={{0,8},{8,0},{1,9},{9,1},{2,10},{10,2},{3,11},{11,3},{4,12},{12,4},... | collective-permute-start | bytes 2015240 | tf_op jit(solution)/shard_map/ppermute | solution.py:25
  55.1 30.2 %copy-start.2 = (bf16[128,8192]{1,0:T(8,128)(2,1)S(1)}, bf16[128,8192]{1,0:T(8,128)(2,1)}, u32[]{:S(2)}) copy-start(bf16[128,8192]{1,0:T(8,128)(2,1)} %fusion.2.normed_ref) | copy-start | bytes 6291460
  78.3 48.3 %collective-permute-start.4 = (bf16[1024,512]{1,0:T(8,128)(2,1)}, bf16[1024,512]{1,0:T(8,128)(2,1)}, u32[]{:S(2)}, u32[]{:S(2)}) collective-permute-start(bf16[1024,512]{1,0:T(8,128)(2,1)} %pad_maximum_fusion), channel_id=1, source_target_pairs={{128,0},{256,128},{384,256},{0,384},{129,1},{257,129},{385,257},{1... | collective-permute-start | bytes 3145736 | tf_op jit(solution)/shard_map/ppermute | solution.py:29
  83.3 45.2 %collective-permute-start.5 = (bf16[1024,512]{1,0:T(8,128)(2,1)}, bf16[1024,512]{1,0:T(8,128)(2,1)}, u32[]{:S(2)}, u32[]{:S(2)}) collective-permute-start(bf16[1024,512]{1,0:T(8,128)(2,1)} %pad_maximum_fusion), channel_id=1, source_target_pairs={{384,0},{0,128},{128,256},{256,384},{385,1},{1,129},{129,257},{257... | collective-permute-start | bytes 3145736 | tf_op jit(solution)/shard_map/ppermute | solution.py:29
  86.9 25.3 %all-to-all-start.2 = ((f32[8,8,128]{2,1,0:T(8,128)}), f32[8,8,128]{2,1,0:T(8,128)S(1)}, u32[]{:S(2)}, u32[]{:S(2)}) async-start(f32[8,8,128]{2,1,0:T(8,128)} %bitcast.38), calls=%async_computation.2 | async-start | bytes 65536 | tf_op jit(solution)/shard_map/all_to_all | solution.py:145
  130.4 30.3 %collective-permute-start.7 = (bf16[512,512]{1,0:T(8,128)(2,1)}, bf16[512,512]{1,0:T(8,128)(2,1)}, u32[]{:S(2)}, u32[]{:S(2)}) collective-permute-start(bf16[512,512]{1,0:T(8,128)(2,1)} %slice.32), channel_id=1, source_target_pairs={{128,0},{256,128},{384,256},{0,384},{129,1},{257,129},{385,257},{1... | collective-permute-start | bytes 1572872 | tf_op jit(solution)/shard_map/ppermute | solution.py:29
  134.7 25.9 %collective-permute-start.8 = (bf16[512,512]{1,0:T(8,128)(2,1)}, bf16[512,512]{1,0:T(8,128)(2,1)}, u32[]{:S(2)}, u32[]{:S(2)}) collective-permute-start(bf16[512,512]{1,0:T(8,128)(2,1)} %slice.33), channel_id=1, source_target_pairs={{384,0},{0,128},{128,256},{256,384},{385,1},{1,129},{129,257},{257... | collective-permute-start | bytes 1572872 | tf_op jit(solution)/shard_map/ppermute | solution.py:29
  137.6 19.1 %all-to-all-start.3 = ((f32[64,1,512]{2,1,0:T(1,128)}), f32[64,1,512]{2,1,0:T(1,128)S(1)}, u32[]{:S(2)}, u32[]{:S(2)}) async-start(f32[64,1,512]{2,1,0:T(1,128)} %reshape.114), calls=%async_computation.3 | async-start | bytes 262144 | tf_op jit(solution)/shard_map/all_to_all | solution.py:165
  142.3 28.0 %copy-start.12 = (s32[8]{0:T(128)S(1)}, s32[8]{0:T(128)}, u32[]{:S(2)}) copy-start(s32[8]{0:T(128)} %constant.58.clone) | copy-start | bytes 100
  144.6 33.8 %copy-start.11 = (s32[4]{0:T(128)S(1)}, s32[4]{0:T(128)}, u32[]{:S(2)}) copy-start(s32[4]{0:T(128)} %constant.57.clone) | copy-start | bytes 52
  144.6 50.1 %copy-start.8 = (bf16[128,4096]{1,0:T(8,128)(2,1)S(1)}, bf16[128,4096]{1,0:T(8,128)(2,1)}, u32[]{:S(2)}) copy-start(bf16[128,4096]{1,0:T(8,128)(2,1)} %all-gather.2.cloned.1.call-done) | copy-start | bytes 3145732
  147.0 48.7 %copy-start.4 = (bf16[128,512]{1,0:T(8,128)(2,1)S(1)}, bf16[128,512]{1,0:T(8,128)(2,1)}, u32[]{:S(2)}) copy-start(bf16[128,512]{1,0:T(8,128)(2,1)} %grad_ref.1) | copy-start | bytes 393220
  164.4 31.2 %collective-permute-start.9 = (bf16[4096,512]{1,0:T(8,128)(2,1)}, bf16[4096,512]{1,0:T(8,128)(2,1)}, u32[]{:S(2)}, u32[]{:S(2)}) collective-permute-start(bf16[4096,512]{1,0:T(8,128)(2,1)} %constant_dynamic-update-slice_fusion.own_ref), channel_id=1, source_target_pairs={{0,8},{8,0},{1,9},{9,1},{2,10},{10,2},{3,11},{11,3},{4,12},{12,4},... | collective-permute-start | bytes 12582920 | tf_op jit(solution)/shard_map/ppermute | solution.py:25
  172.1 19.2 %all-to-all-start.4 = ((bf16[64,2,256]{2,1,0:T(2,128)(2,1)}), bf16[64,2,256]{2,1,0:T(2,128)(2,1)S(1)}, u32[]{:S(2)}, u32[]{:S(2)}) async-start(bf16[64,2,256]{2,1,0:T(2,128)(2,1)} %reshape.116), calls=%async_computation.4 | async-start | bytes 131072 | tf_op jit(solution)/shard_map/all_to_all | solution.py:21
  (5 other events, 29.2 us)
Sparse Core Ops, SparseCore 0:
  32.1 94.4 all-gather.1

commit v3 on v2

v3 whole, which is shorter than its diff:
```python
import jax
import jax.numpy as jnp
from jax import lax
from jax.experimental import pallas as pl
from jax.experimental.pallas import tpu as pltpu
from jax.sharding import Mesh
from jax.sharding import PartitionSpec as P

EPSILON = 1e-05
DP = ("y", "zl", "core")
SCORE = ("zh", "x")
Y_STEPS = (0, 1, -1, 2)
Z_STEPS = (-1, 0, 1, 2, 3, 4, -3, -2)
BLOCK = 128
LIMIT = 24 * 1024 * 1024


def spread_to_all(value, axes):
    count = lax.axis_size(axes)
    copies = jnp.broadcast_to(value[None], (count,) + value.shape)
    return lax.all_to_all(copies, axes, 0, 0, tiled=True)


def swapped(value, axis):
    return lax.ppermute(value, axis, [(0, 1), (1, 0)])


def from_y(value, step):
    return lax.ppermute(value, "y", [((y + step) % 4, y) for y in range(4)])


def from_z(value, step):
    def place(z):
        return (z % 8) * 2 + z // 8

    return lax.ppermute(
        value, ("zl", "zh"), [(place((z + step) % 16), place(z)) for z in range(16)]
    )


def contract_last(left_side, right_side):
    return lax.dot_general(
        left_side, right_side, (((1,), (1,)), ((), ())), preferred_element_type=jnp.float32
    )


def ordered(first, own, other):
    return jnp.where(first, own, other), jnp.where(first, other, own)


def after(value, earlier):
    return lax.optimization_barrier((value, earlier))[0]


def left_kernel(core_ref, normed_ref, own_ref, other_ref, left_ref):
    first = core_ref[0] == 0
    rank = left_ref.shape[0]
    total = jnp.zeros(left_ref.shape, jnp.float32)
    for pair in range(32):
        y, z = divmod(pair, 8)
        own = own_ref[y, z * rank : (z + 1) * rank]
        other = other_ref[y, z * rank : (z + 1) * rank]
        factor = jnp.concatenate(ordered(first, own, other), 1)
        total += contract_last(factor, normed_ref[:, pair * 256 : (pair + 1) * 256])
    left_ref[...] = total


def joined_kernel(*refs):
    out_ref = refs[-1]
    start = 0
    for ref in refs[:-1]:
        out_ref[start : start + ref.shape[0]] = ref[...]
        start += ref.shape[0]


def halves_kernel(ahead_ref, behind_ref, low_ref, high_ref):
    half = low_ref.shape[0]
    low_ref[...] = ahead_ref[:half]
    high_ref[...] = behind_ref[half:]


def weights(first, own_ref, other_ref, pair):
    rows = slice(pair * BLOCK, (pair + 1) * BLOCK)
    return jnp.concatenate(ordered(first, own_ref[rows], other_ref[rows]), 0)


def columns(place_ref, pair):
    return pl.ds(pl.multiple_of(place_ref[pair] * 256, 256), 256)


def near_kernel(core_ref, place_ref, normed_ref, gain_ref, scale_ref, grad_ref, *refs):
    own_refs, other_refs, (total_ref, base_ref) = refs[:3], refs[3:6], refs[6:]
    first = core_ref[0] == 0
    grad = grad_ref[...]
    inv_rms = scale_ref[...]
    total = jnp.zeros(total_ref.shape, jnp.float32)
    for group in range(3):
        for step in range(8):
            pair = group * 8 + step
            where = columns(place_ref, pair)
            weight = weights(first, own_refs[group], other_refs[group], step)
            total += jnp.dot(normed_ref[:, where], weight, preferred_element_type=jnp.float32)
            back = contract_last(grad, weight) * gain_ref[:, where]
            base_ref[:, pair * 256 : (pair + 1) * 256] = inv_rms * back
    total_ref[...] = total


def far_kernel(
    core_ref, place_ref, normed_ref, hidden_ref, gain_ref, scale_ref, grad_ref, total_ref, base_ref,
    own_low, own_high, other_low, other_high, values_ref, hidden_grad_ref,
):
    first = core_ref[0] == 0
    width = normed_ref.shape[1]
    grad = grad_ref[...]
    inv_rms = scale_ref[...]
    own_refs, other_refs = (own_low, own_high), (other_low, other_high)
    total = total_ref[...]
    for step in range(8):
        weight = weights(first, own_refs[step // 4], other_refs[step // 4], step % 4)
        total += jnp.dot(
            normed_ref[:, columns(place_ref, 24 + step)], weight, preferred_element_type=jnp.float32
        )
    values_ref[...] = total.astype(jnp.bfloat16)
    along = jnp.sum(total * grad.astype(jnp.float32), axis=1, keepdims=True)
    pull = inv_rms * inv_rms * along / width
    for pair in range(32):
        where = columns(place_ref, pair)
        if pair < 24:
            base = base_ref[:, pair * 256 : (pair + 1) * 256]
        else:
            step = pair - 24
            weight = weights(first, own_refs[step // 4], other_refs[step // 4], step % 4)
            base = inv_rms * (contract_last(grad, weight) * gain_ref[:, where])
        wide = hidden_ref[:, where].astype(jnp.float32)
        hidden_grad_ref[:, where] = (base - wide * pull).astype(jnp.bfloat16)


def score_kernel(index_ref, docs_ref, here_ref, one_ref, two_ref, three_ref, scores_ref):
    lane = lax.broadcasted_iota(jnp.int32, docs_ref.shape[1:], 1)
    low = lane < docs_ref.shape[2] // 2
    pieces = []
    for pair in range(docs_ref.shape[0] // 2):
        even = docs_ref[2 * pair].astype(jnp.float32)
        odd = docs_ref[2 * pair + 1].astype(jnp.float32)
        pieces.append(jnp.where(low, even, odd).astype(jnp.bfloat16))
    docs = jnp.concatenate(pieces, 1)
    found = [contract_last(docs, ref[...]) for ref in (here_ref, one_ref, two_ref, three_ref)]
    size = here_ref.shape[0] // 2
    mine = [piece[:, :size] for piece in found]
    others = [piece[:, size:] for piece in found]
    zh, x = index_ref[0], index_ref[1]
    result = jnp.zeros(scores_ref.shape, jnp.float32)
    for turn in range(4):
        order = [(place - turn) % 4 for place in range(4)]
        one_half = [mine[step] for step in order]
        other_half = [others[step] for step in order]
        for side, parts in ((0, one_half + other_half), (1, other_half + one_half)):
            chosen = jnp.logical_and(zh == side, x == turn)
            result = jnp.where(chosen, jnp.concatenate(parts, 1), result)
    scores_ref[...] = result


def call(body, out_shape, scalars, name, limit=LIMIT):
    def run(*operands):
        smem = pl.BlockSpec(memory_space=pltpu.SMEM)
        vmem = pl.BlockSpec(memory_space=pltpu.VMEM)
        return pl.pallas_call(
            body,
            out_shape=out_shape,
            in_specs=[smem] * scalars + [vmem] * (len(operands) - scalars),
            out_specs=jax.tree.map(lambda _: vmem, out_shape),
            compiler_params=pltpu.CompilerParams(vmem_limit_bytes=limit),
            name=name,
        )(*operands)

    return run


def from_x(value, step):
    return lax.ppermute(value, "x", [((x + step) % 4, x) for x in range(4)])


def struct(shape, dtype):
    return jax.ShapeDtypeStruct(shape, dtype)


def shards(
    hidden_in, norm_gain, value_weight, input_proj, value_grad, output_proj, doc_ids, queries
):
    rows, width = hidden_in.shape
    kv = value_weight.shape[1]
    rank = input_proj.shape[1]
    core = lax.axis_index("core")
    core_row = core.astype(jnp.int32).reshape(1)
    on_first = core == 0

    factor = input_proj.T.reshape(4, 8, 2, BLOCK).transpose(0, 2, 1, 3).reshape(rank, BLOCK)
    right_t = lax.dot_general(
        output_proj, value_grad, (((0,), (1,)), ((), ())), preferred_element_type=jnp.float32
    ).astype(jnp.bfloat16)
    ids_rows = jnp.broadcast_to(doc_ids.astype(jnp.bfloat16)[None], (16, rows))
    factor_z = spread_to_all(factor, "zl").reshape(-1, BLOCK)
    packed = spread_to_all(jnp.concatenate([factor_z, right_t, ids_rows], 0), "y")
    packed_other = swapped(packed, "core")

    ahead, behind = from_z(value_weight, 1), from_z(value_weight, -1)
    three = call(joined_kernel, struct((3 * BLOCK, kv), jnp.bfloat16), 0, "near_three")
    two = call(joined_kernel, struct((2 * BLOCK, kv), jnp.bfloat16), 0, "near_two")
    near = after(three(behind, value_weight, ahead), factor_z)
    near_two = after(two(value_weight, ahead), factor_z)
    far_ahead, far_behind = from_z(near, 3), from_z(near_two, -3)

    wide_in = hidden_in.astype(jnp.float32)
    inv_rms = lax.rsqrt(jnp.mean(wide_in * wide_in, axis=1, keepdims=True) + EPSILON)
    normed = (wide_in * inv_rms * norm_gain).astype(jnp.bfloat16)
    left_t = call(left_kernel, struct((rank, rows), jnp.float32), 1, "left_factor")(
        core_row, normed, packed, packed_other
    )

    q_other = swapped(after(queries, left_t), "zh")

    left_all = lax.all_to_all(
        left_t.reshape(8, rank // 8, rows), ("y", "core"), 0, 0, tiled=True
    )

    far_ahead, far_behind = after((far_ahead, far_behind), left_all)
    w_z = call(joined_kernel, struct((8 * BLOCK, kv), jnp.bfloat16), 0, "along_z")(
        near, far_ahead, far_behind
    )
    y_ahead, y_behind = from_y(w_z, 1), from_y(w_z, -1)

    base = 8 * rank
    tail = jnp.stack(ordered(on_first, packed[:, base:], packed_other[:, base:]), 1)
    tail = tail.reshape(8, -1, rows).astype(jnp.float32)
    right_flat = tail[:, :rank].transpose(1, 0, 2).reshape(rank, -1)
    ids_all = tail[:, rank].reshape(1, -1)
    left_flat = left_all.transpose(1, 0, 2).reshape(8, 1, -1)
    doc_count = 64
    doc_range = jnp.arange(doc_count, dtype=jnp.float32)[:, None]
    onehot = (ids_all == doc_range).astype(jnp.float32)
    spread = (onehot[None] * left_flat).reshape(8 * doc_count, -1)
    doc_term = lax.dot_general(
        spread, right_flat, (((1,), (1,)), ((), ())), precision=lax.Precision.HIGHEST
    )
    doc_parts = lax.all_to_all(
        doc_term.reshape(64, 8, rank), ("zl", "zh", "x"), 0, 0, tiled=True
    )
    q_here = after(jnp.concatenate([queries, q_other], 0), doc_term)
    q_turns = [from_x(q_here, step) for step in (1, 2, 3)]
    w_z_other = swapped(w_z, "core")
    doc_parts, q_turns, w_z_other = lax.optimization_barrier((doc_parts, q_turns, w_z_other))
    own_docs = jnp.sum(doc_parts, 0).astype(jnp.bfloat16)
    own_docs = jnp.concatenate([own_docs, own_docs], 1)
    doc_copies = jnp.broadcast_to(own_docs[None], (64,) + own_docs.shape)
    y_ahead, y_behind, doc_copies = lax.optimization_barrier((y_ahead, y_behind, doc_copies))
    doc_low = lax.all_to_all(doc_copies, DP, 0, 0, tiled=True)
    low, high = call(
        halves_kernel, (struct((4 * BLOCK, kv), jnp.bfloat16),) * 2, 0, "far_halves"
    )(y_ahead, y_behind)
    y_low, y_high = from_y(low, 1), from_y(high, -1)

    y_index, z_index = lax.axis_index("y"), lax.axis_index("zl")
    y_place = (y_index + jnp.array(Y_STEPS, jnp.int32)) % 4
    z_place = (z_index + jnp.array(Z_STEPS, jnp.int32)) % 8
    place = (y_place[:, None] * 8 + z_place[None, :]).reshape(32).astype(jnp.int32)
    gain_row = norm_gain.reshape(1, width)
    total, near_base = call(
        near_kernel,
        (struct((rows, kv), jnp.float32), struct((rows, width * 3 // 4), jnp.float32)),
        2,
        "near_layer",
    )(
        core_row, place, normed, gain_row, inv_rms, value_grad, w_z, y_ahead, y_behind,
        w_z_other, swapped(y_ahead, "core"), swapped(y_behind, "core"),
    )
    doc_low, total = lax.optimization_barrier((doc_low, total))
    values_out, hidden_grad = call(
        far_kernel,
        (struct((rows, kv), jnp.bfloat16), struct((rows, width), jnp.bfloat16)),
        2,
        "far_layer",
    )(
        core_row, place, normed, hidden_in, gain_row, inv_rms, value_grad, total, near_base,
        y_low, y_high, swapped(y_low, "core"), swapped(y_high, "core"),
    )
    score_index = jnp.stack([lax.axis_index("zh"), lax.axis_index("x")]).astype(jnp.int32)
    scores = call(score_kernel, struct((8, 8 * queries.shape[0]), jnp.float32), 1, "scores")(
        score_index, doc_low, q_here, *q_turns
    )
    return (values_out, hidden_grad, scores)


def solution(mesh):
    fine = Mesh(mesh.devices.reshape(4, 8, 2, 2, 4), DP + SCORE)
    tokens = SCORE + DP
    placed = (
        P(tokens, None),
        P(),
        P(DP, None),
        P(DP, None),
        P(tokens, None),
        P(),
        P(tokens),
        P(DP + SCORE, None),
    )
    return jax.shard_map(
        shards,
        mesh=fine,
        in_specs=placed,
        out_specs=(P(tokens, None), P(tokens, None), P(SCORE, DP)),
        check_vma=False,
    )
```

time: 214 us -> 193 us (0.902)
  waiting for transfers between devices: 70.1 us -> 24.3 us
  starting transfers between devices: 75.8 us -> 114 us
  between operations: 14.4 us -> 1.16 us
  local copies, waits for them, and re-layouts: 28.4 us -> 19.6 us
  Pallas kernels: 9.9 us -> 18.5 us
  matrix products: 5.22 us -> 2.25 us
    ppermute x2 -> x7, starting transfers between devices: 10 us -> 30.9 us  [swapped(): return lax.ppermute(value, axis, [(0, 1), (1, 0)])]
    all_to_all x1, waiting for transfers between devices: 18.1 us -> 0.01 us  [shards(): lax.all_to_all(left_t.reshape(8, rank // 8, rows), ('y', 'core'), 0, 0, t...]
    ppermute x4, waiting for transfers between devices: 20.9 us -> 6.92 us  [from_z(): lax.ppermute(value, ('zl', 'zh'), [(place((z + step) % 16), place(z)) for...]
    ppermute x0 -> x3, starting transfers between devices: none -> 11.1 us  [from_x(): return lax.ppermute(value, 'x', [((x + step) % 4, x) for x in range(4)])]
    all_gather x1 -> x0, waiting for transfers between devices: 11 us -> none  [shards(): q_all = lax.all_gather(queries, SCORE, axis=0, tiled=True)]
    all_to_all x0 -> x1, starting transfers between devices: none -> 10.3 us  [shards(): doc_low = lax.all_to_all(doc_copies, DP, 0, 0, tiled=True)]
    pallas_call x2 -> x8, Pallas kernels: 9.9 us -> 18.5 us  [run(): pl.pallas_call(body, out_shape=out_shape, in_specs=[smem] * scalars + [vm...]
    all_to_all x1, starting transfers between devices: 4.62 us -> 11.9 us  [shards(): lax.all_to_all(doc_term.reshape(64, 8, rank), ('zl', 'zh', 'x'), 0, 0, ti...]
  transfers between devices with their start and end apart: 16 -> 23, of which waited for: 6 -> 4; matrix products, arithmetic and copies ran while one was open for 15% -> 10% of each run, Pallas kernels for 0% -> 6%
where the time goes in v3:
time: 193 us; the launch traced here: 192 us
  starting transfers between devices  114 us (59%)
  waiting for transfers between devices  24.3 us (13%)
  local copies, waits for them, and re-layouts  19.6 us (10%)
  Pallas kernels  18.5 us (10%)
  other arithmetic  11.4 us (6%)
  matrix products  2.25 us (1%)
    ppermute x7, starting transfers between devices, swapped(): return lax.ppermute(value, axis, [(0, 1), (1, 0)])  30.9 us
    pallas_call x8, Pallas kernels, run(): pl.pallas_call(body, out_shape=out_shape, in_specs=[smem] * scalars + [vm...  18.5 us
    all_to_all x2, starting transfers between devices, spread_to_all(): return lax.all_to_all(copies, axes, 0, 0, tiled=True)  17.3 us
    ppermute x4, starting transfers between devices, from_z(): lax.ppermute(value, ('zl', 'zh'), [(place((z + step) % 16), place(z)) for...  17.2 us
    unnamed x51, local copies, waits for them, and re-layouts  14.1 us
    all_to_all x1, starting transfers between devices, shards(): lax.all_to_all(doc_term.reshape(64, 8, rank), ('zl', 'zh', 'x'), 0, 0, ti...  11.9 us
    ppermute x4, starting transfers between devices, from_y(): return lax.ppermute(value, 'y', [((y + step) % 4, y) for y in range(4)])  11.3 us
    ppermute x3, starting transfers between devices, from_x(): return lax.ppermute(value, 'x', [((x + step) % 4, x) for x in range(4)])  11.1 us
  transfers between devices with their start and end apart: 23, of which 4 were waited for; matrix products, arithmetic and copies ran while one was open for 10% of the time, Pallas kernels for 6%

profile of v3, /device:TPU:1, one launch (start us, length us, event | category | flops | bytes accessed | tf_op | source)
XLA Modules:
  0.0 191.5 jit_solution(15684646853156065609)
XLA Ops:
  2.2 13.1 %all-to-all-start = ((bf16[8,64,128]{2,1,0:T(8,128)(2,1)}), bf16[8,64,128]{2,1,0:T(8,128)(2,1)S(1)}, u32[]{:S(2)}, u32[]{:S(2)}) async-start(bf16[8,64,128]{2,1,0:T(8,128)(2,1)} %broadcast_in_dim.14), calls=%async_computation | async-start | bytes 262144 | tf_op jit(solution)/shard_map/all_to_all | solution.py:21
  15.3 3.4 %collective-permute-start = (bf16[128,512]{1,0:T(8,128)(2,1)}, bf16[128,512]{1,0:T(8,128)(2,1)S(1)}, u32[]{:S(2)}, u32[]{:S(2)}) collective-permute-start(bf16[128,512]{1,0:T(8,128)(2,1)} %refs_0_.1), channel_id=1, source_target_pairs={{116,0},{0,16},{16,32},{32,48},{48,64},{64,80},{80,96},{96,112},{1... | collective-permute-start | bytes 393224 | tf_op jit(solution)/shard_map/ppermute | solution.py:36
  18.6 6.8 %collective-permute-start.1 = (bf16[128,512]{1,0:T(8,128)(2,1)}, bf16[128,512]{1,0:T(8,128)(2,1)S(1)}, u32[]{:S(2)}, u32[]{:S(2)}) collective-permute-start(bf16[128,512]{1,0:T(8,128)(2,1)} %refs_0_.1), channel_id=1, source_target_pairs={{16,0},{32,16},{48,32},{64,48},{80,64},{96,80},{112,96},{4,112},{2... | collective-permute-start | bytes 393224 | tf_op jit(solution)/shard_map/ppermute | solution.py:36
  28.1 4.2 %all-to-all-start.1 = ((bf16[4,592,128]{2,1,0:T(8,128)(2,1)}), bf16[4,592,128]{2,1,0:T(8,128)(2,1)S(1)}, u32[]{:S(2)}, u32[]{:S(2)}) async-start(bf16[4,592,128]{2,1,0:T(8,128)(2,1)} %broadcast_in_dim.16), calls=%async_computation.1 | async-start | bytes 1212416 | tf_op jit(solution)/shard_map/all_to_all | solution.py:21
  33.3 7.3 %all-to-all-done.1.own_ref = bf16[4,592,128]{2,1,0:T(8,128)(2,1)S(1)} async-done(((bf16[4,592,128]{2,1,0:T(8,128)(2,1)}), bf16[4,592,128]{2,1,0:T(8,128)(2,1)S(1)}, u32[]{:S(2)}, u32[]{:S(2)}) %all-to-all-start.1) | async-done | bytes 606240 | tf_op jit(solution)/shard_map/all_to_all | solution.py:21
  40.6 4.9 %collective-permute-start.4 = (bf16[4,592,128]{2,1,0:T(8,128)(2,1)S(1)}, bf16[4,592,128]{2,1,0:T(8,128)(2,1)}, u32[]{:S(2)}, u32[]{:S(2)}) collective-permute-start(bf16[4,592,128]{2,1,0:T(8,128)(2,1)S(1)} %all-to-all-done.1.own_ref), channel_id=1, source_target_pairs={{0,8},{8,0},{1,9},{9,1},{2,10},{10,2},{3,11},{11,3},{4,12},{12,4},... | collective-permute-start | bytes 1818632 | tf_op jit(solution)/shard_map/ppermute | solution.py:25
  48.5 3.4 %collective-permute-start.2 = (bf16[384,512]{1,0:T(8,128)(2,1)S(1)}, bf16[384,512]{1,0:T(8,128)(2,1)S(1)}, u32[]{:S(2)}, u32[]{:S(2)}) collective-permute-start(bf16[384,512]{1,0:T(8,128)(2,1)S(1)} %near_three.1.refs_0_), channel_id=1, source_target_pairs={{48,0},{64,16},{80,32},{96,48},{112,64},{4,80},{20,96},{36,112},{5... | collective-permute-start | bytes 1179656 | tf_op jit(solution)/shard_map/ppermute | solution.py:36
  51.9 3.7 %collective-permute-start.3 = (bf16[256,512]{1,0:T(8,128)(2,1)}, bf16[256,512]{1,0:T(8,128)(2,1)}, u32[]{:S(2)}, u32[]{:S(2)}) collective-permute-start(bf16[256,512]{1,0:T(8,128)(2,1)} %near_two.1), channel_id=1, source_target_pairs={{84,0},{100,16},{116,32},{0,48},{16,64},{32,80},{48,96},{64,112},{... | collective-permute-start | bytes 786440 | tf_op jit(solution)/shard_map/ppermute | solution.py:36
  58.2 4.4 %all-to-all-start.2 = ((f32[8,8,128]{2,1,0:T(8,128)}), f32[8,8,128]{2,1,0:T(8,128)}, u32[]{:S(2)}, u32[]{:S(2)}) async-start(f32[8,8,128]{2,1,0:T(8,128)} %bitcast.38), calls=%async_computation.2 | async-start | bytes 65536 | tf_op jit(solution)/shard_map/all_to_all | solution.py:222
  64.3 6.5 %collective-permute-start.7 = (bf16[16,4096]{1,0:T(8,128)(2,1)}, bf16[16,4096]{1,0:T(8,128)(2,1)}, u32[]{:S(2)}, u32[]{:S(2)}) collective-permute-start(bf16[16,4096]{1,0:T(8,128)(2,1)} %param.17), channel_id=1, source_target_pairs={{0,4},{4,0},{1,5},{5,1},{2,6},{6,2},{3,7},{7,3},{8,12},{12,8},{9,1... | collective-permute-start | bytes 393224 | tf_op jit(solution)/shard_map/ppermute | solution.py:25
  70.8 6.9 %collective-permute-done.3.refs_2_ = bf16[256,512]{1,0:T(8,128)(2,1)} collective-permute-done((bf16[256,512]{1,0:T(8,128)(2,1)}, bf16[256,512]{1,0:T(8,128)(2,1)}, u32[]{:S(2)}, u32[]{:S(2)}) %collective-permute-start.3) | collective-permute-done | bytes 262176 | tf_op jit(solution)/shard_map/ppermute | solution.py:36
  83.5 3.3 %collective-permute-start.6 = (bf16[1024,512]{1,0:T(8,128)(2,1)S(1)}, bf16[1024,512]{1,0:T(8,128)(2,1)}, u32[]{:S(2)}, u32[]{:S(2)}) collective-permute-start(bf16[1024,512]{1,0:T(8,128)(2,1)S(1)} %along_z.1.refs_0_), channel_id=1, source_target_pairs={{384,0},{0,128},{128,256},{256,384},{385,1},{1,129},{129,257},{257... | collective-permute-start | bytes 3145736 | tf_op jit(solution)/shard_map/ppermute | solution.py:29
  86.8 8.4 %collective-permute-start.11 = (bf16[1024,512]{1,0:T(8,128)(2,1)S(1)}, bf16[1024,512]{1,0:T(8,128)(2,1)}, u32[]{:S(2)}, u32[]{:S(2)}) collective-permute-start(bf16[1024,512]{1,0:T(8,128)(2,1)S(1)} %along_z.1.refs_0_), channel_id=1, source_target_pairs={{0,8},{8,0},{1,9},{9,1},{2,10},{10,2},{3,11},{11,3},{4,12},{12,4},... | collective-permute-start | bytes 3145736 | tf_op jit(solution)/shard_map/ppermute | solution.py:25
  99.1 4.5 %collective-permute-start.8 = (bf16[32,4096]{1,0:T(8,128)(2,1)}, bf16[32,4096]{1,0:T(8,128)(2,1)}, u32[]{:S(2)}, u32[]{:S(2)}) collective-permute-start(bf16[32,4096]{1,0:T(8,128)(2,1)} %pad_maximum_fusion.here_ref), channel_id=1, source_target_pairs={{1,0},{2,1},{3,2},{0,3},{5,4},{6,5},{7,6},{4,7},{9,8},{10,9},{11,1... | collective-permute-start | bytes 786440 | tf_op jit(solution)/shard_map/ppermute | solution.py:180
  106.3 11.9 %all-to-all-start.3 = ((f32[64,1,512]{2,1,0:T(1,128)}), f32[64,1,512]{2,1,0:T(1,128)S(1)}, u32[]{:S(2)}, u32[]{:S(2)}) async-start(f32[64,1,512]{2,1,0:T(1,128)} %reshape.110), calls=%async_computation.3 | async-start | bytes 262144 | tf_op jit(solution)/shard_map/all_to_all | solution.py:245
  118.2 4.4 %collective-permute-start.9 = (bf16[32,4096]{1,0:T(8,128)(2,1)}, bf16[32,4096]{1,0:T(8,128)(2,1)}, u32[]{:S(2)}, u32[]{:S(2)}) collective-permute-start(bf16[32,4096]{1,0:T(8,128)(2,1)} %pad_maximum_fusion.here_ref), channel_id=1, source_target_pairs={{2,0},{3,1},{0,2},{1,3},{6,4},{7,5},{4,6},{5,7},{10,8},{11,9},{8,1... | collective-permute-start | bytes 786440 | tf_op jit(solution)/shard_map/ppermute | solution.py:180
  124.8 8.9 %all-to-all-done.3 = f32[64,1,512]{2,1,0:T(1,128)S(1)} async-done(((f32[64,1,512]{2,1,0:T(1,128)}), f32[64,1,512]{2,1,0:T(1,128)S(1)}, u32[]{:S(2)}, u32[]{:S(2)}) %all-to-all-start.3) | async-done | bytes 131104 | tf_op jit(solution)/shard_map/all_to_all | solution.py:245
  139.3 2.5 %far_halves.1 = (bf16[512,512]{1,0:T(8,128)(2,1)}, bf16[512,512]{1,0:T(8,128)(2,1)}) custom-call(bf16[1024,512]{1,0:T(8,128)(2,1)} %collective-permute-done.5.refs_1_.ahead_ref, bf16[1024,512]{1,0:T(8,128)(2,1)} %collective-permute-done.6.refs_2_.behind_ref), custom_call_target="tpu_custom_call" | custom-call | tf_op jit(solution)/shard_map/far_halves/pallas_call | solution.py:167
  141.9 4.1 %collective-permute-start.14 = (bf16[512,512]{1,0:T(8,128)(2,1)}, bf16[512,512]{1,0:T(8,128)(2,1)}, u32[]{:S(2)}, u32[]{:S(2)}) collective-permute-start(bf16[512,512]{1,0:T(8,128)(2,1)} %get-tuple-element.39), channel_id=1, source_target_pairs={{128,0},{256,128},{384,256},{0,384},{129,1},{257,129},{385,257},{1... | collective-permute-start | bytes 1572872 | tf_op jit(solution)/shard_map/ppermute | solution.py:29
  147.9 4.7 %collective-permute-start.12 = (bf16[1024,512]{1,0:T(8,128)(2,1)}, bf16[1024,512]{1,0:T(8,128)(2,1)}, u32[]{:S(2)}, u32[]{:S(2)}) collective-permute-start(bf16[1024,512]{1,0:T(8,128)(2,1)} %collective-permute-done.5.refs_1_.ahead_ref), channel_id=1, source_target_pairs={{0,8},{8,0},{1,9},{9,1},{2,10},{10,2},{3,11},{11,3},{4,12},{12,4},... | collective-permute-start | bytes 3145736 | tf_op jit(solution)/shard_map/ppermute | solution.py:25
  154.5 10.3 %all-to-all-start.4 = ((bf16[64,8,128]{2,1,0:T(8,128)(2,1)}), bf16[64,8,128]{2,1,0:T(8,128)(2,1)S(1)}, u32[]{:S(2)}, u32[]{:S(2)}) async-start(bf16[64,8,128]{2,1,0:T(8,128)(2,1)} %broadcast_in_dim.17), calls=%async_computation.4 | async-start | bytes 262144 | tf_op jit(solution)/shard_map/all_to_all | solution.py:256
  164.8 2.4 %collective-permute-start.16 = (bf16[512,512]{1,0:T(8,128)(2,1)}, bf16[512,512]{1,0:T(8,128)(2,1)}, u32[]{:S(2)}, u32[]{:S(2)}) collective-permute-start(bf16[512,512]{1,0:T(8,128)(2,1)} %collective-permute-done.14.own_low), channel_id=1, source_target_pairs={{0,8},{8,0},{1,9},{9,1},{2,10},{10,2},{3,11},{11,3},{4,12},{12,4},... | collective-permute-start | bytes 1572872 | tf_op jit(solution)/shard_map/ppermute | solution.py:25
  170.5 5.4 %near_layer.1 = (f32[128,512]{1,0:T(8,128)S(1)}, f32[128,6144]{1,0:T(8,128)S(1)}) custom-call(s32[1]{0:T(128)} %bitcast.core_ref, s32[32]{0:T(128)S(1)} %add.66.place_ref, bf16[128,8192]{1,0:T(8,128)(2,1)S(1)} %fusion.2.normed_ref, f32[1,8192]{1,0:T(1,128)S(1)} %bitcast.36, f32[128,1]{1,0:T(8,128)S(1)} %copy.25.scale_ref, bf16[128,512]{1,0:T(8,128)(2,1)S(1)} %copy-done.7, ...), custom_call_target="tpu_custom_call" | custom-call | tf_op jit(solution)/shard_map/near_layer/pallas_call | solution.py:167
  186.9 4.7 %far_layer.1 = (bf16[128,512]{1,0:T(8,128)(2,1)}, bf16[128,8192]{1,0:T(8,128)(2,1)}) custom-call(s32[1]{0:T(128)} %bitcast.core_ref, s32[32]{0:T(128)S(1)} %add.66.place_ref, bf16[128,8192]{1,0:T(8,128)(2,1)S(1)} %fusion.2.normed_ref, bf16[128,8192]{1,0:T(8,128)(2,1)S(1)} %copy-done.2, f32[1,8192]{1,0:T(1,128)S(1)} %bitcast.37, ...), custom_call_target="tpu_custom_call" | custom-call | tf_op jit(solution)/shard_map/far_layer/pallas_call | solution.py:167
  (112 shorter events, 50.6 us)
Async XLA Ops:
  2.2 25.0 %all-to-all-start = ((bf16[8,64,128]{2,1,0:T(8,128)(2,1)}), bf16[8,64,128]{2,1,0:T(8,128)(2,1)S(1)}, u32[]{:S(2)}, u32[]{:S(2)}) async-start(bf16[8,64,128]{2,1,0:T(8,128)(2,1)} %broadcast_in_dim.14), calls=%async_computation | async-start | bytes 262144 | tf_op jit(solution)/shard_map/all_to_all | solution.py:21
  15.3 33.2 %collective-permute-start = (bf16[128,512]{1,0:T(8,128)(2,1)}, bf16[128,512]{1,0:T(8,128)(2,1)S(1)}, u32[]{:S(2)}, u32[]{:S(2)}) collective-permute-start(bf16[128,512]{1,0:T(8,128)(2,1)} %refs_0_.1), channel_id=1, source_target_pairs={{116,0},{0,16},{16,32},{32,48},{48,64},{64,80},{80,96},{96,112},{1... | collective-permute-start | bytes 393224 | tf_op jit(solution)/shard_map/ppermute | solution.py:36
  18.6 29.1 %collective-permute-start.1 = (bf16[128,512]{1,0:T(8,128)(2,1)}, bf16[128,512]{1,0:T(8,128)(2,1)S(1)}, u32[]{:S(2)}, u32[]{:S(2)}) collective-permute-start(bf16[128,512]{1,0:T(8,128)(2,1)} %refs_0_.1), channel_id=1, source_target_pairs={{16,0},{32,16},{48,32},{64,48},{80,64},{96,80},{112,96},{4,112},{2... | collective-permute-start | bytes 393224 | tf_op jit(solution)/shard_map/ppermute | solution.py:36
  28.1 12.5 %all-to-all-start.1 = ((bf16[4,592,128]{2,1,0:T(8,128)(2,1)}), bf16[4,592,128]{2,1,0:T(8,128)(2,1)S(1)}, u32[]{:S(2)}, u32[]{:S(2)}) async-start(bf16[4,592,128]{2,1,0:T(8,128)(2,1)} %broadcast_in_dim.16), calls=%async_computation.1 | async-start | bytes 1212416 | tf_op jit(solution)/shard_map/all_to_all | solution.py:21
  40.6 15.0 %collective-permute-start.4 = (bf16[4,592,128]{2,1,0:T(8,128)(2,1)S(1)}, bf16[4,592,128]{2,1,0:T(8,128)(2,1)}, u32[]{:S(2)}, u32[]{:S(2)}) collective-permute-start(bf16[4,592,128]{2,1,0:T(8,128)(2,1)S(1)} %all-to-all-done.1.own_ref), channel_id=1, source_target_pairs={{0,8},{8,0},{1,9},{9,1},{2,10},{10,2},{3,11},{11,3},{4,12},{12,4},... | collective-permute-start | bytes 1818632 | tf_op jit(solution)/shard_map/ppermute | solution.py:25
  48.5 29.1 %collective-permute-start.2 = (bf16[384,512]{1,0:T(8,128)(2,1)S(1)}, bf16[384,512]{1,0:T(8,128)(2,1)S(1)}, u32[]{:S(2)}, u32[]{:S(2)}) collective-permute-start(bf16[384,512]{1,0:T(8,128)(2,1)S(1)} %near_three.1.refs_0_), channel_id=1, source_target_pairs={{48,0},{64,16},{80,32},{96,48},{112,64},{4,80},{20,96},{36,112},{5... | collective-permute-start | bytes 1179656 | tf_op jit(solution)/shard_map/ppermute | solution.py:36
  51.9 25.8 %collective-permute-start.3 = (bf16[256,512]{1,0:T(8,128)(2,1)}, bf16[256,512]{1,0:T(8,128)(2,1)}, u32[]{:S(2)}, u32[]{:S(2)}) collective-permute-start(bf16[256,512]{1,0:T(8,128)(2,1)} %near_two.1), channel_id=1, source_target_pairs={{84,0},{100,16},{116,32},{0,48},{16,64},{32,80},{48,96},{64,112},{... | collective-permute-start | bytes 786440 | tf_op jit(solution)/shard_map/ppermute | solution.py:36
  58.2 20.3 %all-to-all-start.2 = ((f32[8,8,128]{2,1,0:T(8,128)}), f32[8,8,128]{2,1,0:T(8,128)}, u32[]{:S(2)}, u32[]{:S(2)}) async-start(f32[8,8,128]{2,1,0:T(8,128)} %bitcast.38), calls=%async_computation.2 | async-start | bytes 65536 | tf_op jit(solution)/shard_map/all_to_all | solution.py:222
  64.3 33.2 %collective-permute-start.7 = (bf16[16,4096]{1,0:T(8,128)(2,1)}, bf16[16,4096]{1,0:T(8,128)(2,1)}, u32[]{:S(2)}, u32[]{:S(2)}) collective-permute-start(bf16[16,4096]{1,0:T(8,128)(2,1)} %param.17), channel_id=1, source_target_pairs={{0,4},{4,0},{1,5},{5,1},{2,6},{6,2},{3,7},{7,3},{8,12},{12,8},{9,1... | collective-permute-start | bytes 393224 | tf_op jit(solution)/shard_map/ppermute | solution.py:25
  81.5 57.2 %collective-permute-start.5 = (bf16[1024,512]{1,0:T(8,128)(2,1)S(1)}, bf16[1024,512]{1,0:T(8,128)(2,1)}, u32[]{:S(2)}, u32[]{:S(2)}) collective-permute-start(bf16[1024,512]{1,0:T(8,128)(2,1)S(1)} %along_z.1.refs_0_), channel_id=1, source_target_pairs={{128,0},{256,128},{384,256},{0,384},{129,1},{257,129},{385,257},{1... | collective-permute-start | bytes 3145736 | tf_op jit(solution)/shard_map/ppermute | solution.py:29
  83.5 55.2 %collective-permute-start.6 = (bf16[1024,512]{1,0:T(8,128)(2,1)S(1)}, bf16[1024,512]{1,0:T(8,128)(2,1)}, u32[]{:S(2)}, u32[]{:S(2)}) collective-permute-start(bf16[1024,512]{1,0:T(8,128)(2,1)S(1)} %along_z.1.refs_0_), channel_id=1, source_target_pairs={{384,0},{0,128},{128,256},{256,384},{385,1},{1,129},{129,257},{257... | collective-permute-start | bytes 3145736 | tf_op jit(solution)/shard_map/ppermute | solution.py:29
  86.8 50.7 %collective-permute-start.11 = (bf16[1024,512]{1,0:T(8,128)(2,1)S(1)}, bf16[1024,512]{1,0:T(8,128)(2,1)}, u32[]{:S(2)}, u32[]{:S(2)}) collective-permute-start(bf16[1024,512]{1,0:T(8,128)(2,1)S(1)} %along_z.1.refs_0_), channel_id=1, source_target_pairs={{0,8},{8,0},{1,9},{9,1},{2,10},{10,2},{3,11},{11,3},{4,12},{12,4},... | collective-permute-start | bytes 3145736 | tf_op jit(solution)/shard_map/ppermute | solution.py:25
  99.1 23.5 %collective-permute-start.8 = (bf16[32,4096]{1,0:T(8,128)(2,1)}, bf16[32,4096]{1,0:T(8,128)(2,1)}, u32[]{:S(2)}, u32[]{:S(2)}) collective-permute-start(bf16[32,4096]{1,0:T(8,128)(2,1)} %pad_maximum_fusion.here_ref), channel_id=1, source_target_pairs={{1,0},{2,1},{3,2},{0,3},{5,4},{6,5},{7,6},{4,7},{9,8},{10,9},{11,1... | collective-permute-start | bytes 786440 | tf_op jit(solution)/shard_map/ppermute | solution.py:180
  104.5 65.3 %copy-start.7 = (bf16[128,512]{1,0:T(8,128)(2,1)S(1)}, bf16[128,512]{1,0:T(8,128)(2,1)}, u32[]{:S(2)}) copy-start(bf16[128,512]{1,0:T(8,128)(2,1)} %grad_ref.3) | copy-start | bytes 393220
  106.3 27.4 %all-to-all-start.3 = ((f32[64,1,512]{2,1,0:T(1,128)}), f32[64,1,512]{2,1,0:T(1,128)S(1)}, u32[]{:S(2)}, u32[]{:S(2)}) async-start(f32[64,1,512]{2,1,0:T(1,128)} %reshape.110), calls=%async_computation.3 | async-start | bytes 262144 | tf_op jit(solution)/shard_map/all_to_all | solution.py:245
  118.2 19.3 %collective-permute-start.9 = (bf16[32,4096]{1,0:T(8,128)(2,1)}, bf16[32,4096]{1,0:T(8,128)(2,1)}, u32[]{:S(2)}, u32[]{:S(2)}) collective-permute-start(bf16[32,4096]{1,0:T(8,128)(2,1)} %pad_maximum_fusion.here_ref), channel_id=1, source_target_pairs={{2,0},{3,1},{0,2},{1,3},{6,4},{7,5},{4,6},{5,7},{10,8},{11,9},{8,1... | collective-permute-start | bytes 786440 | tf_op jit(solution)/shard_map/ppermute | solution.py:180
  122.6 14.9 %collective-permute-start.10 = (bf16[32,4096]{1,0:T(8,128)(2,1)}, bf16[32,4096]{1,0:T(8,128)(2,1)}, u32[]{:S(2)}, u32[]{:S(2)}) collective-permute-start(bf16[32,4096]{1,0:T(8,128)(2,1)} %pad_maximum_fusion.here_ref), channel_id=1, source_target_pairs={{3,0},{0,1},{1,2},{2,3},{7,4},{4,5},{5,6},{6,7},{11,8},{8,9},{9,10... | collective-permute-start | bytes 786440 | tf_op jit(solution)/shard_map/ppermute | solution.py:180
  141.9 23.0 %collective-permute-start.14 = (bf16[512,512]{1,0:T(8,128)(2,1)}, bf16[512,512]{1,0:T(8,128)(2,1)}, u32[]{:S(2)}, u32[]{:S(2)}) collective-permute-start(bf16[512,512]{1,0:T(8,128)(2,1)} %get-tuple-element.39), channel_id=1, source_target_pairs={{128,0},{256,128},{384,256},{0,384},{129,1},{257,129},{385,257},{1... | collective-permute-start | bytes 1572872 | tf_op jit(solution)/shard_map/ppermute | solution.py:29
  145.9 21.3 %collective-permute-start.15 = (bf16[512,512]{1,0:T(8,128)(2,1)}, bf16[512,512]{1,0:T(8,128)(2,1)}, u32[]{:S(2)}, u32[]{:S(2)}) collective-permute-start(bf16[512,512]{1,0:T(8,128)(2,1)} %get-tuple-element.40), channel_id=1, source_target_pairs={{384,0},{0,128},{128,256},{256,384},{385,1},{1,129},{129,257},{257... | collective-permute-start | bytes 1572872 | tf_op jit(solution)/shard_map/ppermute | solution.py:29
  147.9 21.9 %collective-permute-start.12 = (bf16[1024,512]{1,0:T(8,128)(2,1)}, bf16[1024,512]{1,0:T(8,128)(2,1)}, u32[]{:S(2)}, u32[]{:S(2)}) collective-permute-start(bf16[1024,512]{1,0:T(8,128)(2,1)} %collective-permute-done.5.refs_1_.ahead_ref), channel_id=1, source_target_pairs={{0,8},{8,0},{1,9},{9,1},{2,10},{10,2},{3,11},{11,3},{4,12},{12,4},... | collective-permute-start | bytes 3145736 | tf_op jit(solution)/shard_map/ppermute | solution.py:25
  152.6 17.2 %collective-permute-start.13 = (bf16[1024,512]{1,0:T(8,128)(2,1)}, bf16[1024,512]{1,0:T(8,128)(2,1)}, u32[]{:S(2)}, u32[]{:S(2)}) collective-permute-start(bf16[1024,512]{1,0:T(8,128)(2,1)} %collective-permute-done.6.refs_2_.behind_ref), channel_id=1, source_target_pairs={{0,8},{8,0},{1,9},{9,1},{2,10},{10,2},{3,11},{11,3},{4,12},{12,4},... | collective-permute-start | bytes 3145736 | tf_op jit(solution)/shard_map/ppermute | solution.py:25
  154.5 24.8 %all-to-all-start.4 = ((bf16[64,8,128]{2,1,0:T(8,128)(2,1)}), bf16[64,8,128]{2,1,0:T(8,128)(2,1)S(1)}, u32[]{:S(2)}, u32[]{:S(2)}) async-start(bf16[64,8,128]{2,1,0:T(8,128)(2,1)} %broadcast_in_dim.17), calls=%async_computation.4 | async-start | bytes 262144 | tf_op jit(solution)/shard_map/all_to_all | solution.py:256
  164.8 16.8 %collective-permute-start.16 = (bf16[512,512]{1,0:T(8,128)(2,1)}, bf16[512,512]{1,0:T(8,128)(2,1)}, u32[]{:S(2)}, u32[]{:S(2)}) collective-permute-start(bf16[512,512]{1,0:T(8,128)(2,1)} %collective-permute-done.14.own_low), channel_id=1, source_target_pairs={{0,8},{8,0},{1,9},{9,1},{2,10},{10,2},{3,11},{11,3},{4,12},{12,4},... | collective-permute-start | bytes 1572872 | tf_op jit(solution)/shard_map/ppermute | solution.py:25
  167.2 14.5 %collective-permute-start.17 = (bf16[512,512]{1,0:T(8,128)(2,1)}, bf16[512,512]{1,0:T(8,128)(2,1)}, u32[]{:S(2)}, u32[]{:S(2)}) collective-permute-start(bf16[512,512]{1,0:T(8,128)(2,1)} %collective-permute-done.15.own_high), channel_id=1, source_target_pairs={{0,8},{8,0},{1,9},{9,1},{2,10},{10,2},{3,11},{11,3},{4,12},{12,4},... | collective-permute-start | bytes 1572872 | tf_op jit(solution)/shard_map/ppermute | solution.py:25
  (24 other events, 330.5 us)

commit v4 on v3

v4 whole, which is shorter than its diff:
```python
import jax
import jax.numpy as jnp
from jax import lax
from jax.experimental import pallas as pl
from jax.experimental.pallas import tpu as pltpu
from jax.sharding import Mesh
from jax.sharding import PartitionSpec as P

EPSILON = 1e-05
DP = ("y", "zl", "core")
SCORE = ("zh", "x")
BLOCK = 128
LIMIT = 32 * 1024 * 1024


def spread_to_all(value, axes):
    count = lax.axis_size(axes)
    copies = jnp.broadcast_to(value[None], (count,) + value.shape)
    return lax.all_to_all(copies, axes, 0, 0, tiled=True)


def swapped(value, axis):
    return lax.ppermute(value, axis, [(0, 1), (1, 0)])


def contract_last(left_side, right_side):
    return lax.dot_general(
        left_side, right_side, (((1,), (1,)), ((), ())), preferred_element_type=jnp.float32
    )


def ordered(first, own, other):
    return jnp.where(first, own, other), jnp.where(first, other, own)


def after(value, earlier):
    return lax.optimization_barrier((value, earlier))[0]


def left_kernel(core_ref, normed_ref, own_ref, other_ref, left_ref):
    first = core_ref[0] == 0
    rank = left_ref.shape[0]
    total = jnp.zeros(left_ref.shape, jnp.float32)
    for pair in range(32):
        y, z = divmod(pair, 8)
        own = own_ref[y, z * rank : (z + 1) * rank]
        other = other_ref[y, z * rank : (z + 1) * rank]
        factor = jnp.concatenate(ordered(first, own, other), 1)
        total += contract_last(factor, normed_ref[:, pair * 256 : (pair + 1) * 256])
    left_ref[...] = total


def layer_kernel(
    normed_ref, hidden_ref, gain_ref, scale_ref, grad_ref, weight_ref,
    values_ref, hidden_grad_ref, held, base, wide_in, arrived,
):
    chunks = held.shape[0]
    depth = held.shape[1]
    width = normed_ref.shape[1]
    copies = [
        pltpu.make_async_copy(
            weight_ref.at[pl.ds(chunk * depth, depth)], held.at[chunk], arrived.at[chunk]
        )
        for chunk in range(chunks)
    ]
    for copy in copies:
        copy.start()
    hidden_copy = pltpu.make_async_copy(hidden_ref, wide_in, arrived.at[chunks])
    hidden_copy.start()
    grad = grad_ref[...]
    inv_rms = scale_ref[...]
    total = jnp.zeros(values_ref.shape, jnp.float32)
    for chunk, copy in enumerate(copies):
        copy.wait()
        for start in range(0, depth, 256):
            where = slice(chunk * depth + start, chunk * depth + start + 256)
            weight = held[chunk, start : start + 256]
            total += jnp.dot(normed_ref[:, where], weight, preferred_element_type=jnp.float32)
            base[:, where] = inv_rms * (contract_last(grad, weight) * gain_ref[:, where])
    values_ref[...] = total.astype(jnp.bfloat16)
    along = jnp.sum(total * grad.astype(jnp.float32), axis=1, keepdims=True)
    pull = inv_rms * inv_rms * along / width
    hidden_copy.wait()
    for start in range(0, width, 512):
        where = slice(start, start + 512)
        wide = wide_in[:, where].astype(jnp.float32)
        hidden_grad_ref[:, where] = (base[:, where] - wide * pull).astype(jnp.bfloat16)


def score_kernel(index_ref, docs_ref, here_ref, one_ref, two_ref, three_ref, scores_ref):
    lane = lax.broadcasted_iota(jnp.int32, docs_ref.shape[1:], 1)
    low = lane < docs_ref.shape[2] // 2
    pieces = []
    for pair in range(docs_ref.shape[0] // 2):
        even = docs_ref[2 * pair].astype(jnp.float32)
        odd = docs_ref[2 * pair + 1].astype(jnp.float32)
        pieces.append(jnp.where(low, even, odd).astype(jnp.bfloat16))
    docs = jnp.concatenate(pieces, 1)
    found = [contract_last(docs, ref[...]) for ref in (here_ref, one_ref, two_ref, three_ref)]
    size = here_ref.shape[0] // 2
    mine = [piece[:, :size] for piece in found]
    others = [piece[:, size:] for piece in found]
    zh, x = index_ref[0], index_ref[1]
    result = jnp.zeros(scores_ref.shape, jnp.float32)
    for turn in range(4):
        order = [(place - turn) % 4 for place in range(4)]
        one_half = [mine[step] for step in order]
        other_half = [others[step] for step in order]
        for side, parts in ((0, one_half + other_half), (1, other_half + one_half)):
            chosen = jnp.logical_and(zh == side, x == turn)
            result = jnp.where(chosen, jnp.concatenate(parts, 1), result)
    scores_ref[...] = result


def call(body, out_shape, scalars, name, limit=LIMIT):
    def run(*operands):
        smem = pl.BlockSpec(memory_space=pltpu.SMEM)
        vmem = pl.BlockSpec(memory_space=pltpu.VMEM)
        return pl.pallas_call(
            body,
            out_shape=out_shape,
            in_specs=[smem] * scalars + [vmem] * (len(operands) - scalars),
            out_specs=jax.tree.map(lambda _: vmem, out_shape),
            compiler_params=pltpu.CompilerParams(vmem_limit_bytes=limit),
            name=name,
        )(*operands)

    return run


def from_x(value, step):
    return lax.ppermute(value, "x", [((x + step) % 4, x) for x in range(4)])


def struct(shape, dtype):
    return jax.ShapeDtypeStruct(shape, dtype)


def shards(
    hidden_in, norm_gain, value_weight, input_proj, value_grad, output_proj, doc_ids, queries
):
    rows, width = hidden_in.shape
    kv = value_weight.shape[1]
    rank = input_proj.shape[1]
    core = lax.axis_index("core")
    core_row = core.astype(jnp.int32).reshape(1)
    on_first = core == 0

    factor = input_proj.T.reshape(4, 8, 2, BLOCK).transpose(0, 2, 1, 3).reshape(rank, BLOCK)
    right_t = lax.dot_general(
        output_proj, value_grad, (((0,), (1,)), ((), ())), preferred_element_type=jnp.float32
    ).astype(jnp.bfloat16)
    ids_rows = jnp.broadcast_to(doc_ids.astype(jnp.bfloat16)[None], (16, rows))
    factor_z = spread_to_all(factor, "zl").reshape(-1, BLOCK)
    packed = spread_to_all(jnp.concatenate([factor_z, right_t, ids_rows], 0), "y")
    packed_other = swapped(packed, "core")

    w_all = lax.all_gather(value_weight, DP, axis=0, tiled=True)

    wide_in = hidden_in.astype(jnp.float32)
    inv_rms = lax.rsqrt(jnp.mean(wide_in * wide_in, axis=1, keepdims=True) + EPSILON)
    normed = (wide_in * inv_rms * norm_gain).astype(jnp.bfloat16)
    left_t = call(left_kernel, struct((rank, rows), jnp.float32), 1, "left_factor")(
        core_row, normed, packed, packed_other
    )

    q_other = swapped(after(queries, left_t), "zh")

    left_all = lax.all_to_all(
        left_t.reshape(8, rank // 8, rows), ("y", "core"), 0, 0, tiled=True
    )

    base = 8 * rank
    tail = jnp.stack(ordered(on_first, packed[:, base:], packed_other[:, base:]), 1)
    tail = tail.reshape(8, -1, rows).astype(jnp.float32)
    right_flat = tail[:, :rank].transpose(1, 0, 2).reshape(rank, -1)
    ids_all = tail[:, rank].reshape(1, -1)
    left_flat = left_all.transpose(1, 0, 2).reshape(8, 1, -1)
    doc_count = 64
    doc_range = jnp.arange(doc_count, dtype=jnp.float32)[:, None]
    onehot = (ids_all == doc_range).astype(jnp.float32)
    spread = (onehot[None] * left_flat).reshape(8 * doc_count, -1)
    doc_term = lax.dot_general(
        spread, right_flat, (((1,), (1,)), ((), ())), precision=lax.Precision.HIGHEST
    )
    doc_parts = lax.all_to_all(
        doc_term.reshape(64, 8, rank), ("zl", "zh", "x"), 0, 0, tiled=True
    )
    q_here = after(jnp.concatenate([queries, q_other], 0), doc_term)
    q_turns = [from_x(q_here, step) for step in (1, 2, 3)]
    doc_parts, q_turns = lax.optimization_barrier((doc_parts, q_turns))
    own_docs = jnp.sum(doc_parts, 0).astype(jnp.bfloat16)
    doc_low = spread_to_all(jnp.concatenate([own_docs, own_docs], 1), DP)

    vmem = pl.BlockSpec(memory_space=pltpu.VMEM)
    hbm = pl.BlockSpec(memory_space=pltpu.HBM)
    chunks = 8
    values_out, hidden_grad = pl.pallas_call(
        layer_kernel,
        out_shape=(struct((rows, kv), jnp.bfloat16), struct((rows, width), jnp.bfloat16)),
        in_specs=[vmem, hbm, vmem, vmem, vmem, hbm],
        out_specs=(vmem, vmem),
        scratch_shapes=[
            pltpu.VMEM((chunks, width // chunks, kv), jnp.bfloat16),
            pltpu.VMEM((rows, width), jnp.float32),
            pltpu.VMEM((rows, width), jnp.bfloat16),
            pltpu.SemaphoreType.DMA((chunks + 1,)),
        ],
        compiler_params=pltpu.CompilerParams(vmem_limit_bytes=LIMIT),
        name="layer",
    )(normed, hidden_in, norm_gain.reshape(1, width), inv_rms, value_grad, w_all)
    score_index = jnp.stack([lax.axis_index("zh"), lax.axis_index("x")]).astype(jnp.int32)
    scores = call(score_kernel, struct((8, 8 * queries.shape[0]), jnp.float32), 1, "scores")(
        score_index, doc_low, q_here, *q_turns
    )
    return (values_out, hidden_grad, scores)


def solution(mesh):
    fine = Mesh(mesh.devices.reshape(4, 8, 2, 2, 4), DP + SCORE)
    tokens = SCORE + DP
    placed = (
        P(tokens, None),
        P(),
        P(DP, None),
        P(DP, None),
        P(tokens, None),
        P(),
        P(tokens),
        P(DP + SCORE, None),
    )
    return jax.shard_map(
        shards,
        mesh=fine,
        in_specs=placed,
        out_specs=(P(tokens, None), P(tokens, None), P(SCORE, DP)),
        check_vma=False,
    )
```

time: 193 us -> 180 us (0.933)
  starting transfers between devices: 114 us -> 62.2 us
  waiting for transfers between devices: 24.3 us -> 69.1 us
  between operations: 1.16 us -> 14.3 us
  Pallas kernels: 18.5 us -> 10.9 us
  local copies, waits for them, and re-layouts: 19.6 us -> 13.4 us
  other arithmetic: 11.4 us -> 7.35 us
    all_to_all x2 -> x3, waiting for transfers between devices: 7.28 us -> 36.4 us  [spread_to_all(): return lax.all_to_all(copies, axes, 0, 0, tiled=True)]
    ppermute x8 -> x0, starting transfers between devices: 28.5 us -> none  [the longest x4 17.2 us: from_z(): lax.ppermute(value, ('zl', 'zh'), [(place((z + step) % 16), place(z)) for...]
    ppermute x7 -> x2, starting transfers between devices: 30.9 us -> 13.1 us  [swapped(): return lax.ppermute(value, axis, [(0, 1), (1, 0)])]
    all_gather x0 -> x1, waiting for transfers between devices: none -> 16 us  [shards(): w_all = lax.all_gather(value_weight, DP, axis=0, tiled=True)]
    pallas_call x8 -> x2, Pallas kernels: 18.5 us -> 3.05 us  [run(): pl.pallas_call(body, out_shape=out_shape, in_specs=[smem] * scalars + [vm...]
    all_to_all x2 -> x3, starting transfers between devices: 17.3 us -> 28 us  [spread_to_all(): return lax.all_to_all(copies, axes, 0, 0, tiled=True)]
    all_to_all x1 -> x0, starting transfers between devices: 10.3 us -> none  [shards(): doc_low = lax.all_to_all(doc_copies, DP, 0, 0, tiled=True)]
    all_to_all x1, waiting for transfers between devices: 8.86 us -> 0.27 us  [shards(): lax.all_to_all(doc_term.reshape(64, 8, rank), ('zl', 'zh', 'x'), 0, 0, ti...]
  transfers between devices with their start and end apart: 23 -> 11, of which waited for: 4 -> 8; matrix products, arithmetic and copies ran while one was open for 10% -> 8% of each run, Pallas kernels for 6% -> 2%
where the time goes in v4:
time: 180 us; the launch traced here: 179 us
  waiting for transfers between devices  69.1 us (38%)
  starting transfers between devices  62.2 us (35%)
  between operations  14.3 us (8%)
  local copies, waits for them, and re-layouts  13.4 us (7%)
  Pallas kernels  10.9 us (6%)
  other arithmetic  7.35 us (4%)
  matrix products  2.25 us (1%)
    all_to_all x3, waiting for transfers between devices, spread_to_all(): return lax.all_to_all(copies, axes, 0, 0, tiled=True)  36.4 us
    all_to_all x3, starting transfers between devices, spread_to_all(): return lax.all_to_all(copies, axes, 0, 0, tiled=True)  28 us
    all_gather x1, waiting for transfers between devices, shards(): w_all = lax.all_gather(value_weight, DP, axis=0, tiled=True)  16 us
    ppermute x2, starting transfers between devices, swapped(): return lax.ppermute(value, axis, [(0, 1), (1, 0)])  13.1 us
    ppermute x3, starting transfers between devices, from_x(): return lax.ppermute(value, 'x', [((x + step) % 4, x) for x in range(4)])  9.37 us
    unnamed x19, local copies, waits for them, and re-layouts  8.89 us
    ppermute x3, waiting for transfers between devices, from_x(): return lax.ppermute(value, 'x', [((x + step) % 4, x) for x in range(4)])  8.38 us
    all_to_all x1, starting transfers between devices, shards(): lax.all_to_all(doc_term.reshape(64, 8, rank), ('zl', 'zh', 'x'), 0, 0, ti...  8.37 us
  transfers between devices with their start and end apart: 11, of which 8 were waited for; matrix products, arithmetic and copies ran while one was open for 8% of the time, Pallas kernels for 2%

profile of v4, /device:TPU:1, one launch (start us, length us, event | category | flops | bytes accessed | tf_op | source)
XLA Modules:
  0.0 179.5 jit_solution(7052361175133420146)
XLA Ops:
  9.3 13.1 %all-to-all-start = ((bf16[8,64,128]{2,1,0:T(8,128)(2,1)}), bf16[8,64,128]{2,1,0:T(8,128)(2,1)S(1)}, u32[]{:S(2)}, u32[]{:S(2)}) async-start(bf16[8,64,128]{2,1,0:T(8,128)(2,1)} %broadcast_in_dim.14), calls=%async_computation | async-start | bytes 262144 | tf_op jit(solution)/shard_map/all_to_all | solution.py:19
  24.1 8.6 %all-to-all-done = bf16[8,64,128]{2,1,0:T(8,128)(2,1)S(1)} async-done(((bf16[8,64,128]{2,1,0:T(8,128)(2,1)}), bf16[8,64,128]{2,1,0:T(8,128)(2,1)S(1)}, u32[]{:S(2)}, u32[]{:S(2)}) %all-to-all-start) | async-done | bytes 131104 | tf_op jit(solution)/shard_map/all_to_all | solution.py:19
  33.7 4.2 %all-to-all-start.1 = ((bf16[4,592,128]{2,1,0:T(8,128)(2,1)}), bf16[4,592,128]{2,1,0:T(8,128)(2,1)S(1)}, u32[]{:S(2)}, u32[]{:S(2)}) async-start(bf16[4,592,128]{2,1,0:T(8,128)(2,1)} %broadcast_in_dim.16), calls=%async_computation.1 | async-start | bytes 1212416 | tf_op jit(solution)/shard_map/all_to_all | solution.py:19
  38.3 12.5 %all-to-all-done.1.own_ref = bf16[4,592,128]{2,1,0:T(8,128)(2,1)S(1)} async-done(((bf16[4,592,128]{2,1,0:T(8,128)(2,1)}), bf16[4,592,128]{2,1,0:T(8,128)(2,1)S(1)}, u32[]{:S(2)}, u32[]{:S(2)}) %all-to-all-start.1) | async-done | bytes 606240 | tf_op jit(solution)/shard_map/all_to_all | solution.py:19
  50.8 4.8 %collective-permute-start = (bf16[4,592,128]{2,1,0:T(8,128)(2,1)S(1)}, bf16[4,592,128]{2,1,0:T(8,128)(2,1)S(1)}, u32[]{:S(2)}, u32[]{:S(2)}) collective-permute-start(bf16[4,592,128]{2,1,0:T(8,128)(2,1)S(1)} %all-to-all-done.1.own_ref), channel_id=1, source_target_pairs={{0,8},{8,0},{1,9},{9,1},{2,10},{10,2},{3,11},{11,3},{4,12},{12,4},... | collective-permute-start | bytes 1818632 | tf_op jit(solution)/shard_map/ppermute | solution.py:23
  55.6 1.9 %fusion.2.normed_ref = bf16[128,8192]{1,0:T(8,128)(2,1)} fusion(bf16[128,8192]{1,0:T(8,128)(2,1)S(1)} %copy-done.1, f32[8192]{0:T(1024)S(1)} %copy-done.6, f32[128]{0:T(128)S(1)} %get-tuple-element.22), kind=kLoop, calls=%fused_computation.4 | loop fusion | flops 4194304 | bytes 4227584 | tf_op jit(solution)/shard_map/convert_element_type | solution.py:162
  57.5 1.6 copy-done.2
  60.6 3.3 %all-to-all-start.2 = ((f32[8,8,128]{2,1,0:T(8,128)}), f32[8,8,128]{2,1,0:T(8,128)S(1)}, u32[]{:S(2)}, u32[]{:S(2)}) async-start(f32[8,8,128]{2,1,0:T(8,128)} %bitcast.14), calls=%async_computation.2 | async-start | bytes 65536 | tf_op jit(solution)/shard_map/all_to_all | solution.py:169
  64.0 8.3 %collective-permute-start.1 = (bf16[16,4096]{1,0:T(8,128)(2,1)}, bf16[16,4096]{1,0:T(8,128)(2,1)S(1)}, u32[]{:S(2)}, u32[]{:S(2)}) collective-permute-start(bf16[16,4096]{1,0:T(8,128)(2,1)} %param.15), channel_id=1, source_target_pairs={{0,4},{4,0},{1,5},{5,1},{2,6},{6,2},{3,7},{7,3},{8,12},{12,8},{9,1... | collective-permute-start | bytes 393224 | tf_op jit(solution)/shard_map/ppermute | solution.py:23
  74.8 8.4 %all-to-all-start.3 = ((f32[64,1,512]{2,1,0:T(1,128)}), f32[64,1,512]{2,1,0:T(1,128)S(1)}, u32[]{:S(2)}, u32[]{:S(2)}) async-start(f32[64,1,512]{2,1,0:T(1,128)} %reshape.103), calls=%async_computation.3 | async-start | bytes 262144 | tf_op jit(solution)/shard_map/all_to_all | solution.py:186
  83.2 7.3 %collective-permute-done.1 = bf16[16,4096]{1,0:T(8,128)(2,1)S(1)} collective-permute-done((bf16[16,4096]{1,0:T(8,128)(2,1)}, bf16[16,4096]{1,0:T(8,128)(2,1)S(1)}, u32[]{:S(2)}, u32[]{:S(2)}) %collective-permute-start.1) | collective-permute-done | bytes 131104 | tf_op jit(solution)/shard_map/ppermute | solution.py:23
  91.4 4.6 %collective-permute-start.2 = (bf16[32,4096]{1,0:T(8,128)(2,1)S(1)}, bf16[32,4096]{1,0:T(8,128)(2,1)S(1)}, u32[]{:S(2)}, u32[]{:S(2)}) collective-permute-start(bf16[32,4096]{1,0:T(8,128)(2,1)S(1)} %pad_maximum_fusion.here_ref), channel_id=1, source_target_pairs={{1,0},{2,1},{3,2},{0,3},{5,4},{6,5},{7,6},{4,7},{9,8},{10,9},{11,1... | collective-permute-start | bytes 786440 | tf_op jit(solution)/shard_map/ppermute | solution.py:132
  96.1 2.7 %collective-permute-start.3 = (bf16[32,4096]{1,0:T(8,128)(2,1)S(1)}, bf16[32,4096]{1,0:T(8,128)(2,1)S(1)}, u32[]{:S(2)}, u32[]{:S(2)}) collective-permute-start(bf16[32,4096]{1,0:T(8,128)(2,1)S(1)} %pad_maximum_fusion.here_ref), channel_id=1, source_target_pairs={{2,0},{3,1},{0,2},{1,3},{6,4},{7,5},{4,6},{5,7},{10,8},{11,9},{8,1... | collective-permute-start | bytes 786440 | tf_op jit(solution)/shard_map/ppermute | solution.py:132
  98.7 2.1 %collective-permute-start.4 = (bf16[32,4096]{1,0:T(8,128)(2,1)S(1)}, bf16[32,4096]{1,0:T(8,128)(2,1)S(1)}, u32[]{:S(2)}, u32[]{:S(2)}) collective-permute-start(bf16[32,4096]{1,0:T(8,128)(2,1)S(1)} %pad_maximum_fusion.here_ref), channel_id=1, source_target_pairs={{3,0},{0,1},{1,2},{2,3},{7,4},{4,5},{5,6},{6,7},{11,8},{8,9},{9,10... | collective-permute-start | bytes 786440 | tf_op jit(solution)/shard_map/ppermute | solution.py:132
  102.3 1.9 %reduce = f32[64,512]{1,0:T(8,128)S(1)} reduce(f32[64,1,512]{2,1,0:T(1,128)} %copy-done.8, f32[]{:T(128)} %broadcast.48), dimensions={1}, to_apply=%all_to_all.18.reduce_sub_computation | reduce | bytes 262148 | tf_op jit(solution)/shard_map/all_to_all | solution.py:186
  104.9 1.7 collective-permute-done.3.two_ref
  106.7 6.6 %collective-permute-done.4.three_ref = bf16[32,4096]{1,0:T(8,128)(2,1)S(1)} collective-permute-done((bf16[32,4096]{1,0:T(8,128)(2,1)S(1)}, bf16[32,4096]{1,0:T(8,128)(2,1)S(1)}, u32[]{:S(2)}, u32[]{:S(2)}) %collective-permute-start.4) | collective-permute-done | bytes 262176 | tf_op jit(solution)/shard_map/ppermute | solution.py:132
  115.1 10.7 %all-to-all-start.4 = ((bf16[64,8,128]{2,1,0:T(8,128)(2,1)}), bf16[64,8,128]{2,1,0:T(8,128)(2,1)S(1)}, u32[]{:S(2)}, u32[]{:S(2)}) async-start(bf16[64,8,128]{2,1,0:T(8,128)(2,1)} %broadcast_in_dim.17), calls=%async_computation.4 | async-start | bytes 262144 | tf_op jit(solution)/shard_map/all_to_all | solution.py:19
  126.1 15.3 %all-to-all-done.4.docs_ref = bf16[64,8,128]{2,1,0:T(8,128)(2,1)S(1)} async-done(((bf16[64,8,128]{2,1,0:T(8,128)(2,1)}), bf16[64,8,128]{2,1,0:T(8,128)(2,1)S(1)}, u32[]{:S(2)}, u32[]{:S(2)}) %all-to-all-start.4) | async-done | bytes 131104 | tf_op jit(solution)/shard_map/all_to_all | solution.py:19
  141.4 1.6 scores.1
  143.0 16.0 %all-gather.2.cloned.1.call-done.weight_ref = bf16[8192,512]{1,0:T(8,128)(2,1)} async-done(((bf16[128,512]{1,0:T(8,128)(2,1)}), bf16[8192,512]{1,0:T(8,128)(2,1)}) %all-gather.2.cloned.1.call-update) | async-done | bytes 8388624 | tf_op jit(solution)/shard_map/all_gather | solution.py:158
  159.0 1.6 copy-done.3
  160.6 3.4 %copy-done.4 = bf16[8192,512]{1,0:T(8,128)(2,1)S(1)} copy-done((bf16[8192,512]{1,0:T(8,128)(2,1)S(1)}, bf16[8192,512]{1,0:T(8,128)(2,1)}, u32[]{:S(2)}) %copy-start.4) | copy-done | bytes 8388632
  164.8 7.8 %layer.1 = (bf16[128,512]{1,0:T(8,128)(2,1)}, bf16[128,8192]{1,0:T(8,128)(2,1)}) custom-call(bf16[128,8192]{1,0:T(8,128)(2,1)S(1)} %copy-done.3, bf16[128,8192]{1,0:T(8,128)(2,1)S(1)} %copy-done.1, f32[1,8192]{1,0:T(1,128)S(1)} %bitcast.36, f32[128,1]{1,0:T(8,128)S(1)} %copy.16.scale_ref, bf16[128,512]{1,0:T(8,128)(2,1)S(1)} %copy-done.5, ...), custom_call_target="tpu_custom_call" | custom-call | tf_op jit(solution)/shard_map/layer/pallas_call | solution.py:198
  (48 shorter events, 15.1 us)
Async XLA Ops:
  7.2 15.9 %copy-start = (bf16[512,64]{0,1:T(8,128)(2,1)S(1)}, bf16[512,64]{0,1:T(8,128)(2,1)}, u32[]{:S(2)}) copy-start(bf16[512,64]{0,1:T(8,128)(2,1)} %param.13) | copy-start | bytes 196612
  7.2 30.7 %copy-start.1 = (bf16[128,8192]{1,0:T(8,128)(2,1)S(1)}, bf16[128,8192]{1,0:T(8,128)(2,1)}, u32[]{:S(2)}) copy-start(bf16[128,8192]{1,0:T(8,128)(2,1)} %hidden_ref.1) | copy-start | bytes 6291460
  7.2 151.8 %all-gather.2.cloned.1.call-start = ((), (), s32[]{:S(2)}) async-start(), calls=%async_computation.5 | async-start | bytes 8519680 | tf_op jit(solution)/shard_map/all_gather | solution.py:158
  9.3 23.4 %all-to-all-start = ((bf16[8,64,128]{2,1,0:T(8,128)(2,1)}), bf16[8,64,128]{2,1,0:T(8,128)(2,1)S(1)}, u32[]{:S(2)}, u32[]{:S(2)}) async-start(bf16[8,64,128]{2,1,0:T(8,128)(2,1)} %broadcast_in_dim.14), calls=%async_computation | async-start | bytes 262144 | tf_op jit(solution)/shard_map/all_to_all | solution.py:19
  32.7 22.9 %copy-start.6 = (f32[8192]{0:T(1024)S(1)}, f32[8192]{0:T(1024)}, u32[]{:S(2)}) copy-start(f32[8192]{0:T(1024)} %param.9) | copy-start | bytes 98308
  33.7 17.2 %all-to-all-start.1 = ((bf16[4,592,128]{2,1,0:T(8,128)(2,1)}), bf16[4,592,128]{2,1,0:T(8,128)(2,1)S(1)}, u32[]{:S(2)}, u32[]{:S(2)}) async-start(bf16[4,592,128]{2,1,0:T(8,128)(2,1)} %broadcast_in_dim.16), calls=%async_computation.1 | async-start | bytes 1212416 | tf_op jit(solution)/shard_map/all_to_all | solution.py:19
  50.8 6.7 %collective-permute-start = (bf16[4,592,128]{2,1,0:T(8,128)(2,1)S(1)}, bf16[4,592,128]{2,1,0:T(8,128)(2,1)S(1)}, u32[]{:S(2)}, u32[]{:S(2)}) collective-permute-start(bf16[4,592,128]{2,1,0:T(8,128)(2,1)S(1)} %all-to-all-done.1.own_ref), channel_id=1, source_target_pairs={{0,8},{8,0},{1,9},{9,1},{2,10},{10,2},{3,11},{11,3},{4,12},{12,4},... | collective-permute-start | bytes 1818632 | tf_op jit(solution)/shard_map/ppermute | solution.py:23
  57.5 1.6 copy-start.2
  60.6 11.7 %all-to-all-start.2 = ((f32[8,8,128]{2,1,0:T(8,128)}), f32[8,8,128]{2,1,0:T(8,128)S(1)}, u32[]{:S(2)}, u32[]{:S(2)}) async-start(f32[8,8,128]{2,1,0:T(8,128)} %bitcast.14), calls=%async_computation.2 | async-start | bytes 65536 | tf_op jit(solution)/shard_map/all_to_all | solution.py:169
  64.0 26.5 %collective-permute-start.1 = (bf16[16,4096]{1,0:T(8,128)(2,1)}, bf16[16,4096]{1,0:T(8,128)(2,1)S(1)}, u32[]{:S(2)}, u32[]{:S(2)}) collective-permute-start(bf16[16,4096]{1,0:T(8,128)(2,1)} %param.15), channel_id=1, source_target_pairs={{0,4},{4,0},{1,5},{5,1},{2,6},{6,2},{3,7},{7,3},{8,12},{12,8},{9,1... | collective-permute-start | bytes 393224 | tf_op jit(solution)/shard_map/ppermute | solution.py:23
  73.8 85.2 %copy-start.5 = (bf16[128,512]{1,0:T(8,128)(2,1)S(1)}, bf16[128,512]{1,0:T(8,128)(2,1)}, u32[]{:S(2)}) copy-start(bf16[128,512]{1,0:T(8,128)(2,1)} %grad_ref.1) | copy-start | bytes 393220
  74.8 26.3 %all-to-all-start.3 = ((f32[64,1,512]{2,1,0:T(1,128)}), f32[64,1,512]{2,1,0:T(1,128)S(1)}, u32[]{:S(2)}, u32[]{:S(2)}) async-start(f32[64,1,512]{2,1,0:T(1,128)} %reshape.103), calls=%async_computation.3 | async-start | bytes 262144 | tf_op jit(solution)/shard_map/all_to_all | solution.py:186
  91.4 13.5 %collective-permute-start.2 = (bf16[32,4096]{1,0:T(8,128)(2,1)S(1)}, bf16[32,4096]{1,0:T(8,128)(2,1)S(1)}, u32[]{:S(2)}, u32[]{:S(2)}) collective-permute-start(bf16[32,4096]{1,0:T(8,128)(2,1)S(1)} %pad_maximum_fusion.here_ref), channel_id=1, source_target_pairs={{1,0},{2,1},{3,2},{0,3},{5,4},{6,5},{7,6},{4,7},{9,8},{10,9},{11,1... | collective-permute-start | bytes 786440 | tf_op jit(solution)/shard_map/ppermute | solution.py:132
  96.1 10.6 %collective-permute-start.3 = (bf16[32,4096]{1,0:T(8,128)(2,1)S(1)}, bf16[32,4096]{1,0:T(8,128)(2,1)S(1)}, u32[]{:S(2)}, u32[]{:S(2)}) collective-permute-start(bf16[32,4096]{1,0:T(8,128)(2,1)S(1)} %pad_maximum_fusion.here_ref), channel_id=1, source_target_pairs={{2,0},{3,1},{0,2},{1,3},{6,4},{7,5},{4,6},{5,7},{10,8},{11,9},{8,1... | collective-permute-start | bytes 786440 | tf_op jit(solution)/shard_map/ppermute | solution.py:132
  98.7 14.6 %collective-permute-start.4 = (bf16[32,4096]{1,0:T(8,128)(2,1)S(1)}, bf16[32,4096]{1,0:T(8,128)(2,1)S(1)}, u32[]{:S(2)}, u32[]{:S(2)}) collective-permute-start(bf16[32,4096]{1,0:T(8,128)(2,1)S(1)} %pad_maximum_fusion.here_ref), channel_id=1, source_target_pairs={{3,0},{0,1},{1,2},{2,3},{7,4},{4,5},{5,6},{6,7},{11,8},{8,9},{9,10... | collective-permute-start | bytes 786440 | tf_op jit(solution)/shard_map/ppermute | solution.py:132
  101.1 0.7 copy-start.8
  115.1 26.3 %all-to-all-start.4 = ((bf16[64,8,128]{2,1,0:T(8,128)(2,1)}), bf16[64,8,128]{2,1,0:T(8,128)(2,1)S(1)}, u32[]{:S(2)}, u32[]{:S(2)}) async-start(bf16[64,8,128]{2,1,0:T(8,128)(2,1)} %broadcast_in_dim.17), calls=%async_computation.4 | async-start | bytes 262144 | tf_op jit(solution)/shard_map/all_to_all | solution.py:19
  159.0 1.6 copy-start.3
  160.6 3.4 %copy-start.4 = (bf16[8192,512]{1,0:T(8,128)(2,1)S(1)}, bf16[8192,512]{1,0:T(8,128)(2,1)}, u32[]{:S(2)}) copy-start(bf16[8192,512]{1,0:T(8,128)(2,1)} %all-gather.2.cloned.1.call-done.weight_ref) | copy-start | bytes 25165828
  164.0 0.8 copy-start.7
Sparse Core Ops, SparseCore 0:
  10.2 148.7 all-gather.1

commit v5 on v4

--- a/solution.py
+++ b/solution.py
@@ -9,8 +9,9 @@
 EPSILON = 1e-05
 DP = ("y", "zl", "core")
 SCORE = ("zh", "x")
+Z_STEPS = (-1, 0, 1, 2, 3, 4, -3, -2)
 BLOCK = 128
-LIMIT = 32 * 1024 * 1024
+LIMIT = 16 * 1024 * 1024
 
 
 def spread_to_all(value, axes):
@@ -21,6 +22,15 @@
 
 def swapped(value, axis):
     return lax.ppermute(value, axis, [(0, 1), (1, 0)])
+
+
+def from_z(value, step):
+    def place(z):
+        return (z % 8) * 2 + z // 8
+
+    return lax.ppermute(
+        value, ("zl", "zh"), [(place((z + step) % 16), place(z)) for z in range(16)]
+    )
 
 
 def contract_last(left_side, right_side):
@@ -50,31 +60,51 @@
     left_ref[...] = total
 
 
+def joined_kernel(*refs):
+    out_ref = refs[-1]
+    start = 0
+    for ref in refs[:-1]:
+        out_ref[start : start + ref.shape[0]] = ref[...]
+        start += ref.shape[0]
+
+
+def along_z_kernel(near_ref, ahead_ref, behind_ref, out_ref):
+    three = 3 * BLOCK
+    out_ref[:three] = near_ref[...]
+    out_ref[three : 2 * three] = ahead_ref[...]
+    out_ref[2 * three :] = behind_ref[BLOCK:]
+
+
 def layer_kernel(
-    normed_ref, hidden_ref, gain_ref, scale_ref, grad_ref, weight_ref,
-    values_ref, hidden_grad_ref, held, base, wide_in, arrived,
+    place_ref, normed_hbm, hidden_hbm, gain_ref, scale_ref, grad_ref, weight_hbm,
+    values_ref, hidden_grad_ref, held, base, normed_ref, hidden_ref, arrived,
 ):
-    chunks = held.shape[0]
-    depth = held.shape[1]
+    chunks, depth = held.shape[:2]
     width = normed_ref.shape[1]
     copies = [
         pltpu.make_async_copy(
-            weight_ref.at[pl.ds(chunk * depth, depth)], held.at[chunk], arrived.at[chunk]
+            weight_hbm.at[pl.ds(chunk * depth, depth)], held.at[chunk], arrived.at[chunk]
         )
         for chunk in range(chunks)
     ]
+    normed_copy = pltpu.make_async_copy(normed_hbm, normed_ref, arrived.at[chunks])
+    hidden_copy = pltpu.make_async_copy(hidden_hbm, hidden_ref, arrived.at[chunks + 1])
+    normed_copy.start()
     for copy in copies:
         copy.start()
-    hidden_copy = pltpu.make_async_copy(hidden_ref, wide_in, arrived.at[chunks])
     hidden_copy.start()
     grad = grad_ref[...]
     inv_rms = scale_ref[...]
     total = jnp.zeros(values_ref.shape, jnp.float32)
-    for chunk, copy in enumerate(copies):
-        copy.wait()
-        for start in range(0, depth, 256):
-            where = slice(chunk * depth + start, chunk * depth + start + 256)
-            weight = held[chunk, start : start + 256]
+    normed_copy.wait()
+    for y in range(chunks // 2):
+        copies[2 * y].wait()
+        copies[2 * y + 1].wait()
+        for step in range(depth // BLOCK):
+            rows = slice(step * BLOCK, (step + 1) * BLOCK)
+            weight = jnp.concatenate([held[2 * y, rows], held[2 * y + 1, rows]], 0)
+            offset = pl.multiple_of(y * (width // 4) + place_ref[step] * 256, 256)
+            where = pl.ds(offset, 256)
             total += jnp.dot(normed_ref[:, where], weight, preferred_element_type=jnp.float32)
             base[:, where] = inv_rms * (contract_last(grad, weight) * gain_ref[:, where])
     values_ref[...] = total.astype(jnp.bfloat16)
@@ -83,7 +113,7 @@
     hidden_copy.wait()
     for start in range(0, width, 512):
         where = slice(start, start + 512)
-        wide = wide_in[:, where].astype(jnp.float32)
+        wide = hidden_ref[:, where].astype(jnp.float32)
         hidden_grad_ref[:, where] = (base[:, where] - wide * pull).astype(jnp.bfloat16)
 
 
@@ -155,7 +185,12 @@
     packed = spread_to_all(jnp.concatenate([factor_z, right_t, ids_rows], 0), "y")
     packed_other = swapped(packed, "core")
 
-    w_all = lax.all_gather(value_weight, DP, axis=0, tiled=True)
+    ahead, behind = from_z(value_weight, 1), from_z(value_weight, -1)
+    near = call(joined_kernel, struct((3 * BLOCK, kv), jnp.bfloat16), 0, "near_three")(
+        behind, value_weight, ahead
+    )
+    near = after(near, factor_z)
+    far_ahead, far_behind = from_z(near, 3), from_z(near, -3)
 
     wide_in = hidden_in.astype(jnp.float32)
     inv_rms = lax.rsqrt(jnp.mean(wide_in * wide_in, axis=1, keepdims=True) + EPSILON)
@@ -163,6 +198,12 @@
     left_t = call(left_kernel, struct((rank, rows), jnp.float32), 1, "left_factor")(
         core_row, normed, packed, packed_other
     )
+
+    w_z = call(along_z_kernel, struct((8 * BLOCK, kv), jnp.bfloat16), 0, "along_z")(
+        near, *after((far_ahead, far_behind), left_t)
+    )
+    w_all = lax.all_gather(w_z, ("y", "core"), axis=0, tiled=True)
+    z_place = (lax.axis_index("zl") + jnp.array(Z_STEPS, jnp.int32)) % 8
 
     q_other = swapped(after(queries, left_t), "zh")
 
@@ -188,7 +229,6 @@
     )
     q_here = after(jnp.concatenate([queries, q_other], 0), doc_term)
     q_turns = [from_x(q_here, step) for step in (1, 2, 3)]
-    doc_parts, q_turns = lax.optimization_barrier((doc_parts, q_turns))
     own_docs = jnp.sum(doc_parts, 0).astype(jnp.bfloat16)
     doc_low = spread_to_all(jnp.concatenate([own_docs, own_docs], 1), DP)
 
@@ -198,17 +238,22 @@
     values_out, hidden_grad = pl.pallas_call(
         layer_kernel,
         out_shape=(struct((rows, kv), jnp.bfloat16), struct((rows, width), jnp.bfloat16)),
-        in_specs=[vmem, hbm, vmem, vmem, vmem, hbm],
+        in_specs=[pl.BlockSpec(memory_space=pltpu.SMEM), hbm, hbm, vmem, vmem, vmem, hbm],
         out_specs=(vmem, vmem),
         scratch_shapes=[
             pltpu.VMEM((chunks, width // chunks, kv), jnp.bfloat16),
             pltpu.VMEM((rows, width), jnp.float32),
             pltpu.VMEM((rows, width), jnp.bfloat16),
-            pltpu.SemaphoreType.DMA((chunks + 1,)),
+            pltpu.VMEM((rows, width), jnp.bfloat16),
+            pltpu.SemaphoreType.DMA((chunks + 2,)),
         ],
-        compiler_params=pltpu.CompilerParams(vmem_limit_bytes=LIMIT),
+        compiler_params=pltpu.CompilerParams(vmem_limit_bytes=58 * 1024 * 1024),
         name="layer",
-    )(normed, hidden_in, norm_gain.reshape(1, width), inv_rms, value_grad, w_all)
+    )(
+        z_place.astype(jnp.int32), normed, hidden_in, norm_gain.reshape(1, width), inv_rms,
+        value_grad, w_all,
+    )
+    doc_low, values_out = lax.optimization_barrier((doc_low, values_out))
     score_index = jnp.stack([lax.axis_index("zh"), lax.axis_index("x")]).astype(jnp.int32)
     scores = call(score_kernel, struct((8, 8 * queries.shape[0]), jnp.float32), 1, "scores")(
         score_index, doc_low, q_here, *q_turns

time: 180 us -> 162 us (0.900)
  waiting for transfers between devices: 69.1 us -> 24 us
  starting transfers between devices: 62.2 us -> 91.6 us
  local copies, waits for them, and re-layouts: 13.4 us -> 6.12 us
  Pallas kernels: 10.9 us -> 15.7 us
    all_to_all x3, waiting for transfers between devices: 36.4 us -> 0.13 us  [spread_to_all(): return lax.all_to_all(copies, axes, 0, 0, tiled=True)]
    ppermute x0 -> x4, starting transfers between devices: none -> 17.2 us  [from_z(): lax.ppermute(value, ('zl', 'zh'), [(place((z + step) % 16), place(z)) for...]
    all_gather x1, waiting for transfers between devices: 16 us -> 0.01 us  [shards(): w_all = lax.all_gather(w_z, ('y', 'core'), axis=0, tiled=True)]
    ppermute x0 -> x4, waiting for transfers between devices: none -> 15.2 us  [from_z(): lax.ppermute(value, ('zl', 'zh'), [(place((z + step) % 16), place(z)) for...]
    ppermute x3, waiting for transfers between devices: 8.38 us -> 0.9 us  [from_x(): return lax.ppermute(value, 'x', [((x + step) % 4, x) for x in range(4)])]
    ppermute x2, waiting for transfers between devices: 7.35 us -> 0.01 us  [swapped(): return lax.ppermute(value, axis, [(0, 1), (1, 0)])]
    unnamed x19 -> x18, local copies, waits for them, and re-layouts: 8.89 us -> 1.6 us
    all_to_all x1, starting transfers between devices: 3.29 us -> 8.33 us  [shards(): lax.all_to_all(left_t.reshape(8, rank // 8, rows), ('y', 'core'), 0, 0, t...]
  transfers between devices with their start and end apart: 11 -> 15, of which waited for: 8 -> 6; matrix products, arithmetic and copies ran while one was open for 8% -> 8% of each run, Pallas kernels for 2% -> 7%
where the time goes in v5:
time: 162 us; the launch traced here: 161 us
  starting transfers between devices  91.6 us (57%)
  waiting for transfers between devices  24 us (15%)
  Pallas kernels  15.7 us (10%)
  between operations  14.4 us (9%)
  other arithmetic  6.81 us (4%)
  local copies, waits for them, and re-layouts  6.12 us (4%)
  matrix products  2.25 us (1%)
    all_to_all x3, starting transfers between devices, spread_to_all(): return lax.all_to_all(copies, axes, 0, 0, tiled=True)  32.8 us
    ppermute x4, starting transfers between devices, from_z(): lax.ppermute(value, ('zl', 'zh'), [(place((z + step) % 16), place(z)) for...  17.2 us
    ppermute x2, starting transfers between devices, swapped(): return lax.ppermute(value, axis, [(0, 1), (1, 0)])  16.5 us
    ppermute x4, waiting for transfers between devices, from_z(): lax.ppermute(value, ('zl', 'zh'), [(place((z + step) % 16), place(z)) for...  15.2 us
    pallas_call x1, Pallas kernels, shards(): pl.pallas_call(layer_kernel, out_shape=(struct((rows, kv), jnp.bfloat16),...  9.66 us
    all_to_all x1, starting transfers between devices, shards(): lax.all_to_all(doc_term.reshape(64, 8, rank), ('zl', 'zh', 'x'), 0, 0, ti...  9.5 us
    all_to_all x1, starting transfers between devices, shards(): lax.all_to_all(left_t.reshape(8, rank // 8, rows), ('y', 'core'), 0, 0, t...  8.33 us
    ppermute x3, starting transfers between devices, from_x(): return lax.ppermute(value, 'x', [((x + step) % 4, x) for x in range(4)])  7.2 us
  transfers between devices with their start and end apart: 15, of which 6 were waited for; matrix products, arithmetic and copies ran while one was open for 8% of the time, Pallas kernels for 7%

profile of v5, /device:TPU:1, one launch (start us, length us, event | category | flops | bytes accessed | tf_op | source)
XLA Modules:
  0.0 160.8 jit_solution(3136777530076309147)
XLA Ops:
  8.7 13.1 %all-to-all-start = ((bf16[8,64,128]{2,1,0:T(8,128)(2,1)}), bf16[8,64,128]{2,1,0:T(8,128)(2,1)S(1)}, u32[]{:S(2)}, u32[]{:S(2)}) async-start(bf16[8,64,128]{2,1,0:T(8,128)(2,1)} %broadcast_in_dim.13), calls=%async_computation | async-start | bytes 262144 | tf_op jit(solution)/shard_map/all_to_all | solution.py:20
  21.8 3.4 %collective-permute-start.1 = (bf16[128,512]{1,0:T(8,128)(2,1)}, bf16[128,512]{1,0:T(8,128)(2,1)S(1)}, u32[]{:S(2)}, u32[]{:S(2)}) collective-permute-start(bf16[128,512]{1,0:T(8,128)(2,1)} %refs_1_.1), channel_id=1, source_target_pairs={{116,0},{0,16},{16,32},{32,48},{48,64},{64,80},{80,96},{96,112},{1... | collective-permute-start | bytes 393224 | tf_op jit(solution)/shard_map/ppermute | solution.py:31
  25.2 6.8 %collective-permute-start.2 = (bf16[128,512]{1,0:T(8,128)(2,1)}, bf16[128,512]{1,0:T(8,128)(2,1)S(1)}, u32[]{:S(2)}, u32[]{:S(2)}) collective-permute-start(bf16[128,512]{1,0:T(8,128)(2,1)} %refs_1_.1), channel_id=1, source_target_pairs={{16,0},{32,16},{48,32},{64,48},{80,64},{96,80},{112,96},{4,112},{2... | collective-permute-start | bytes 393224 | tf_op jit(solution)/shard_map/ppermute | solution.py:31
  34.7 4.2 %all-to-all-start.1 = ((bf16[4,592,128]{2,1,0:T(8,128)(2,1)}), bf16[4,592,128]{2,1,0:T(8,128)(2,1)S(1)}, u32[]{:S(2)}, u32[]{:S(2)}) async-start(bf16[4,592,128]{2,1,0:T(8,128)(2,1)} %broadcast_in_dim.15), calls=%async_computation.1 | async-start | bytes 1212416 | tf_op jit(solution)/shard_map/all_to_all | solution.py:20
  39.9 3.4 %collective-permute-start.3 = (bf16[384,512]{1,0:T(8,128)(2,1)S(1)}, bf16[384,512]{1,0:T(8,128)(2,1)S(1)}, u32[]{:S(2)}, u32[]{:S(2)}) collective-permute-start(bf16[384,512]{1,0:T(8,128)(2,1)S(1)} %near_three.1.near_ref), channel_id=1, source_target_pairs={{48,0},{64,16},{80,32},{96,48},{112,64},{4,80},{20,96},{36,112},{5... | collective-permute-start | bytes 1179656 | tf_op jit(solution)/shard_map/ppermute | solution.py:31
  43.3 3.7 %collective-permute-start.4 = (bf16[384,512]{1,0:T(8,128)(2,1)S(1)}, bf16[384,512]{1,0:T(8,128)(2,1)}, u32[]{:S(2)}, u32[]{:S(2)}) collective-permute-start(bf16[384,512]{1,0:T(8,128)(2,1)S(1)} %near_three.1.near_ref), channel_id=1, source_target_pairs={{84,0},{100,16},{116,32},{0,48},{16,64},{32,80},{48,96},{64,112},{... | collective-permute-start | bytes 1179656 | tf_op jit(solution)/shard_map/ppermute | solution.py:31
  47.1 4.9 %collective-permute-start = (bf16[4,592,128]{2,1,0:T(8,128)(2,1)S(1)}, bf16[4,592,128]{2,1,0:T(8,128)(2,1)}, u32[]{:S(2)}, u32[]{:S(2)}) collective-permute-start(bf16[4,592,128]{2,1,0:T(8,128)(2,1)S(1)} %all-to-all-done.1.own_ref), channel_id=1, source_target_pairs={{0,8},{8,0},{1,9},{9,1},{2,10},{10,2},{3,11},{11,3},{4,12},{12,4},... | collective-permute-start | bytes 1818632 | tf_op jit(solution)/shard_map/ppermute | solution.py:24
  52.1 2.2 %fusion.2.normed_ref.normed_hbm = bf16[128,8192]{1,0:T(8,128)(2,1)S(1)} fusion(bf16[128,8192]{1,0:T(8,128)(2,1)} %hidden_hbm.1, f32[8192]{0:T(1024)} %param.10, f32[128]{0:T(128)} %get-tuple-element.24), kind=kLoop, calls=%fused_computation.4 | loop fusion | flops 4194304 | bytes 4227584 | tf_op jit(solution)/shard_map/convert_element_type | solution.py:197
  54.3 2.4 %left_factor.1 = f32[64,128]{1,0:T(8,128)S(1)} custom-call(s32[1]{0:T(128)} %bitcast.9.core_ref, bf16[128,8192]{1,0:T(8,128)(2,1)S(1)} %fusion.2.normed_ref.normed_hbm, bf16[4,592,128]{2,1,0:T(8,128)(2,1)S(1)} %all-to-all-done.1.own_ref, bf16[4,592,128]{2,1,0:T(8,128)(2,1)} %collective-permute-done.other_ref), custom_call_target="tpu_custom_call" | custom-call | tf_op jit(solution)/shard_map/left_factor/pallas_call | solution.py:149
  57.3 12.0 %collective-permute-done.3.ahead_ref = bf16[384,512]{1,0:T(8,128)(2,1)S(1)} collective-permute-done((bf16[384,512]{1,0:T(8,128)(2,1)S(1)}, bf16[384,512]{1,0:T(8,128)(2,1)S(1)}, u32[]{:S(2)}, u32[]{:S(2)}) %collective-permute-start.3) | collective-permute-done | bytes 393248 | tf_op jit(solution)/shard_map/ppermute | solution.py:31
  69.3 3.1 %collective-permute-done.4.behind_ref = bf16[384,512]{1,0:T(8,128)(2,1)} collective-permute-done((bf16[384,512]{1,0:T(8,128)(2,1)S(1)}, bf16[384,512]{1,0:T(8,128)(2,1)}, u32[]{:S(2)}, u32[]{:S(2)}) %collective-permute-start.4) | collective-permute-done | bytes 393248 | tf_op jit(solution)/shard_map/ppermute | solution.py:31
  72.4 2.0 %along_z.1 = bf16[1024,512]{1,0:T(8,128)(2,1)} custom-call(bf16[384,512]{1,0:T(8,128)(2,1)S(1)} %near_three.1.near_ref, bf16[384,512]{1,0:T(8,128)(2,1)S(1)} %collective-permute-done.3.ahead_ref, bf16[384,512]{1,0:T(8,128)(2,1)} %collective-permute-done.4.behind_ref), custom_call_target="tpu_custom_call" | custom-call | tf_op jit(solution)/shard_map/along_z/pallas_call | solution.py:149
  75.4 8.3 %all-to-all-start.2 = ((f32[8,8,128]{2,1,0:T(8,128)}), f32[8,8,128]{2,1,0:T(8,128)S(1)}, u32[]{:S(2)}, u32[]{:S(2)}) async-start(f32[8,8,128]{2,1,0:T(8,128)} %bitcast.36), calls=%async_computation.2 | async-start | bytes 65536 | tf_op jit(solution)/shard_map/all_to_all | solution.py:210
  83.8 4.7 %all-to-all-done.2 = f32[8,8,128]{2,1,0:T(8,128)S(1)} async-done(((f32[8,8,128]{2,1,0:T(8,128)}), f32[8,8,128]{2,1,0:T(8,128)S(1)}, u32[]{:S(2)}, u32[]{:S(2)}) %all-to-all-start.2) | async-done | bytes 32800 | tf_op jit(solution)/shard_map/all_to_all | solution.py:210
  88.8 1.2 fusion.4
  90.9 9.5 %all-to-all-start.3 = ((f32[64,1,512]{2,1,0:T(1,128)}), f32[64,1,512]{2,1,0:T(1,128)S(1)}, u32[]{:S(2)}, u32[]{:S(2)}) async-start(f32[64,1,512]{2,1,0:T(1,128)} %reshape.103), calls=%async_computation.3 | async-start | bytes 262144 | tf_op jit(solution)/shard_map/all_to_all | solution.py:227
  100.4 11.6 %collective-permute-start.5 = (bf16[16,4096]{1,0:T(8,128)(2,1)S(1)}, bf16[16,4096]{1,0:T(8,128)(2,1)S(1)}, u32[]{:S(2)}, u32[]{:S(2)}) collective-permute-start(bf16[16,4096]{1,0:T(8,128)(2,1)S(1)} %copy-done.5), channel_id=1, source_target_pairs={{0,4},{4,0},{1,5},{5,1},{2,6},{6,2},{3,7},{7,3},{8,12},{12,8},{9,1... | collective-permute-start | bytes 393224 | tf_op jit(solution)/shard_map/ppermute | solution.py:24
  112.1 3.1 %all-to-all-done.3 = f32[64,1,512]{2,1,0:T(1,128)S(1)} async-done(((f32[64,1,512]{2,1,0:T(1,128)}), f32[64,1,512]{2,1,0:T(1,128)S(1)}, u32[]{:S(2)}, u32[]{:S(2)}) %all-to-all-start.3) | async-done | bytes 131104 | tf_op jit(solution)/shard_map/all_to_all | solution.py:227
  117.6 15.5 %all-to-all-start.4 = ((bf16[64,8,128]{2,1,0:T(8,128)(2,1)}), bf16[64,8,128]{2,1,0:T(8,128)(2,1)S(1)}, u32[]{:S(2)}, u32[]{:S(2)}) async-start(bf16[64,8,128]{2,1,0:T(8,128)(2,1)} %broadcast_in_dim.16), calls=%async_computation.4 | async-start | bytes 262144 | tf_op jit(solution)/shard_map/all_to_all | solution.py:20
  133.2 1.9 %collective-permute-start.6 = (bf16[32,4096]{1,0:T(8,128)(2,1)S(1)}, bf16[32,4096]{1,0:T(8,128)(2,1)S(1)}, u32[]{:S(2)}, u32[]{:S(2)}) collective-permute-start(bf16[32,4096]{1,0:T(8,128)(2,1)S(1)} %pad_maximum_fusion.here_ref), channel_id=1, source_target_pairs={{1,0},{2,1},{3,2},{0,3},{5,4},{6,5},{7,6},{4,7},{9,8},{10,9},{11,1... | collective-permute-start | bytes 786440 | tf_op jit(solution)/shard_map/ppermute | solution.py:162
  135.1 2.5 %collective-permute-start.7 = (bf16[32,4096]{1,0:T(8,128)(2,1)S(1)}, bf16[32,4096]{1,0:T(8,128)(2,1)S(1)}, u32[]{:S(2)}, u32[]{:S(2)}) collective-permute-start(bf16[32,4096]{1,0:T(8,128)(2,1)S(1)} %pad_maximum_fusion.here_ref), channel_id=1, source_target_pairs={{2,0},{3,1},{0,2},{1,3},{6,4},{7,5},{4,6},{5,7},{10,8},{11,9},{8,1... | collective-permute-start | bytes 786440 | tf_op jit(solution)/shard_map/ppermute | solution.py:162
  137.6 2.8 %collective-permute-start.8 = (bf16[32,4096]{1,0:T(8,128)(2,1)S(1)}, bf16[32,4096]{1,0:T(8,128)(2,1)S(1)}, u32[]{:S(2)}, u32[]{:S(2)}) collective-permute-start(bf16[32,4096]{1,0:T(8,128)(2,1)S(1)} %pad_maximum_fusion.here_ref), channel_id=1, source_target_pairs={{3,0},{0,1},{1,2},{2,3},{7,4},{4,5},{5,6},{6,7},{11,8},{8,9},{9,10... | collective-permute-start | bytes 786440 | tf_op jit(solution)/shard_map/ppermute | solution.py:162
  141.7 9.7 %layer.1 = (bf16[128,512]{1,0:T(8,128)(2,1)}, bf16[128,8192]{1,0:T(8,128)(2,1)}) custom-call(s32[8]{0:T(128)} %and_select_fusion.place_ref, bf16[128,8192]{1,0:T(8,128)(2,1)} %copy-done.1, bf16[128,8192]{1,0:T(8,128)(2,1)} %hidden_hbm.1, f32[1,8192]{1,0:T(1,128)} %bitcast.42, f32[128,1]{1,0:T(8,128)} %copy.21.scale_ref, bf16[128,512]{1,0:T(8,128)(2,1)} %grad_ref.1, ...), custom_call_target="tpu_custom_call" | custom-call | tf_op jit(solution)/shard_map/layer/pallas_call | solution.py:238
  152.3 1.6 %scores.1 = f32[8,128]{1,0:T(8,128)} custom-call(s32[2]{0:T(128)S(1)} %pad_add_fusion.index_ref, bf16[64,8,128]{2,1,0:T(8,128)(2,1)S(1)} %all-to-all-done.4.docs_ref, bf16[32,4096]{1,0:T(8,128)(2,1)S(1)} %pad_maximum_fusion.here_ref, bf16[32,4096]{1,0:T(8,128)(2,1)S(1)} %collective-permute-done.6.one_ref, ...), custom_call_target="tpu_custom_call" | custom-call | tf_op jit(solution)/shard_map/scores/pallas_call | solution.py:149
  (57 shorter events, 12.9 us)
Async XLA Ops:
  7.2 25.5 %copy-start = (bf16[512,64]{0,1:T(8,128)(2,1)S(1)}, bf16[512,64]{0,1:T(8,128)(2,1)}, u32[]{:S(2)}) copy-start(bf16[512,64]{0,1:T(8,128)(2,1)} %param.14) | copy-start | bytes 196612
  7.2 31.7 %copy-start.4 = (bf16[128,8192]{1,0:T(8,128)(2,1)S(1)}, bf16[128,8192]{1,0:T(8,128)(2,1)}, u32[]{:S(2)}) copy-start(bf16[128,8192]{1,0:T(8,128)(2,1)} %hidden_hbm.1) | copy-start | bytes 6291460
  8.7 25.0 %all-to-all-start = ((bf16[8,64,128]{2,1,0:T(8,128)(2,1)}), bf16[8,64,128]{2,1,0:T(8,128)(2,1)S(1)}, u32[]{:S(2)}, u32[]{:S(2)}) async-start(bf16[8,64,128]{2,1,0:T(8,128)(2,1)} %broadcast_in_dim.13), calls=%async_computation | async-start | bytes 262144 | tf_op jit(solution)/shard_map/all_to_all | solution.py:20
  21.8 18.0 %collective-permute-start.1 = (bf16[128,512]{1,0:T(8,128)(2,1)}, bf16[128,512]{1,0:T(8,128)(2,1)S(1)}, u32[]{:S(2)}, u32[]{:S(2)}) collective-permute-start(bf16[128,512]{1,0:T(8,128)(2,1)} %refs_1_.1), channel_id=1, source_target_pairs={{116,0},{0,16},{16,32},{32,48},{48,64},{64,80},{80,96},{96,112},{1... | collective-permute-start | bytes 393224 | tf_op jit(solution)/shard_map/ppermute | solution.py:31
  25.2 14.7 %collective-permute-start.2 = (bf16[128,512]{1,0:T(8,128)(2,1)}, bf16[128,512]{1,0:T(8,128)(2,1)S(1)}, u32[]{:S(2)}, u32[]{:S(2)}) collective-permute-start(bf16[128,512]{1,0:T(8,128)(2,1)} %refs_1_.1), channel_id=1, source_target_pairs={{16,0},{32,16},{48,32},{64,48},{80,64},{96,80},{112,96},{4,112},{2... | collective-permute-start | bytes 393224 | tf_op jit(solution)/shard_map/ppermute | solution.py:31
  33.7 6.1 %copy-start.3 = (bf16[128,512]{1,0:T(8,128)(2,1)S(1)}, bf16[128,512]{1,0:T(8,128)(2,1)}, u32[]{:S(2)}) copy-start(bf16[128,512]{1,0:T(8,128)(2,1)} %refs_1_.1) | copy-start | bytes 393220
  34.7 12.5 %all-to-all-start.1 = ((bf16[4,592,128]{2,1,0:T(8,128)(2,1)}), bf16[4,592,128]{2,1,0:T(8,128)(2,1)S(1)}, u32[]{:S(2)}, u32[]{:S(2)}) async-start(bf16[4,592,128]{2,1,0:T(8,128)(2,1)} %broadcast_in_dim.15), calls=%async_computation.1 | async-start | bytes 1212416 | tf_op jit(solution)/shard_map/all_to_all | solution.py:20
  38.8 102.9 %all-gather.2.cloned.1.call-start = ((), (), s32[]{:S(2)}) async-start(), calls=%async_computation.5 | async-start | bytes 9437184 | tf_op jit(solution)/shard_map/all_gather | solution.py:205
  39.9 29.4 %collective-permute-start.3 = (bf16[384,512]{1,0:T(8,128)(2,1)S(1)}, bf16[384,512]{1,0:T(8,128)(2,1)S(1)}, u32[]{:S(2)}, u32[]{:S(2)}) collective-permute-start(bf16[384,512]{1,0:T(8,128)(2,1)S(1)} %near_three.1.near_ref), channel_id=1, source_target_pairs={{48,0},{64,16},{80,32},{96,48},{112,64},{4,80},{20,96},{36,112},{5... | collective-permute-start | bytes 1179656 | tf_op jit(solution)/shard_map/ppermute | solution.py:31
  43.3 29.1 %collective-permute-start.4 = (bf16[384,512]{1,0:T(8,128)(2,1)S(1)}, bf16[384,512]{1,0:T(8,128)(2,1)}, u32[]{:S(2)}, u32[]{:S(2)}) collective-permute-start(bf16[384,512]{1,0:T(8,128)(2,1)S(1)} %near_three.1.near_ref), channel_id=1, source_target_pairs={{84,0},{100,16},{116,32},{0,48},{16,64},{32,80},{48,96},{64,112},{... | collective-permute-start | bytes 1179656 | tf_op jit(solution)/shard_map/ppermute | solution.py:31
  47.1 7.1 %collective-permute-start = (bf16[4,592,128]{2,1,0:T(8,128)(2,1)S(1)}, bf16[4,592,128]{2,1,0:T(8,128)(2,1)}, u32[]{:S(2)}, u32[]{:S(2)}) collective-permute-start(bf16[4,592,128]{2,1,0:T(8,128)(2,1)S(1)} %all-to-all-done.1.own_ref), channel_id=1, source_target_pairs={{0,8},{8,0},{1,9},{9,1},{2,10},{10,2},{3,11},{11,3},{4,12},{12,4},... | collective-permute-start | bytes 1818632 | tf_op jit(solution)/shard_map/ppermute | solution.py:24
  54.2 20.2 %copy-start.1 = (bf16[128,8192]{1,0:T(8,128)(2,1)}, bf16[128,8192]{1,0:T(8,128)(2,1)S(1)}, u32[]{:S(2)}) copy-start(bf16[128,8192]{1,0:T(8,128)(2,1)S(1)} %fusion.2.normed_ref.normed_hbm) | copy-start | bytes 6291460
  56.6 0.6 copy-start.2
  75.4 13.0 %all-to-all-start.2 = ((f32[8,8,128]{2,1,0:T(8,128)}), f32[8,8,128]{2,1,0:T(8,128)S(1)}, u32[]{:S(2)}, u32[]{:S(2)}) async-start(f32[8,8,128]{2,1,0:T(8,128)} %bitcast.36), calls=%async_computation.2 | async-start | bytes 65536 | tf_op jit(solution)/shard_map/all_to_all | solution.py:210
  88.7 11.7 %copy-start.5 = (bf16[16,4096]{1,0:T(8,128)(2,1)S(1)}, bf16[16,4096]{1,0:T(8,128)(2,1)}, u32[]{:S(2)}) copy-start(bf16[16,4096]{1,0:T(8,128)(2,1)} %param.16) | copy-start | bytes 393220
  88.7 51.7 %copy-start.6 = (f32[128,1]{0,1:T(1,128)S(1)}, f32[128,1]{0,1:T(1,128)}, u32[]{:S(2)}) copy-start(f32[128,1]{0,1:T(1,128)} %get-tuple-element.23) | copy-start | bytes 1540
  88.7 52.5 %copy-start.7 = (s32[8]{0:T(128)S(1)}, s32[8]{0:T(128)}, u32[]{:S(2)}) copy-start(s32[8]{0:T(128)} %constant.42.clone) | copy-start | bytes 100
  90.9 24.3 %all-to-all-start.3 = ((f32[64,1,512]{2,1,0:T(1,128)}), f32[64,1,512]{2,1,0:T(1,128)S(1)}, u32[]{:S(2)}, u32[]{:S(2)}) async-start(f32[64,1,512]{2,1,0:T(1,128)} %reshape.103), calls=%async_computation.3 | async-start | bytes 262144 | tf_op jit(solution)/shard_map/all_to_all | solution.py:227
  100.4 32.7 %collective-permute-start.5 = (bf16[16,4096]{1,0:T(8,128)(2,1)S(1)}, bf16[16,4096]{1,0:T(8,128)(2,1)S(1)}, u32[]{:S(2)}, u32[]{:S(2)}) collective-permute-start(bf16[16,4096]{1,0:T(8,128)(2,1)S(1)} %copy-done.5), channel_id=1, source_target_pairs={{0,4},{4,0},{1,5},{5,1},{2,6},{6,2},{3,7},{7,3},{8,12},{12,8},{9,1... | collective-permute-start | bytes 393224 | tf_op jit(solution)/shard_map/ppermute | solution.py:24
  117.6 33.8 %all-to-all-start.4 = ((bf16[64,8,128]{2,1,0:T(8,128)(2,1)}), bf16[64,8,128]{2,1,0:T(8,128)(2,1)S(1)}, u32[]{:S(2)}, u32[]{:S(2)}) async-start(bf16[64,8,128]{2,1,0:T(8,128)(2,1)} %broadcast_in_dim.16), calls=%async_computation.4 | async-start | bytes 262144 | tf_op jit(solution)/shard_map/all_to_all | solution.py:20
  133.2 18.3 %collective-permute-start.6 = (bf16[32,4096]{1,0:T(8,128)(2,1)S(1)}, bf16[32,4096]{1,0:T(8,128)(2,1)S(1)}, u32[]{:S(2)}, u32[]{:S(2)}) collective-permute-start(bf16[32,4096]{1,0:T(8,128)(2,1)S(1)} %pad_maximum_fusion.here_ref), channel_id=1, source_target_pairs={{1,0},{2,1},{3,2},{0,3},{5,4},{6,5},{7,6},{4,7},{9,8},{10,9},{11,1... | collective-permute-start | bytes 786440 | tf_op jit(solution)/shard_map/ppermute | solution.py:162
  135.1 16.3 %collective-permute-start.7 = (bf16[32,4096]{1,0:T(8,128)(2,1)S(1)}, bf16[32,4096]{1,0:T(8,128)(2,1)S(1)}, u32[]{:S(2)}, u32[]{:S(2)}) collective-permute-start(bf16[32,4096]{1,0:T(8,128)(2,1)S(1)} %pad_maximum_fusion.here_ref), channel_id=1, source_target_pairs={{2,0},{3,1},{0,2},{1,3},{6,4},{7,5},{4,6},{5,7},{10,8},{11,9},{8,1... | collective-permute-start | bytes 786440 | tf_op jit(solution)/shard_map/ppermute | solution.py:162
  137.6 14.7 %collective-permute-start.8 = (bf16[32,4096]{1,0:T(8,128)(2,1)S(1)}, bf16[32,4096]{1,0:T(8,128)(2,1)S(1)}, u32[]{:S(2)}, u32[]{:S(2)}) collective-permute-start(bf16[32,4096]{1,0:T(8,128)(2,1)S(1)} %pad_maximum_fusion.here_ref), channel_id=1, source_target_pairs={{3,0},{0,1},{1,2},{2,3},{7,4},{4,5},{5,6},{6,7},{11,8},{8,9},{9,10... | collective-permute-start | bytes 786440 | tf_op jit(solution)/shard_map/ppermute | solution.py:162
Sparse Core Ops, SparseCore 0:
  74.6 56.6 all-gather.1

commit v6 on v5

--- a/solution.py
+++ b/solution.py
@@ -83,12 +83,15 @@
     width = normed_ref.shape[1]
     copies = [
         pltpu.make_async_copy(
-            weight_hbm.at[pl.ds(chunk * depth, depth)], held.at[chunk], arrived.at[chunk]
+            weight_hbm.at[pl.ds((chunk * 4 + part) * depth, depth)],
+            held.at[chunk, :, pl.ds(part * BLOCK, BLOCK)],
+            arrived.at[chunk * 4 + part],
         )
         for chunk in range(chunks)
+        for part in range(4)
     ]
-    normed_copy = pltpu.make_async_copy(normed_hbm, normed_ref, arrived.at[chunks])
-    hidden_copy = pltpu.make_async_copy(hidden_hbm, hidden_ref, arrived.at[chunks + 1])
+    normed_copy = pltpu.make_async_copy(normed_hbm, normed_ref, arrived.at[4 * chunks])
+    hidden_copy = pltpu.make_async_copy(hidden_hbm, hidden_ref, arrived.at[4 * chunks + 1])
     normed_copy.start()
     for copy in copies:
         copy.start()
@@ -98,8 +101,8 @@
     total = jnp.zeros(values_ref.shape, jnp.float32)
     normed_copy.wait()
     for y in range(chunks // 2):
-        copies[2 * y].wait()
-        copies[2 * y + 1].wait()
+        for copy in copies[8 * y : 8 * y + 8]:
+            copy.wait()
         for step in range(depth // BLOCK):
             rows = slice(step * BLOCK, (step + 1) * BLOCK)
             weight = jnp.concatenate([held[2 * y, rows], held[2 * y + 1, rows]], 0)
@@ -185,9 +188,10 @@
     packed = spread_to_all(jnp.concatenate([factor_z, right_t, ids_rows], 0), "y")
     packed_other = swapped(packed, "core")
 
-    ahead, behind = from_z(value_weight, 1), from_z(value_weight, -1)
-    near = call(joined_kernel, struct((3 * BLOCK, kv), jnp.bfloat16), 0, "near_three")(
-        behind, value_weight, ahead
+    quarter = lax.dynamic_slice_in_dim(value_weight, lax.axis_index("x") * BLOCK, BLOCK, 1)
+    ahead, behind = from_z(quarter, 1), from_z(quarter, -1)
+    near = call(joined_kernel, struct((3 * BLOCK, BLOCK), jnp.bfloat16), 0, "near_three")(
+        behind, quarter, ahead
     )
     near = after(near, factor_z)
     far_ahead, far_behind = from_z(near, 3), from_z(near, -3)
@@ -199,10 +203,10 @@
         core_row, normed, packed, packed_other
     )
 
-    w_z = call(along_z_kernel, struct((8 * BLOCK, kv), jnp.bfloat16), 0, "along_z")(
+    w_z = call(along_z_kernel, struct((8 * BLOCK, BLOCK), jnp.bfloat16), 0, "along_z")(
         near, *after((far_ahead, far_behind), left_t)
     )
-    w_all = lax.all_gather(w_z, ("y", "core"), axis=0, tiled=True)
+    w_all = lax.all_gather(w_z, ("y", "core", "x"), axis=0, tiled=True)
     z_place = (lax.axis_index("zl") + jnp.array(Z_STEPS, jnp.int32)) % 8
 
     q_other = swapped(after(queries, left_t), "zh")
@@ -245,7 +249,7 @@
             pltpu.VMEM((rows, width), jnp.float32),
             pltpu.VMEM((rows, width), jnp.bfloat16),
             pltpu.VMEM((rows, width), jnp.bfloat16),
-            pltpu.SemaphoreType.DMA((chunks + 2,)),
+            pltpu.SemaphoreType.DMA((4 * chunks + 2,)),
         ],
         compiler_params=pltpu.CompilerParams(vmem_limit_bytes=58 * 1024 * 1024),
         name="layer",

time: 162 us -> 147 us (0.907)
  the two profiles are of different devices: /device:TPU:1 before, /device:TPU:257 now
where the time goes in v6:
time: 147 us; the launch traced here: 146 us
  starting transfers between devices  79 us (54%)
  waiting for transfers between devices  24.7 us (17%)
  between operations  14.4 us (10%)
  Pallas kernels  14 us (10%)
  local copies, waits for them, and re-layouts  6.11 us (4%)
  other arithmetic  5.37 us (4%)
  matrix products  2.29 us (2%)
    all_to_all x3, starting transfers between devices, spread_to_all(): return lax.all_to_all(copies, axes, 0, 0, tiled=True)  25.4 us
    ppermute x4, starting transfers between devices, from_z(): lax.ppermute(value, ('zl', 'zh'), [(place((z + step) % 16), place(z)) for...  15.3 us
    all_to_all x1, starting transfers between devices, shards(): lax.all_to_all(doc_term.reshape(64, 8, rank), ('zl', 'zh', 'x'), 0, 0, ti...  15 us
    all_gather x1, waiting for transfers between devices, shards(): w_all = lax.all_gather(w_z, ('y', 'core', 'x'), axis=0, tiled=True)  14.1 us
    ppermute x3, starting transfers between devices, from_x(): return lax.ppermute(value, 'x', [((x + step) % 4, x) for x in range(4)])  10 us
    pallas_call x1, Pallas kernels, shards(): pl.pallas_call(layer_kernel, out_shape=(struct((rows, kv), jnp.bfloat16),...  9.86 us
    ppermute x2, starting transfers between devices, swapped(): return lax.ppermute(value, axis, [(0, 1), (1, 0)])  7.96 us
    all_to_all x1, waiting for transfers between devices, shards(): lax.all_to_all(doc_term.reshape(64, 8, rank), ('zl', 'zh', 'x'), 0, 0, ti...  5.64 us
  transfers between devices with their start and end apart: 15, of which 4 were waited for; matrix products, arithmetic and copies ran while one was open for 8% of the time, Pallas kernels for 7%

profile of v6, /device:TPU:257, one launch (start us, length us, event | category | flops | bytes accessed | tf_op | source)
XLA Modules:
  0.0 145.9 jit_solution(11459125026961940171)
XLA Ops:
  8.7 4.7 %all-to-all-start = ((bf16[8,64,128]{2,1,0:T(8,128)(2,1)}), bf16[8,64,128]{2,1,0:T(8,128)(2,1)S(1)}, u32[]{:S(2)}, u32[]{:S(2)}) async-start(bf16[8,64,128]{2,1,0:T(8,128)(2,1)} %broadcast_in_dim.13), calls=%async_computation | async-start | bytes 262144 | tf_op jit(solution)/shard_map/all_to_all | solution.py:20
  13.5 3.4 %collective-permute-start.1 = (bf16[128,128]{1,0:T(8,128)(2,1)S(1)}, bf16[128,128]{1,0:T(8,128)(2,1)S(1)}, u32[]{:S(2)}, u32[]{:S(2)}) collective-permute-start(bf16[128,128]{1,0:T(8,128)(2,1)S(1)} %constant_dynamic-slice_fusion.refs_1_), channel_id=1, source_target_pairs={{116,0},{0,16},{16,32},{32,48},{48,64},{64,80},{80,96},{96,112},{1... | collective-permute-start | bytes 98312 | tf_op jit(solution)/shard_map/ppermute | solution.py:31
  16.9 4.9 %collective-permute-start.2 = (bf16[128,128]{1,0:T(8,128)(2,1)S(1)}, bf16[128,128]{1,0:T(8,128)(2,1)S(1)}, u32[]{:S(2)}, u32[]{:S(2)}) collective-permute-start(bf16[128,128]{1,0:T(8,128)(2,1)S(1)} %constant_dynamic-slice_fusion.refs_1_), channel_id=1, source_target_pairs={{16,0},{32,16},{48,32},{64,48},{80,64},{96,80},{112,96},{4,112},{2... | collective-permute-start | bytes 98312 | tf_op jit(solution)/shard_map/ppermute | solution.py:31
  22.4 1.1 convolution_convert_fusion
  24.8 4.2 %all-to-all-start.1 = ((bf16[4,592,128]{2,1,0:T(8,128)(2,1)}), bf16[4,592,128]{2,1,0:T(8,128)(2,1)S(1)}, u32[]{:S(2)}, u32[]{:S(2)}) async-start(bf16[4,592,128]{2,1,0:T(8,128)(2,1)} %broadcast_in_dim.15), calls=%async_computation.1 | async-start | bytes 1212416 | tf_op jit(solution)/shard_map/all_to_all | solution.py:20
  29.5 3.1 %collective-permute-start.3 = (bf16[384,128]{1,0:T(8,128)(2,1)S(1)}, bf16[384,128]{1,0:T(8,128)(2,1)}, u32[]{:S(2)}, u32[]{:S(2)}) collective-permute-start(bf16[384,128]{1,0:T(8,128)(2,1)S(1)} %near_three.1.near_ref), channel_id=1, source_target_pairs={{48,0},{64,16},{80,32},{96,48},{112,64},{4,80},{20,96},{36,112},{5... | collective-permute-start | bytes 294920 | tf_op jit(solution)/shard_map/ppermute | solution.py:31
  32.6 4.0 %collective-permute-start.4 = (bf16[384,128]{1,0:T(8,128)(2,1)S(1)}, bf16[384,128]{1,0:T(8,128)(2,1)}, u32[]{:S(2)}, u32[]{:S(2)}) collective-permute-start(bf16[384,128]{1,0:T(8,128)(2,1)S(1)} %near_three.1.near_ref), channel_id=1, source_target_pairs={{84,0},{100,16},{116,32},{0,48},{16,64},{32,80},{48,96},{64,112},{... | collective-permute-start | bytes 294920 | tf_op jit(solution)/shard_map/ppermute | solution.py:31
  36.6 5.6 %collective-permute-start = (bf16[4,592,128]{2,1,0:T(8,128)(2,1)S(1)}, bf16[4,592,128]{2,1,0:T(8,128)(2,1)S(1)}, u32[]{:S(2)}, u32[]{:S(2)}) collective-permute-start(bf16[4,592,128]{2,1,0:T(8,128)(2,1)S(1)} %all-to-all-done.1.own_ref), channel_id=1, source_target_pairs={{0,8},{8,0},{1,9},{9,1},{2,10},{10,2},{3,11},{11,3},{4,12},{12,4},... | collective-permute-start | bytes 1818632 | tf_op jit(solution)/shard_map/ppermute | solution.py:24
  42.2 2.2 %fusion.2.normed_ref.normed_hbm = bf16[128,8192]{1,0:T(8,128)(2,1)S(1)} fusion(bf16[128,8192]{1,0:T(8,128)(2,1)} %hidden_hbm.1, f32[8192]{0:T(1024)} %param.10, f32[128]{0:T(128)S(1)} %get-tuple-element.24), kind=kLoop, calls=%fused_computation.4 | loop fusion | flops 4194304 | bytes 4227584 | tf_op jit(solution)/shard_map/convert_element_type | solution.py:201
  45.8 1.7 %along_z.1 = bf16[1024,128]{1,0:T(8,128)(2,1)} custom-call(bf16[384,128]{1,0:T(8,128)(2,1)S(1)} %near_three.1.near_ref, bf16[384,128]{1,0:T(8,128)(2,1)} %collective-permute-done.3.ahead_ref, bf16[384,128]{1,0:T(8,128)(2,1)} %collective-permute-done.4.behind_ref), custom_call_target="tpu_custom_call" | custom-call | tf_op jit(solution)/shard_map/along_z/pallas_call | solution.py:152
  47.5 5.4 %all-to-all-start.2 = ((f32[8,8,128]{2,1,0:T(8,128)}), f32[8,8,128]{2,1,0:T(8,128)S(1)}, u32[]{:S(2)}, u32[]{:S(2)}) async-start(f32[8,8,128]{2,1,0:T(8,128)} %bitcast.36), calls=%async_computation.2 | async-start | bytes 65536 | tf_op jit(solution)/shard_map/all_to_all | solution.py:214
  53.0 4.6 %all-to-all-done.2 = f32[8,8,128]{2,1,0:T(8,128)S(1)} async-done(((f32[8,8,128]{2,1,0:T(8,128)}), f32[8,8,128]{2,1,0:T(8,128)S(1)}, u32[]{:S(2)}, u32[]{:S(2)}) %all-to-all-start.2) | async-done | bytes 32800 | tf_op jit(solution)/shard_map/all_to_all | solution.py:214
  57.9 1.2 fusion.4
  60.1 15.0 %all-to-all-start.3 = ((f32[64,1,512]{2,1,0:T(1,128)}), f32[64,1,512]{2,1,0:T(1,128)S(1)}, u32[]{:S(2)}, u32[]{:S(2)}) async-start(f32[64,1,512]{2,1,0:T(1,128)} %reshape.103), calls=%async_computation.3 | async-start | bytes 262144 | tf_op jit(solution)/shard_map/all_to_all | solution.py:231
  75.1 2.4 %collective-permute-start.5 = (bf16[16,4096]{1,0:T(8,128)(2,1)S(1)}, bf16[16,4096]{1,0:T(8,128)(2,1)S(1)}, u32[]{:S(2)}, u32[]{:S(2)}) collective-permute-start(bf16[16,4096]{1,0:T(8,128)(2,1)S(1)} %copy-done.4), channel_id=1, source_target_pairs={{0,4},{4,0},{1,5},{5,1},{2,6},{6,2},{3,7},{7,3},{8,12},{12,8},{9,1... | collective-permute-start | bytes 393224 | tf_op jit(solution)/shard_map/ppermute | solution.py:24
  77.5 5.6 %all-to-all-done.3 = f32[64,1,512]{2,1,0:T(1,128)S(1)} async-done(((f32[64,1,512]{2,1,0:T(1,128)}), f32[64,1,512]{2,1,0:T(1,128)S(1)}, u32[]{:S(2)}, u32[]{:S(2)}) %all-to-all-start.3) | async-done | bytes 131104 | tf_op jit(solution)/shard_map/all_to_all | solution.py:231
  83.6 0.9 reduce
  85.5 16.5 %all-to-all-start.4 = ((bf16[64,8,128]{2,1,0:T(8,128)(2,1)}), bf16[64,8,128]{2,1,0:T(8,128)(2,1)S(1)}, u32[]{:S(2)}, u32[]{:S(2)}) async-start(bf16[64,8,128]{2,1,0:T(8,128)(2,1)} %broadcast_in_dim.16), calls=%async_computation.4 | async-start | bytes 262144 | tf_op jit(solution)/shard_map/all_to_all | solution.py:20
  102.0 5.6 %collective-permute-start.6 = (bf16[32,4096]{1,0:T(8,128)(2,1)S(1)}, bf16[32,4096]{1,0:T(8,128)(2,1)S(1)}, u32[]{:S(2)}, u32[]{:S(2)}) collective-permute-start(bf16[32,4096]{1,0:T(8,128)(2,1)S(1)} %pad_maximum_fusion.here_ref), channel_id=1, source_target_pairs={{1,0},{2,1},{3,2},{0,3},{5,4},{6,5},{7,6},{4,7},{9,8},{10,9},{11,1... | collective-permute-start | bytes 786440 | tf_op jit(solution)/shard_map/ppermute | solution.py:165
  107.6 1.9 %collective-permute-start.7 = (bf16[32,4096]{1,0:T(8,128)(2,1)S(1)}, bf16[32,4096]{1,0:T(8,128)(2,1)S(1)}, u32[]{:S(2)}, u32[]{:S(2)}) collective-permute-start(bf16[32,4096]{1,0:T(8,128)(2,1)S(1)} %pad_maximum_fusion.here_ref), channel_id=1, source_target_pairs={{2,0},{3,1},{0,2},{1,3},{6,4},{7,5},{4,6},{5,7},{10,8},{11,9},{8,1... | collective-permute-start | bytes 786440 | tf_op jit(solution)/shard_map/ppermute | solution.py:165
  109.6 2.5 %collective-permute-start.8 = (bf16[32,4096]{1,0:T(8,128)(2,1)S(1)}, bf16[32,4096]{1,0:T(8,128)(2,1)S(1)}, u32[]{:S(2)}, u32[]{:S(2)}) collective-permute-start(bf16[32,4096]{1,0:T(8,128)(2,1)S(1)} %pad_maximum_fusion.here_ref), channel_id=1, source_target_pairs={{3,0},{0,1},{1,2},{2,3},{7,4},{4,5},{5,6},{6,7},{11,8},{8,9},{9,10... | collective-permute-start | bytes 786440 | tf_op jit(solution)/shard_map/ppermute | solution.py:165
  113.4 14.1 %all-gather.2.cloned.1.call-done.weight_hbm = bf16[32768,128]{1,0:T(8,128)(2,1)} async-done(((bf16[1024,128]{1,0:T(8,128)(2,1)}), bf16[32768,128]{1,0:T(8,128)(2,1)}) %all-gather.2.cloned.1.call-update) | async-done | bytes 8388624 | tf_op jit(solution)/shard_map/all_gather | solution.py:209
  127.5 9.9 %layer.1 = (bf16[128,512]{1,0:T(8,128)(2,1)}, bf16[128,8192]{1,0:T(8,128)(2,1)}) custom-call(s32[8]{0:T(128)} %and_select_fusion.place_ref, bf16[128,8192]{1,0:T(8,128)(2,1)} %copy-done.1, bf16[128,8192]{1,0:T(8,128)(2,1)} %hidden_hbm.1, f32[1,8192]{1,0:T(1,128)} %bitcast.42, f32[128,1]{1,0:T(8,128)} %copy.21.scale_ref, bf16[128,512]{1,0:T(8,128)(2,1)} %grad_ref.1, ...), custom_call_target="tpu_custom_call" | custom-call | tf_op jit(solution)/shard_map/layer/pallas_call | solution.py:242
  137.4 1.6 %scores.1 = f32[8,128]{1,0:T(8,128)} custom-call(s32[2]{0:T(128)S(1)} %pad_add_fusion.index_ref, bf16[64,8,128]{2,1,0:T(8,128)(2,1)S(1)} %all-to-all-done.4.docs_ref, bf16[32,4096]{1,0:T(8,128)(2,1)S(1)} %pad_maximum_fusion.here_ref, bf16[32,4096]{1,0:T(8,128)(2,1)S(1)} %collective-permute-done.6.one_ref, ...), custom_call_target="tpu_custom_call" | custom-call | tf_op jit(solution)/shard_map/scores/pallas_call | solution.py:152
  (54 shorter events, 9.5 us)
Async XLA Ops:
  7.2 6.3 %copy-start = (bf16[128,512]{1,0:T(8,128)(2,1)S(1)}, bf16[128,512]{1,0:T(8,128)(2,1)}, u32[]{:S(2)}) copy-start(bf16[128,512]{1,0:T(8,128)(2,1)} %param.11) | copy-start | bytes 393220
  7.2 21.8 %copy-start.3 = (bf16[128,8192]{1,0:T(8,128)(2,1)S(1)}, bf16[128,8192]{1,0:T(8,128)(2,1)}, u32[]{:S(2)}) copy-start(bf16[128,8192]{1,0:T(8,128)(2,1)} %hidden_hbm.1) | copy-start | bytes 6291460
  8.7 15.1 %all-to-all-start = ((bf16[8,64,128]{2,1,0:T(8,128)(2,1)}), bf16[8,64,128]{2,1,0:T(8,128)(2,1)S(1)}, u32[]{:S(2)}, u32[]{:S(2)}) async-start(bf16[8,64,128]{2,1,0:T(8,128)(2,1)} %broadcast_in_dim.13), calls=%async_computation | async-start | bytes 262144 | tf_op jit(solution)/shard_map/all_to_all | solution.py:20
  13.5 15.9 %collective-permute-start.1 = (bf16[128,128]{1,0:T(8,128)(2,1)S(1)}, bf16[128,128]{1,0:T(8,128)(2,1)S(1)}, u32[]{:S(2)}, u32[]{:S(2)}) collective-permute-start(bf16[128,128]{1,0:T(8,128)(2,1)S(1)} %constant_dynamic-slice_fusion.refs_1_), channel_id=1, source_target_pairs={{116,0},{0,16},{16,32},{32,48},{48,64},{64,80},{80,96},{96,112},{1... | collective-permute-start | bytes 98312 | tf_op jit(solution)/shard_map/ppermute | solution.py:31
  16.9 12.6 %collective-permute-start.2 = (bf16[128,128]{1,0:T(8,128)(2,1)S(1)}, bf16[128,128]{1,0:T(8,128)(2,1)S(1)}, u32[]{:S(2)}, u32[]{:S(2)}) collective-permute-start(bf16[128,128]{1,0:T(8,128)(2,1)S(1)} %constant_dynamic-slice_fusion.refs_1_), channel_id=1, source_target_pairs={{16,0},{32,16},{48,32},{64,48},{80,64},{96,80},{112,96},{4,112},{2... | collective-permute-start | bytes 98312 | tf_op jit(solution)/shard_map/ppermute | solution.py:31
  24.8 11.8 %all-to-all-start.1 = ((bf16[4,592,128]{2,1,0:T(8,128)(2,1)}), bf16[4,592,128]{2,1,0:T(8,128)(2,1)S(1)}, u32[]{:S(2)}, u32[]{:S(2)}) async-start(bf16[4,592,128]{2,1,0:T(8,128)(2,1)} %broadcast_in_dim.15), calls=%async_computation.1 | async-start | bytes 1212416 | tf_op jit(solution)/shard_map/all_to_all | solution.py:20
  28.9 98.6 %all-gather.2.cloned.1.call-start = ((), (), s32[]{:S(2)}) async-start(), calls=%async_computation.5 | async-start | bytes 8650752 | tf_op jit(solution)/shard_map/all_gather | solution.py:209
  29.5 16.4 %collective-permute-start.3 = (bf16[384,128]{1,0:T(8,128)(2,1)S(1)}, bf16[384,128]{1,0:T(8,128)(2,1)}, u32[]{:S(2)}, u32[]{:S(2)}) collective-permute-start(bf16[384,128]{1,0:T(8,128)(2,1)S(1)} %near_three.1.near_ref), channel_id=1, source_target_pairs={{48,0},{64,16},{80,32},{96,48},{112,64},{4,80},{20,96},{36,112},{5... | collective-permute-start | bytes 294920 | tf_op jit(solution)/shard_map/ppermute | solution.py:31
  32.6 13.3 %collective-permute-start.4 = (bf16[384,128]{1,0:T(8,128)(2,1)S(1)}, bf16[384,128]{1,0:T(8,128)(2,1)}, u32[]{:S(2)}, u32[]{:S(2)}) collective-permute-start(bf16[384,128]{1,0:T(8,128)(2,1)S(1)} %near_three.1.near_ref), channel_id=1, source_target_pairs={{84,0},{100,16},{116,32},{0,48},{16,64},{32,80},{48,96},{64,112},{... | collective-permute-start | bytes 294920 | tf_op jit(solution)/shard_map/ppermute | solution.py:31
  36.6 7.8 %collective-permute-start = (bf16[4,592,128]{2,1,0:T(8,128)(2,1)S(1)}, bf16[4,592,128]{2,1,0:T(8,128)(2,1)S(1)}, u32[]{:S(2)}, u32[]{:S(2)}) collective-permute-start(bf16[4,592,128]{2,1,0:T(8,128)(2,1)S(1)} %all-to-all-done.1.own_ref), channel_id=1, source_target_pairs={{0,8},{8,0},{1,9},{9,1},{2,10},{10,2},{3,11},{11,3},{4,12},{12,4},... | collective-permute-start | bytes 1818632 | tf_op jit(solution)/shard_map/ppermute | solution.py:24
  44.4 3.2 %copy-start.1 = (bf16[128,8192]{1,0:T(8,128)(2,1)}, bf16[128,8192]{1,0:T(8,128)(2,1)S(1)}, u32[]{:S(2)}) copy-start(bf16[128,8192]{1,0:T(8,128)(2,1)S(1)} %fusion.2.normed_ref.normed_hbm) | copy-start | bytes 6291460
  45.2 0.6 copy-start.2
  47.5 10.1 %all-to-all-start.2 = ((f32[8,8,128]{2,1,0:T(8,128)}), f32[8,8,128]{2,1,0:T(8,128)S(1)}, u32[]{:S(2)}, u32[]{:S(2)}) async-start(f32[8,8,128]{2,1,0:T(8,128)} %bitcast.36), calls=%async_computation.2 | async-start | bytes 65536 | tf_op jit(solution)/shard_map/all_to_all | solution.py:214
  57.9 17.2 %copy-start.4 = (bf16[16,4096]{1,0:T(8,128)(2,1)S(1)}, bf16[16,4096]{1,0:T(8,128)(2,1)}, u32[]{:S(2)}) copy-start(bf16[16,4096]{1,0:T(8,128)(2,1)} %param.16) | copy-start | bytes 393220
  57.9 55.0 %copy-start.5 = (s32[8]{0:T(128)S(1)}, s32[8]{0:T(128)}, u32[]{:S(2)}) copy-start(s32[8]{0:T(128)} %constant.46.clone) | copy-start | bytes 100
  60.1 23.0 %all-to-all-start.3 = ((f32[64,1,512]{2,1,0:T(1,128)}), f32[64,1,512]{2,1,0:T(1,128)S(1)}, u32[]{:S(2)}, u32[]{:S(2)}) async-start(f32[64,1,512]{2,1,0:T(1,128)} %reshape.103), calls=%async_computation.3 | async-start | bytes 262144 | tf_op jit(solution)/shard_map/all_to_all | solution.py:231
  75.1 26.9 %collective-permute-start.5 = (bf16[16,4096]{1,0:T(8,128)(2,1)S(1)}, bf16[16,4096]{1,0:T(8,128)(2,1)S(1)}, u32[]{:S(2)}, u32[]{:S(2)}) collective-permute-start(bf16[16,4096]{1,0:T(8,128)(2,1)S(1)} %copy-done.4), channel_id=1, source_target_pairs={{0,4},{4,0},{1,5},{5,1},{2,6},{6,2},{3,7},{7,3},{8,12},{12,8},{9,1... | collective-permute-start | bytes 393224 | tf_op jit(solution)/shard_map/ppermute | solution.py:24
  85.5 51.9 %all-to-all-start.4 = ((bf16[64,8,128]{2,1,0:T(8,128)(2,1)}), bf16[64,8,128]{2,1,0:T(8,128)(2,1)S(1)}, u32[]{:S(2)}, u32[]{:S(2)}) async-start(bf16[64,8,128]{2,1,0:T(8,128)(2,1)} %broadcast_in_dim.16), calls=%async_computation.4 | async-start | bytes 262144 | tf_op jit(solution)/shard_map/all_to_all | solution.py:20
  102.0 35.4 %collective-permute-start.6 = (bf16[32,4096]{1,0:T(8,128)(2,1)S(1)}, bf16[32,4096]{1,0:T(8,128)(2,1)S(1)}, u32[]{:S(2)}, u32[]{:S(2)}) collective-permute-start(bf16[32,4096]{1,0:T(8,128)(2,1)S(1)} %pad_maximum_fusion.here_ref), channel_id=1, source_target_pairs={{1,0},{2,1},{3,2},{0,3},{5,4},{6,5},{7,6},{4,7},{9,8},{10,9},{11,1... | collective-permute-start | bytes 786440 | tf_op jit(solution)/shard_map/ppermute | solution.py:165
  107.6 29.8 %collective-permute-start.7 = (bf16[32,4096]{1,0:T(8,128)(2,1)S(1)}, bf16[32,4096]{1,0:T(8,128)(2,1)S(1)}, u32[]{:S(2)}, u32[]{:S(2)}) collective-permute-start(bf16[32,4096]{1,0:T(8,128)(2,1)S(1)} %pad_maximum_fusion.here_ref), channel_id=1, source_target_pairs={{2,0},{3,1},{0,2},{1,3},{6,4},{7,5},{4,6},{5,7},{10,8},{11,9},{8,1... | collective-permute-start | bytes 786440 | tf_op jit(solution)/shard_map/ppermute | solution.py:165
  109.6 27.9 %collective-permute-start.8 = (bf16[32,4096]{1,0:T(8,128)(2,1)S(1)}, bf16[32,4096]{1,0:T(8,128)(2,1)S(1)}, u32[]{:S(2)}, u32[]{:S(2)}) collective-permute-start(bf16[32,4096]{1,0:T(8,128)(2,1)S(1)} %pad_maximum_fusion.here_ref), channel_id=1, source_target_pairs={{3,0},{0,1},{1,2},{2,3},{7,4},{4,5},{5,6},{6,7},{11,8},{8,9},{9,10... | collective-permute-start | bytes 786440 | tf_op jit(solution)/shard_map/ppermute | solution.py:165
Sparse Core Ops, SparseCore 0:
  47.7 79.8 all-gather.1

commit v7 on v6

--- a/solution.py
+++ b/solution.py
@@ -76,11 +76,11 @@
 
 
 def layer_kernel(
-    place_ref, normed_hbm, hidden_hbm, gain_ref, scale_ref, grad_ref, weight_hbm,
-    values_ref, hidden_grad_ref, held, base, normed_ref, hidden_ref, arrived,
+    place_ref, hidden_hbm, gain_ref, scale_ref, grad_ref, weight_hbm,
+    values_ref, hidden_grad_ref, held, base, hidden_ref, arrived,
 ):
     chunks, depth = held.shape[:2]
-    width = normed_ref.shape[1]
+    width = hidden_ref.shape[1]
     copies = [
         pltpu.make_async_copy(
             weight_hbm.at[pl.ds((chunk * 4 + part) * depth, depth)],
@@ -90,16 +90,14 @@
         for chunk in range(chunks)
         for part in range(4)
     ]
-    normed_copy = pltpu.make_async_copy(normed_hbm, normed_ref, arrived.at[4 * chunks])
-    hidden_copy = pltpu.make_async_copy(hidden_hbm, hidden_ref, arrived.at[4 * chunks + 1])
-    normed_copy.start()
+    hidden_copy = pltpu.make_async_copy(hidden_hbm, hidden_ref, arrived.at[4 * chunks])
+    hidden_copy.start()
     for copy in copies:
         copy.start()
-    hidden_copy.start()
     grad = grad_ref[...]
     inv_rms = scale_ref[...]
     total = jnp.zeros(values_ref.shape, jnp.float32)
-    normed_copy.wait()
+    hidden_copy.wait()
     for y in range(chunks // 2):
         for copy in copies[8 * y : 8 * y + 8]:
             copy.wait()
@@ -108,12 +106,13 @@
             weight = jnp.concatenate([held[2 * y, rows], held[2 * y + 1, rows]], 0)
             offset = pl.multiple_of(y * (width // 4) + place_ref[step] * 256, 256)
             where = pl.ds(offset, 256)
-            total += jnp.dot(normed_ref[:, where], weight, preferred_element_type=jnp.float32)
+            wide = hidden_ref[:, where].astype(jnp.float32)
+            normed = (wide * inv_rms * gain_ref[:, where]).astype(jnp.bfloat16)
+            total += jnp.dot(normed, weight, preferred_element_type=jnp.float32)
             base[:, where] = inv_rms * (contract_last(grad, weight) * gain_ref[:, where])
     values_ref[...] = total.astype(jnp.bfloat16)
     along = jnp.sum(total * grad.astype(jnp.float32), axis=1, keepdims=True)
     pull = inv_rms * inv_rms * along / width
-    hidden_copy.wait()
     for start in range(0, width, 512):
         where = slice(start, start + 512)
         wide = hidden_ref[:, where].astype(jnp.float32)
@@ -179,22 +178,23 @@
     core_row = core.astype(jnp.int32).reshape(1)
     on_first = core == 0
 
+    quarter = lax.dynamic_slice_in_dim(value_weight, lax.axis_index("x") * BLOCK, BLOCK, 1)
+    ahead, behind = from_z(quarter, 1), from_z(quarter, -1)
+    near = call(joined_kernel, struct((3 * BLOCK, BLOCK), jnp.bfloat16), 0, "near_three")(
+        behind, quarter, ahead
+    )
+    far_ahead, far_behind = from_z(near, 3), from_z(near, -3)
+
     factor = input_proj.T.reshape(4, 8, 2, BLOCK).transpose(0, 2, 1, 3).reshape(rank, BLOCK)
     right_t = lax.dot_general(
         output_proj, value_grad, (((0,), (1,)), ((), ())), preferred_element_type=jnp.float32
     ).astype(jnp.bfloat16)
     ids_rows = jnp.broadcast_to(doc_ids.astype(jnp.bfloat16)[None], (16, rows))
-    factor_z = spread_to_all(factor, "zl").reshape(-1, BLOCK)
+    factor_z = spread_to_all(after(factor, near), "zl").reshape(-1, BLOCK)
     packed = spread_to_all(jnp.concatenate([factor_z, right_t, ids_rows], 0), "y")
     packed_other = swapped(packed, "core")
-
-    quarter = lax.dynamic_slice_in_dim(value_weight, lax.axis_index("x") * BLOCK, BLOCK, 1)
-    ahead, behind = from_z(quarter, 1), from_z(quarter, -1)
-    near = call(joined_kernel, struct((3 * BLOCK, BLOCK), jnp.bfloat16), 0, "near_three")(
-        behind, quarter, ahead
-    )
-    near = after(near, factor_z)
-    far_ahead, far_behind = from_z(near, 3), from_z(near, -3)
+    q_other = swapped(after(queries, factor_z), "zh")
+    packed_other, q_other = lax.optimization_barrier((packed_other, q_other))
 
     wide_in = hidden_in.astype(jnp.float32)
     inv_rms = lax.rsqrt(jnp.mean(wide_in * wide_in, axis=1, keepdims=True) + EPSILON)
@@ -204,12 +204,11 @@
     )
 
     w_z = call(along_z_kernel, struct((8 * BLOCK, BLOCK), jnp.bfloat16), 0, "along_z")(
-        near, *after((far_ahead, far_behind), left_t)
+        near, *after((far_ahead, far_behind), factor_z)
     )
     w_all = lax.all_gather(w_z, ("y", "core", "x"), axis=0, tiled=True)
     z_place = (lax.axis_index("zl") + jnp.array(Z_STEPS, jnp.int32)) % 8
 
-    q_other = swapped(after(queries, left_t), "zh")
 
     left_all = lax.all_to_all(
         left_t.reshape(8, rank // 8, rows), ("y", "core"), 0, 0, tiled=True
@@ -242,19 +241,18 @@
     values_out, hidden_grad = pl.pallas_call(
         layer_kernel,
         out_shape=(struct((rows, kv), jnp.bfloat16), struct((rows, width), jnp.bfloat16)),
-        in_specs=[pl.BlockSpec(memory_space=pltpu.SMEM), hbm, hbm, vmem, vmem, vmem, hbm],
+        in_specs=[pl.BlockSpec(memory_space=pltpu.SMEM), hbm, vmem, vmem, vmem, hbm],
         out_specs=(vmem, vmem),
         scratch_shapes=[
             pltpu.VMEM((chunks, width // chunks, kv), jnp.bfloat16),
             pltpu.VMEM((rows, width), jnp.float32),
             pltpu.VMEM((rows, width), jnp.bfloat16),
-            pltpu.VMEM((rows, width), jnp.bfloat16),
-            pltpu.SemaphoreType.DMA((4 * chunks + 2,)),
+            pltpu.SemaphoreType.DMA((4 * chunks + 1,)),
         ],
         compiler_params=pltpu.CompilerParams(vmem_limit_bytes=58 * 1024 * 1024),
         name="layer",
     )(
-        z_place.astype(jnp.int32), normed, hidden_in, norm_gain.reshape(1, width), inv_rms,
+        z_place.astype(jnp.int32), hidden_in, norm_gain.reshape(1, width), inv_rms,
         value_grad, w_all,
     )
     doc_low, values_out = lax.optimization_barrier((doc_low, values_out))

time: 147 us -> 159 us (1.082)
  the two profiles are of different devices: /device:TPU:257 before, /device:TPU:1 now
where the time goes in v7:
time: 159 us; the launch traced here: 158 us
  starting transfers between devices  87.9 us (55%)
  waiting for transfers between devices  26.4 us (17%)
  between operations  14.3 us (9%)
  Pallas kernels  13.3 us (8%)
  other arithmetic  7.05 us (4%)
  local copies, waits for them, and re-layouts  6.87 us (4%)
  matrix products  2.29 us (1%)
    ppermute x4, starting transfers between devices, from_z(): lax.ppermute(value, ('zl', 'zh'), [(place((z + step) % 16), place(z)) for...  24.2 us
    all_to_all x1, starting transfers between devices, shards(): lax.all_to_all(doc_term.reshape(64, 8, rank), ('zl', 'zh', 'x'), 0, 0, ti...  16.5 us
    all_to_all x3, starting transfers between devices, spread_to_all(): return lax.all_to_all(copies, axes, 0, 0, tiled=True)  14.9 us
    all_to_all x1, waiting for transfers between devices, shards(): lax.all_to_all(doc_term.reshape(64, 8, rank), ('zl', 'zh', 'x'), 0, 0, ti...  14.8 us
    ppermute x2, starting transfers between devices, swapped(): return lax.ppermute(value, axis, [(0, 1), (1, 0)])  14.2 us
    pallas_call x1, Pallas kernels, shards(): pl.pallas_call(layer_kernel, out_shape=(struct((rows, kv), jnp.bfloat16),...  9.56 us
    all_to_all x1, starting transfers between devices, shards(): lax.all_to_all(left_t.reshape(8, rank // 8, rows), ('y', 'core'), 0, 0, t...  9.3 us
    ppermute x3, starting transfers between devices, from_x(): return lax.ppermute(value, 'x', [((x + step) % 4, x) for x in range(4)])  8.88 us
  transfers between devices with their start and end apart: 15, of which 4 were waited for; matrix products, arithmetic and copies ran while one was open for 9% of the time, Pallas kernels for 7%

profile of v7, /device:TPU:1, one launch (start us, length us, event | category | flops | bytes accessed | tf_op | source)
XLA Modules:
  0.0 158.2 jit_solution(8810856381405324852)
XLA Ops:
  8.1 11.9 %collective-permute-start.1 = (bf16[128,128]{1,0:T(8,128)(2,1)S(1)}, bf16[128,128]{1,0:T(8,128)(2,1)S(1)}, u32[]{:S(2)}, u32[]{:S(2)}) collective-permute-start(bf16[128,128]{1,0:T(8,128)(2,1)S(1)} %constant_dynamic-slice_fusion.refs_1_), channel_id=1, source_target_pairs={{16,0},{32,16},{48,32},{64,48},{80,64},{96,80},{112,96},{4,112},{2... | collective-permute-start | bytes 98312 | tf_op jit(solution)/shard_map/ppermute | solution.py:31
  20.0 1.9 %collective-permute-start = (bf16[128,128]{1,0:T(8,128)(2,1)S(1)}, bf16[128,128]{1,0:T(8,128)(2,1)S(1)}, u32[]{:S(2)}, u32[]{:S(2)}) collective-permute-start(bf16[128,128]{1,0:T(8,128)(2,1)S(1)} %constant_dynamic-slice_fusion.refs_1_), channel_id=1, source_target_pairs={{116,0},{0,16},{16,32},{32,48},{48,64},{64,80},{80,96},{96,112},{1... | collective-permute-start | bytes 98312 | tf_op jit(solution)/shard_map/ppermute | solution.py:31
  22.7 3.2 %collective-permute-done.refs_0_ = bf16[128,128]{1,0:T(8,128)(2,1)S(1)} collective-permute-done((bf16[128,128]{1,0:T(8,128)(2,1)S(1)}, bf16[128,128]{1,0:T(8,128)(2,1)S(1)}, u32[]{:S(2)}, u32[]{:S(2)}) %collective-permute-start) | collective-permute-done | bytes 32800 | tf_op jit(solution)/shard_map/ppermute | solution.py:31
  26.6 3.4 %all-to-all-start = ((bf16[8,64,128]{2,1,0:T(8,128)(2,1)}), bf16[8,64,128]{2,1,0:T(8,128)(2,1)S(1)}, u32[]{:S(2)}, u32[]{:S(2)}) async-start(bf16[8,64,128]{2,1,0:T(8,128)(2,1)} %broadcast_in_dim.10), calls=%async_computation | async-start | bytes 262144 | tf_op jit(solution)/shard_map/all_to_all | solution.py:20
  30.0 5.0 %collective-permute-start.5 = (bf16[384,128]{1,0:T(8,128)(2,1)S(1)}, bf16[384,128]{1,0:T(8,128)(2,1)S(1)}, u32[]{:S(2)}, u32[]{:S(2)}) collective-permute-start(bf16[384,128]{1,0:T(8,128)(2,1)S(1)} %near_three.1.near_ref), channel_id=1, source_target_pairs={{84,0},{100,16},{116,32},{0,48},{16,64},{32,80},{48,96},{64,112},{... | collective-permute-start | bytes 294920 | tf_op jit(solution)/shard_map/ppermute | solution.py:31
  35.0 5.3 %collective-permute-start.4 = (bf16[384,128]{1,0:T(8,128)(2,1)S(1)}, bf16[384,128]{1,0:T(8,128)(2,1)S(1)}, u32[]{:S(2)}, u32[]{:S(2)}) collective-permute-start(bf16[384,128]{1,0:T(8,128)(2,1)S(1)} %near_three.1.near_ref), channel_id=1, source_target_pairs={{48,0},{64,16},{80,32},{96,48},{112,64},{4,80},{20,96},{36,112},{5... | collective-permute-start | bytes 294920 | tf_op jit(solution)/shard_map/ppermute | solution.py:31
  40.3 4.4 %collective-permute-done.5.behind_ref = bf16[384,128]{1,0:T(8,128)(2,1)S(1)} collective-permute-done((bf16[384,128]{1,0:T(8,128)(2,1)S(1)}, bf16[384,128]{1,0:T(8,128)(2,1)S(1)}, u32[]{:S(2)}, u32[]{:S(2)}) %collective-permute-start.5) | collective-permute-done | bytes 98336 | tf_op jit(solution)/shard_map/ppermute | solution.py:31
  46.1 1.1 convolution_convert_fusion
  48.2 4.2 %all-to-all-start.1 = ((bf16[4,592,128]{2,1,0:T(8,128)(2,1)}), bf16[4,592,128]{2,1,0:T(8,128)(2,1)S(1)}, u32[]{:S(2)}, u32[]{:S(2)}) async-start(bf16[4,592,128]{2,1,0:T(8,128)(2,1)} %broadcast_in_dim.12), calls=%async_computation.1 | async-start | bytes 1212416 | tf_op jit(solution)/shard_map/all_to_all | solution.py:20
  52.9 7.4 %collective-permute-start.3 = (bf16[16,4096]{1,0:T(8,128)(2,1)}, bf16[16,4096]{1,0:T(8,128)(2,1)}, u32[]{:S(2)}, u32[]{:S(2)}) collective-permute-start(bf16[16,4096]{1,0:T(8,128)(2,1)} %param.16), channel_id=1, source_target_pairs={{0,4},{4,0},{1,5},{5,1},{2,6},{6,2},{3,7},{7,3},{8,12},{12,8},{9,1... | collective-permute-start | bytes 393224 | tf_op jit(solution)/shard_map/ppermute | solution.py:24
  60.3 6.8 %collective-permute-start.2 = (bf16[4,592,128]{2,1,0:T(8,128)(2,1)S(1)}, bf16[4,592,128]{2,1,0:T(8,128)(2,1)S(1)}, u32[]{:S(2)}, u32[]{:S(2)}) collective-permute-start(bf16[4,592,128]{2,1,0:T(8,128)(2,1)S(1)} %all-to-all-done.1.own_ref), channel_id=1, source_target_pairs={{0,8},{8,0},{1,9},{9,1},{2,10},{10,2},{3,11},{11,3},{4,12},{12,4},... | collective-permute-start | bytes 1818632 | tf_op jit(solution)/shard_map/ppermute | solution.py:24
  67.1 2.2 %fusion.2.normed_ref = bf16[128,8192]{1,0:T(8,128)(2,1)S(1)} fusion(bf16[128,8192]{1,0:T(8,128)(2,1)} %hidden_hbm.1, f32[8192]{0:T(1024)S(1)} %copy-done.3, f32[128]{0:T(128)S(1)} %get-tuple-element.28), kind=kLoop, calls=%fused_computation.4 | loop fusion | flops 4194304 | bytes 4227584 | tf_op jit(solution)/shard_map/convert_element_type | solution.py:201
  70.0 1.4 left_factor.1
  71.4 9.3 %all-to-all-start.2 = ((f32[8,8,128]{2,1,0:T(8,128)}), f32[8,8,128]{2,1,0:T(8,128)S(1)}, u32[]{:S(2)}, u32[]{:S(2)}) async-start(f32[8,8,128]{2,1,0:T(8,128)} %bitcast.10), calls=%async_computation.2 | async-start | bytes 65536 | tf_op jit(solution)/shard_map/all_to_all | solution.py:213
  81.5 4.0 %all-to-all-done.2 = f32[8,8,128]{2,1,0:T(8,128)S(1)} async-done(((f32[8,8,128]{2,1,0:T(8,128)}), f32[8,8,128]{2,1,0:T(8,128)S(1)}, u32[]{:S(2)}, u32[]{:S(2)}) %all-to-all-start.2) | async-done | bytes 32800 | tf_op jit(solution)/shard_map/all_to_all | solution.py:213
  85.7 1.2 fusion.4
  87.9 16.5 %all-to-all-start.3 = ((f32[64,1,512]{2,1,0:T(1,128)}), f32[64,1,512]{2,1,0:T(1,128)S(1)}, u32[]{:S(2)}, u32[]{:S(2)}) async-start(f32[64,1,512]{2,1,0:T(1,128)} %reshape.107), calls=%async_computation.3 | async-start | bytes 262144 | tf_op jit(solution)/shard_map/all_to_all | solution.py:230
  104.4 14.8 %all-to-all-done.3 = f32[64,1,512]{2,1,0:T(1,128)S(1)} async-done(((f32[64,1,512]{2,1,0:T(1,128)}), f32[64,1,512]{2,1,0:T(1,128)S(1)}, u32[]{:S(2)}, u32[]{:S(2)}) %all-to-all-start.3) | async-done | bytes 131104 | tf_op jit(solution)/shard_map/all_to_all | solution.py:230
  121.5 7.3 %all-to-all-start.4 = ((bf16[64,8,128]{2,1,0:T(8,128)(2,1)}), bf16[64,8,128]{2,1,0:T(8,128)(2,1)S(1)}, u32[]{:S(2)}, u32[]{:S(2)}) async-start(bf16[64,8,128]{2,1,0:T(8,128)(2,1)} %broadcast_in_dim.13), calls=%async_computation.4 | async-start | bytes 262144 | tf_op jit(solution)/shard_map/all_to_all | solution.py:20
  129.9 2.2 %collective-permute-start.8 = (bf16[32,4096]{1,0:T(8,128)(2,1)S(1)}, bf16[32,4096]{1,0:T(8,128)(2,1)S(1)}, u32[]{:S(2)}, u32[]{:S(2)}) collective-permute-start(bf16[32,4096]{1,0:T(8,128)(2,1)S(1)} %pad_maximum_fusion.here_ref), channel_id=1, source_target_pairs={{3,0},{0,1},{1,2},{2,3},{7,4},{4,5},{5,6},{6,7},{11,8},{8,9},{9,10... | collective-permute-start | bytes 786440 | tf_op jit(solution)/shard_map/ppermute | solution.py:164
  132.1 3.9 %collective-permute-start.7 = (bf16[32,4096]{1,0:T(8,128)(2,1)S(1)}, bf16[32,4096]{1,0:T(8,128)(2,1)S(1)}, u32[]{:S(2)}, u32[]{:S(2)}) collective-permute-start(bf16[32,4096]{1,0:T(8,128)(2,1)S(1)} %pad_maximum_fusion.here_ref), channel_id=1, source_target_pairs={{2,0},{3,1},{0,2},{1,3},{6,4},{7,5},{4,6},{5,7},{10,8},{11,9},{8,1... | collective-permute-start | bytes 786440 | tf_op jit(solution)/shard_map/ppermute | solution.py:164
  135.9 2.8 %collective-permute-start.6 = (bf16[32,4096]{1,0:T(8,128)(2,1)S(1)}, bf16[32,4096]{1,0:T(8,128)(2,1)S(1)}, u32[]{:S(2)}, u32[]{:S(2)}) collective-permute-start(bf16[32,4096]{1,0:T(8,128)(2,1)S(1)} %pad_maximum_fusion.here_ref), channel_id=1, source_target_pairs={{1,0},{2,1},{3,2},{0,3},{5,4},{6,5},{7,6},{4,7},{9,8},{10,9},{11,1... | collective-permute-start | bytes 786440 | tf_op jit(solution)/shard_map/ppermute | solution.py:164
  140.1 9.6 %layer.1 = (bf16[128,512]{1,0:T(8,128)(2,1)}, bf16[128,8192]{1,0:T(8,128)(2,1)}) custom-call(s32[8]{0:T(128)} %and_select_fusion.place_ref, bf16[128,8192]{1,0:T(8,128)(2,1)} %hidden_hbm.1, f32[1,8192]{1,0:T(1,128)} %bitcast.41, f32[128,1]{1,0:T(8,128)} %copy.21.scale_ref, bf16[128,512]{1,0:T(8,128)(2,1)} %grad_ref.1, ...), custom_call_target="tpu_custom_call" | custom-call | tf_op jit(solution)/shard_map/layer/pallas_call | solution.py:241
  149.7 1.6 %scores.1 = f32[8,128]{1,0:T(8,128)} custom-call(s32[2]{0:T(128)S(1)} %pad_add_fusion.index_ref, bf16[64,8,128]{2,1,0:T(8,128)(2,1)S(1)} %all-to-all-done.4.docs_ref, bf16[32,4096]{1,0:T(8,128)(2,1)S(1)} %pad_maximum_fusion.here_ref, bf16[32,4096]{1,0:T(8,128)(2,1)S(1)} %collective-permute-done.6.one_ref, ...), custom_call_target="tpu_custom_call" | custom-call | tf_op jit(solution)/shard_map/scores/pallas_call | solution.py:151
  (52 shorter events, 12.6 us)
Async XLA Ops:
  7.2 0.9 copy-start
  7.2 45.2 %copy-start.1 = (bf16[128,8192]{1,0:T(8,128)(2,1)S(1)}, bf16[128,8192]{1,0:T(8,128)(2,1)}, u32[]{:S(2)}) copy-start(bf16[128,8192]{1,0:T(8,128)(2,1)} %hidden_hbm.1) | copy-start | bytes 6291460
  8.1 14.6 %collective-permute-start.1 = (bf16[128,128]{1,0:T(8,128)(2,1)S(1)}, bf16[128,128]{1,0:T(8,128)(2,1)S(1)}, u32[]{:S(2)}, u32[]{:S(2)}) collective-permute-start(bf16[128,128]{1,0:T(8,128)(2,1)S(1)} %constant_dynamic-slice_fusion.refs_1_), channel_id=1, source_target_pairs={{16,0},{32,16},{48,32},{64,48},{80,64},{96,80},{112,96},{4,112},{2... | collective-permute-start | bytes 98312 | tf_op jit(solution)/shard_map/ppermute | solution.py:31
  20.0 5.9 %collective-permute-start = (bf16[128,128]{1,0:T(8,128)(2,1)S(1)}, bf16[128,128]{1,0:T(8,128)(2,1)S(1)}, u32[]{:S(2)}, u32[]{:S(2)}) collective-permute-start(bf16[128,128]{1,0:T(8,128)(2,1)S(1)} %constant_dynamic-slice_fusion.refs_1_), channel_id=1, source_target_pairs={{116,0},{0,16},{16,32},{32,48},{48,64},{64,80},{80,96},{96,112},{1... | collective-permute-start | bytes 98312 | tf_op jit(solution)/shard_map/ppermute | solution.py:31
  26.6 18.2 %all-to-all-start = ((bf16[8,64,128]{2,1,0:T(8,128)(2,1)}), bf16[8,64,128]{2,1,0:T(8,128)(2,1)S(1)}, u32[]{:S(2)}, u32[]{:S(2)}) async-start(bf16[8,64,128]{2,1,0:T(8,128)(2,1)} %broadcast_in_dim.10), calls=%async_computation | async-start | bytes 262144 | tf_op jit(solution)/shard_map/all_to_all | solution.py:20
  30.0 110.2 %all-gather.2.cloned.1.call-start = ((), (), s32[]{:S(2)}) async-start(), calls=%async_computation.5 | async-start | bytes 8650752 | tf_op jit(solution)/shard_map/all_gather | solution.py:209
  30.0 14.7 %collective-permute-start.5 = (bf16[384,128]{1,0:T(8,128)(2,1)S(1)}, bf16[384,128]{1,0:T(8,128)(2,1)S(1)}, u32[]{:S(2)}, u32[]{:S(2)}) collective-permute-start(bf16[384,128]{1,0:T(8,128)(2,1)S(1)} %near_three.1.near_ref), channel_id=1, source_target_pairs={{84,0},{100,16},{116,32},{0,48},{16,64},{32,80},{48,96},{64,112},{... | collective-permute-start | bytes 294920 | tf_op jit(solution)/shard_map/ppermute | solution.py:31
  35.0 9.7 %collective-permute-start.4 = (bf16[384,128]{1,0:T(8,128)(2,1)S(1)}, bf16[384,128]{1,0:T(8,128)(2,1)S(1)}, u32[]{:S(2)}, u32[]{:S(2)}) collective-permute-start(bf16[384,128]{1,0:T(8,128)(2,1)S(1)} %near_three.1.near_ref), channel_id=1, source_target_pairs={{48,0},{64,16},{80,32},{96,48},{112,64},{4,80},{20,96},{36,112},{5... | collective-permute-start | bytes 294920 | tf_op jit(solution)/shard_map/ppermute | solution.py:31
  47.3 19.8 %copy-start.3 = (f32[8192]{0:T(1024)S(1)}, f32[8192]{0:T(1024)}, u32[]{:S(2)}) copy-start(f32[8192]{0:T(1024)} %param.10) | copy-start | bytes 98308
  48.2 12.1 %all-to-all-start.1 = ((bf16[4,592,128]{2,1,0:T(8,128)(2,1)}), bf16[4,592,128]{2,1,0:T(8,128)(2,1)S(1)}, u32[]{:S(2)}, u32[]{:S(2)}) async-start(bf16[4,592,128]{2,1,0:T(8,128)(2,1)} %broadcast_in_dim.12), calls=%async_computation.1 | async-start | bytes 1212416 | tf_op jit(solution)/shard_map/all_to_all | solution.py:20
  52.9 16.4 %collective-permute-start.3 = (bf16[16,4096]{1,0:T(8,128)(2,1)}, bf16[16,4096]{1,0:T(8,128)(2,1)}, u32[]{:S(2)}, u32[]{:S(2)}) collective-permute-start(bf16[16,4096]{1,0:T(8,128)(2,1)} %param.16), channel_id=1, source_target_pairs={{0,4},{4,0},{1,5},{5,1},{2,6},{6,2},{3,7},{7,3},{8,12},{12,8},{9,1... | collective-permute-start | bytes 393224 | tf_op jit(solution)/shard_map/ppermute | solution.py:24
  60.3 9.0 %collective-permute-start.2 = (bf16[4,592,128]{2,1,0:T(8,128)(2,1)S(1)}, bf16[4,592,128]{2,1,0:T(8,128)(2,1)S(1)}, u32[]{:S(2)}, u32[]{:S(2)}) collective-permute-start(bf16[4,592,128]{2,1,0:T(8,128)(2,1)S(1)} %all-to-all-done.1.own_ref), channel_id=1, source_target_pairs={{0,8},{8,0},{1,9},{9,1},{2,10},{10,2},{3,11},{11,3},{4,12},{12,4},... | collective-permute-start | bytes 1818632 | tf_op jit(solution)/shard_map/ppermute | solution.py:24
  71.4 14.3 %copy-start.2 = (bf16[4,2,80,128]{3,2,1,0:T(8,128)(2,1)S(1)}, bf16[4,2,80,128]{3,2,1,0:T(8,128)(2,1)}, u32[]{:S(2)}) copy-start(bf16[4,2,80,128]{3,2,1,0:T(8,128)(2,1)} %copy.18) | copy-start | bytes 491524
  71.4 14.0 %all-to-all-start.2 = ((f32[8,8,128]{2,1,0:T(8,128)}), f32[8,8,128]{2,1,0:T(8,128)S(1)}, u32[]{:S(2)}, u32[]{:S(2)}) async-start(f32[8,8,128]{2,1,0:T(8,128)} %bitcast.10), calls=%async_computation.2 | async-start | bytes 65536 | tf_op jit(solution)/shard_map/all_to_all | solution.py:213
  85.7 53.9 %copy-start.4 = (s32[8]{0:T(128)S(1)}, s32[8]{0:T(128)}, u32[]{:S(2)}) copy-start(s32[8]{0:T(128)} %constant.46.clone) | copy-start | bytes 100
  87.9 31.2 %all-to-all-start.3 = ((f32[64,1,512]{2,1,0:T(1,128)}), f32[64,1,512]{2,1,0:T(1,128)S(1)}, u32[]{:S(2)}, u32[]{:S(2)}) async-start(f32[64,1,512]{2,1,0:T(1,128)} %reshape.107), calls=%async_computation.3 | async-start | bytes 262144 | tf_op jit(solution)/shard_map/all_to_all | solution.py:230
  121.5 28.1 %all-to-all-start.4 = ((bf16[64,8,128]{2,1,0:T(8,128)(2,1)}), bf16[64,8,128]{2,1,0:T(8,128)(2,1)S(1)}, u32[]{:S(2)}, u32[]{:S(2)}) async-start(bf16[64,8,128]{2,1,0:T(8,128)(2,1)} %broadcast_in_dim.13), calls=%async_computation.4 | async-start | bytes 262144 | tf_op jit(solution)/shard_map/all_to_all | solution.py:20
  129.9 19.8 %collective-permute-start.8 = (bf16[32,4096]{1,0:T(8,128)(2,1)S(1)}, bf16[32,4096]{1,0:T(8,128)(2,1)S(1)}, u32[]{:S(2)}, u32[]{:S(2)}) collective-permute-start(bf16[32,4096]{1,0:T(8,128)(2,1)S(1)} %pad_maximum_fusion.here_ref), channel_id=1, source_target_pairs={{3,0},{0,1},{1,2},{2,3},{7,4},{4,5},{5,6},{6,7},{11,8},{8,9},{9,10... | collective-permute-start | bytes 786440 | tf_op jit(solution)/shard_map/ppermute | solution.py:164
  132.1 17.6 %collective-permute-start.7 = (bf16[32,4096]{1,0:T(8,128)(2,1)S(1)}, bf16[32,4096]{1,0:T(8,128)(2,1)S(1)}, u32[]{:S(2)}, u32[]{:S(2)}) collective-permute-start(bf16[32,4096]{1,0:T(8,128)(2,1)S(1)} %pad_maximum_fusion.here_ref), channel_id=1, source_target_pairs={{2,0},{3,1},{0,2},{1,3},{6,4},{7,5},{4,6},{5,7},{10,8},{11,9},{8,1... | collective-permute-start | bytes 786440 | tf_op jit(solution)/shard_map/ppermute | solution.py:164
  135.9 13.8 %collective-permute-start.6 = (bf16[32,4096]{1,0:T(8,128)(2,1)S(1)}, bf16[32,4096]{1,0:T(8,128)(2,1)S(1)}, u32[]{:S(2)}, u32[]{:S(2)}) collective-permute-start(bf16[32,4096]{1,0:T(8,128)(2,1)S(1)} %pad_maximum_fusion.here_ref), channel_id=1, source_target_pairs={{1,0},{2,1},{3,2},{0,3},{5,4},{6,5},{7,6},{4,7},{9,8},{10,9},{11,1... | collective-permute-start | bytes 786440 | tf_op jit(solution)/shard_map/ppermute | solution.py:164
Sparse Core Ops, SparseCore 0:
  45.6 72.5 all-gather.1

commit v8 on v7

--- a/solution.py
+++ b/solution.py
@@ -178,23 +178,22 @@
     core_row = core.astype(jnp.int32).reshape(1)
     on_first = core == 0
 
-    quarter = lax.dynamic_slice_in_dim(value_weight, lax.axis_index("x") * BLOCK, BLOCK, 1)
-    ahead, behind = from_z(quarter, 1), from_z(quarter, -1)
-    near = call(joined_kernel, struct((3 * BLOCK, BLOCK), jnp.bfloat16), 0, "near_three")(
-        behind, quarter, ahead
-    )
-    far_ahead, far_behind = from_z(near, 3), from_z(near, -3)
-
     factor = input_proj.T.reshape(4, 8, 2, BLOCK).transpose(0, 2, 1, 3).reshape(rank, BLOCK)
     right_t = lax.dot_general(
         output_proj, value_grad, (((0,), (1,)), ((), ())), preferred_element_type=jnp.float32
     ).astype(jnp.bfloat16)
     ids_rows = jnp.broadcast_to(doc_ids.astype(jnp.bfloat16)[None], (16, rows))
-    factor_z = spread_to_all(after(factor, near), "zl").reshape(-1, BLOCK)
+    factor_z = spread_to_all(factor, "zl").reshape(-1, BLOCK)
     packed = spread_to_all(jnp.concatenate([factor_z, right_t, ids_rows], 0), "y")
     packed_other = swapped(packed, "core")
-    q_other = swapped(after(queries, factor_z), "zh")
-    packed_other, q_other = lax.optimization_barrier((packed_other, q_other))
+
+    quarter = lax.dynamic_slice_in_dim(value_weight, lax.axis_index("x") * BLOCK, BLOCK, 1)
+    ahead, behind = from_z(quarter, 1), from_z(quarter, -1)
+    near = call(joined_kernel, struct((3 * BLOCK, BLOCK), jnp.bfloat16), 0, "near_three")(
+        behind, quarter, ahead
+    )
+    near = after(near, factor_z)
+    far_ahead, far_behind = from_z(near, 3), from_z(near, -3)
 
     wide_in = hidden_in.astype(jnp.float32)
     inv_rms = lax.rsqrt(jnp.mean(wide_in * wide_in, axis=1, keepdims=True) + EPSILON)
@@ -204,11 +203,12 @@
     )
 
     w_z = call(along_z_kernel, struct((8 * BLOCK, BLOCK), jnp.bfloat16), 0, "along_z")(
-        near, *after((far_ahead, far_behind), factor_z)
+        near, *after((far_ahead, far_behind), left_t)
     )
     w_all = lax.all_gather(w_z, ("y", "core", "x"), axis=0, tiled=True)
     z_place = (lax.axis_index("zl") + jnp.array(Z_STEPS, jnp.int32)) % 8
 
+    q_other = swapped(after(queries, left_t), "zh")
 
     left_all = lax.all_to_all(
         left_t.reshape(8, rank // 8, rows), ("y", "core"), 0, 0, tiled=True
@@ -234,6 +234,12 @@
     q_turns = [from_x(q_here, step) for step in (1, 2, 3)]
     own_docs = jnp.sum(doc_parts, 0).astype(jnp.bfloat16)
     doc_low = spread_to_all(jnp.concatenate([own_docs, own_docs], 1), DP)
+
+    score_index = jnp.stack([lax.axis_index("zh"), lax.axis_index("x")]).astype(jnp.int32)
+    scores = call(score_kernel, struct((8, 8 * queries.shape[0]), jnp.float32), 1, "scores")(
+        score_index, doc_low, q_here, *q_turns
+    )
+    w_all = after(w_all, scores)
 
     vmem = pl.BlockSpec(memory_space=pltpu.VMEM)
     hbm = pl.BlockSpec(memory_space=pltpu.HBM)
@@ -255,11 +261,6 @@
         z_place.astype(jnp.int32), hidden_in, norm_gain.reshape(1, width), inv_rms,
         value_grad, w_all,
     )
-    doc_low, values_out = lax.optimization_barrier((doc_low, values_out))
-    score_index = jnp.stack([lax.axis_index("zh"), lax.axis_index("x")]).astype(jnp.int32)
-    scores = call(score_kernel, struct((8, 8 * queries.shape[0]), jnp.float32), 1, "scores")(
-        score_index, doc_low, q_here, *q_turns
-    )
     return (values_out, hidden_grad, scores)
 
 

time: 159 us -> 151 us (0.950)
  waiting for transfers between devices: 26.4 us -> 19.8 us
  other arithmetic: 7.05 us -> 5.43 us
    all_to_all x3, starting transfers between devices: 14.9 us -> 32.8 us  [spread_to_all(): return lax.all_to_all(copies, axes, 0, 0, tiled=True)]
    all_to_all x1, waiting for transfers between devices: 14.8 us -> 3.11 us  [shards(): lax.all_to_all(doc_term.reshape(64, 8, rank), ('zl', 'zh', 'x'), 0, 0, ti...]
    ppermute x3, waiting for transfers between devices: 0.01 us -> 11.3 us  [from_x(): return lax.ppermute(value, 'x', [((x + step) % 4, x) for x in range(4)])]
    ppermute x4, waiting for transfers between devices: 7.61 us -> 0.01 us  [from_z(): lax.ppermute(value, ('zl', 'zh'), [(place((z + step) % 16), place(z)) for...]
    all_to_all x1, starting transfers between devices: 16.5 us -> 9.08 us  [shards(): lax.all_to_all(doc_term.reshape(64, 8, rank), ('zl', 'zh', 'x'), 0, 0, ti...]
    ppermute x4, starting transfers between devices: 24.2 us -> 17.2 us  [from_z(): lax.ppermute(value, ('zl', 'zh'), [(place((z + step) % 16), place(z)) for...]
    all_to_all x1, starting transfers between devices: 9.3 us -> 6.02 us  [shards(): lax.all_to_all(left_t.reshape(8, rank // 8, rows), ('y', 'core'), 0, 0, t...]
    ppermute x2, starting transfers between devices: 14.2 us -> 16.5 us  [swapped(): return lax.ppermute(value, axis, [(0, 1), (1, 0)])]
  transfers between devices with their start and end apart: 15 -> 15, of which waited for: 4 -> 6; matrix products, arithmetic and copies ran while one was open for 9% -> 8% of each run, Pallas kernels for 7% -> 2%
where the time goes in v8:
time: 151 us; the launch traced here: 150 us
  starting transfers between devices  88.8 us (59%)
  waiting for transfers between devices  19.8 us (13%)
  between operations  14.4 us (10%)
  Pallas kernels  13.7 us (9%)
  local copies, waits for them, and re-layouts  6.11 us (4%)
  other arithmetic  5.43 us (4%)
  matrix products  2.28 us (2%)
    all_to_all x3, starting transfers between devices, spread_to_all(): return lax.all_to_all(copies, axes, 0, 0, tiled=True)  32.8 us
    ppermute x4, starting transfers between devices, from_z(): lax.ppermute(value, ('zl', 'zh'), [(place((z + step) % 16), place(z)) for...  17.2 us
    ppermute x2, starting transfers between devices, swapped(): return lax.ppermute(value, axis, [(0, 1), (1, 0)])  16.5 us
    ppermute x3, waiting for transfers between devices, from_x(): return lax.ppermute(value, 'x', [((x + step) % 4, x) for x in range(4)])  11.3 us
    pallas_call x1, Pallas kernels, shards(): pl.pallas_call(layer_kernel, out_shape=(struct((rows, kv), jnp.bfloat16),...  9.56 us
    all_to_all x1, starting transfers between devices, shards(): lax.all_to_all(doc_term.reshape(64, 8, rank), ('zl', 'zh', 'x'), 0, 0, ti...  9.08 us
    ppermute x3, starting transfers between devices, from_x(): return lax.ppermute(value, 'x', [((x + step) % 4, x) for x in range(4)])  7.2 us
    all_to_all x1, starting transfers between devices, shards(): lax.all_to_all(left_t.reshape(8, rank // 8, rows), ('y', 'core'), 0, 0, t...  6.02 us
  transfers between devices with their start and end apart: 15, of which 6 were waited for; matrix products, arithmetic and copies ran while one was open for 8% of the time, Pallas kernels for 2%

profile of v8, /device:TPU:1, one launch (start us, length us, event | category | flops | bytes accessed | tf_op | source)
XLA Modules:
  0.0 150.5 jit_solution(15490799506655607508)
XLA Ops:
  8.7 13.1 %all-to-all-start = ((bf16[8,64,128]{2,1,0:T(8,128)(2,1)}), bf16[8,64,128]{2,1,0:T(8,128)(2,1)S(1)}, u32[]{:S(2)}, u32[]{:S(2)}) async-start(bf16[8,64,128]{2,1,0:T(8,128)(2,1)} %broadcast_in_dim.11), calls=%async_computation | async-start | bytes 262144 | tf_op jit(solution)/shard_map/all_to_all | solution.py:20
  21.8 3.4 %collective-permute-start = (bf16[128,128]{1,0:T(8,128)(2,1)S(1)}, bf16[128,128]{1,0:T(8,128)(2,1)S(1)}, u32[]{:S(2)}, u32[]{:S(2)}) collective-permute-start(bf16[128,128]{1,0:T(8,128)(2,1)S(1)} %constant_dynamic-slice_fusion.refs_1_), channel_id=1, source_target_pairs={{116,0},{0,16},{16,32},{32,48},{48,64},{64,80},{80,96},{96,112},{1... | collective-permute-start | bytes 98312 | tf_op jit(solution)/shard_map/ppermute | solution.py:31
  25.2 6.8 %collective-permute-start.1 = (bf16[128,128]{1,0:T(8,128)(2,1)S(1)}, bf16[128,128]{1,0:T(8,128)(2,1)S(1)}, u32[]{:S(2)}, u32[]{:S(2)}) collective-permute-start(bf16[128,128]{1,0:T(8,128)(2,1)S(1)} %constant_dynamic-slice_fusion.refs_1_), channel_id=1, source_target_pairs={{16,0},{32,16},{48,32},{64,48},{80,64},{96,80},{112,96},{4,112},{2... | collective-permute-start | bytes 98312 | tf_op jit(solution)/shard_map/ppermute | solution.py:31
  34.7 4.2 %all-to-all-start.1 = ((bf16[4,592,128]{2,1,0:T(8,128)(2,1)}), bf16[4,592,128]{2,1,0:T(8,128)(2,1)S(1)}, u32[]{:S(2)}, u32[]{:S(2)}) async-start(bf16[4,592,128]{2,1,0:T(8,128)(2,1)} %broadcast_in_dim.13), calls=%async_computation.1 | async-start | bytes 1212416 | tf_op jit(solution)/shard_map/all_to_all | solution.py:20
  39.4 3.4 %collective-permute-start.2 = (bf16[384,128]{1,0:T(8,128)(2,1)S(1)}, bf16[384,128]{1,0:T(8,128)(2,1)}, u32[]{:S(2)}, u32[]{:S(2)}) collective-permute-start(bf16[384,128]{1,0:T(8,128)(2,1)S(1)} %near_three.1.near_ref), channel_id=1, source_target_pairs={{48,0},{64,16},{80,32},{96,48},{112,64},{4,80},{20,96},{36,112},{5... | collective-permute-start | bytes 294920 | tf_op jit(solution)/shard_map/ppermute | solution.py:31
  42.8 3.7 %collective-permute-start.3 = (bf16[384,128]{1,0:T(8,128)(2,1)S(1)}, bf16[384,128]{1,0:T(8,128)(2,1)}, u32[]{:S(2)}, u32[]{:S(2)}) collective-permute-start(bf16[384,128]{1,0:T(8,128)(2,1)S(1)} %near_three.1.near_ref), channel_id=1, source_target_pairs={{84,0},{100,16},{116,32},{0,48},{16,64},{32,80},{48,96},{64,112},{... | collective-permute-start | bytes 294920 | tf_op jit(solution)/shard_map/ppermute | solution.py:31
  47.2 4.9 %collective-permute-start.4 = (bf16[4,592,128]{2,1,0:T(8,128)(2,1)S(1)}, bf16[4,592,128]{2,1,0:T(8,128)(2,1)S(1)}, u32[]{:S(2)}, u32[]{:S(2)}) collective-permute-start(bf16[4,592,128]{2,1,0:T(8,128)(2,1)S(1)} %all-to-all-done.1.own_ref), channel_id=1, source_target_pairs={{0,8},{8,0},{1,9},{9,1},{2,10},{10,2},{3,11},{11,3},{4,12},{12,4},... | collective-permute-start | bytes 1818632 | tf_op jit(solution)/shard_map/ppermute | solution.py:24
  52.1 2.2 %fusion.2.normed_ref = bf16[128,8192]{1,0:T(8,128)(2,1)S(1)} fusion(bf16[128,8192]{1,0:T(8,128)(2,1)} %hidden_hbm.1, f32[8192]{0:T(1024)} %param.10, f32[128]{0:T(128)S(1)} %get-tuple-element.21), kind=kLoop, calls=%fused_computation.4 | loop fusion | flops 4194304 | bytes 4227584 | tf_op jit(solution)/shard_map/convert_element_type | solution.py:200
  55.7 1.7 %along_z.1 = bf16[1024,128]{1,0:T(8,128)(2,1)} custom-call(bf16[384,128]{1,0:T(8,128)(2,1)S(1)} %near_three.1.near_ref, bf16[384,128]{1,0:T(8,128)(2,1)} %collective-permute-done.2.ahead_ref, bf16[384,128]{1,0:T(8,128)(2,1)} %collective-permute-done.3.behind_ref), custom_call_target="tpu_custom_call" | custom-call | tf_op jit(solution)/shard_map/along_z/pallas_call | solution.py:151
  57.5 6.0 %all-to-all-start.2 = ((f32[8,8,128]{2,1,0:T(8,128)}), f32[8,8,128]{2,1,0:T(8,128)S(1)}, u32[]{:S(2)}, u32[]{:S(2)}) async-start(f32[8,8,128]{2,1,0:T(8,128)} %bitcast.36), calls=%async_computation.2 | async-start | bytes 65536 | tf_op jit(solution)/shard_map/all_to_all | solution.py:213
  63.6 4.7 %all-to-all-done.2 = f32[8,8,128]{2,1,0:T(8,128)S(1)} async-done(((f32[8,8,128]{2,1,0:T(8,128)}), f32[8,8,128]{2,1,0:T(8,128)S(1)}, u32[]{:S(2)}, u32[]{:S(2)}) %all-to-all-start.2) | async-done | bytes 32800 | tf_op jit(solution)/shard_map/all_to_all | solution.py:213
  68.5 1.2 fusion.4
  70.7 9.1 %all-to-all-start.3 = ((f32[64,1,512]{2,1,0:T(1,128)}), f32[64,1,512]{2,1,0:T(1,128)S(1)}, u32[]{:S(2)}, u32[]{:S(2)}) async-start(f32[64,1,512]{2,1,0:T(1,128)} %reshape.106), calls=%async_computation.3 | async-start | bytes 262144 | tf_op jit(solution)/shard_map/all_to_all | solution.py:230
  79.8 11.6 %collective-permute-start.5 = (bf16[16,4096]{1,0:T(8,128)(2,1)S(1)}, bf16[16,4096]{1,0:T(8,128)(2,1)S(1)}, u32[]{:S(2)}, u32[]{:S(2)}) collective-permute-start(bf16[16,4096]{1,0:T(8,128)(2,1)S(1)} %copy-done.3), channel_id=1, source_target_pairs={{0,4},{4,0},{1,5},{5,1},{2,6},{6,2},{3,7},{7,3},{8,12},{12,8},{9,1... | collective-permute-start | bytes 393224 | tf_op jit(solution)/shard_map/ppermute | solution.py:24
  91.4 3.1 %all-to-all-done.3 = f32[64,1,512]{2,1,0:T(1,128)S(1)} async-done(((f32[64,1,512]{2,1,0:T(1,128)}), f32[64,1,512]{2,1,0:T(1,128)S(1)}, u32[]{:S(2)}, u32[]{:S(2)}) %all-to-all-start.3) | async-done | bytes 131104 | tf_op jit(solution)/shard_map/all_to_all | solution.py:230
  96.9 15.5 %all-to-all-start.4 = ((bf16[64,8,128]{2,1,0:T(8,128)(2,1)}), bf16[64,8,128]{2,1,0:T(8,128)(2,1)S(1)}, u32[]{:S(2)}, u32[]{:S(2)}) async-start(bf16[64,8,128]{2,1,0:T(8,128)(2,1)} %broadcast_in_dim.14), calls=%async_computation.4 | async-start | bytes 262144 | tf_op jit(solution)/shard_map/all_to_all | solution.py:20
  112.5 1.9 %collective-permute-start.6 = (bf16[32,4096]{1,0:T(8,128)(2,1)S(1)}, bf16[32,4096]{1,0:T(8,128)(2,1)S(1)}, u32[]{:S(2)}, u32[]{:S(2)}) collective-permute-start(bf16[32,4096]{1,0:T(8,128)(2,1)S(1)} %pad_maximum_fusion.here_ref), channel_id=1, source_target_pairs={{1,0},{2,1},{3,2},{0,3},{5,4},{6,5},{7,6},{4,7},{9,8},{10,9},{11,1... | collective-permute-start | bytes 786440 | tf_op jit(solution)/shard_map/ppermute | solution.py:164
  114.4 2.5 %collective-permute-start.7 = (bf16[32,4096]{1,0:T(8,128)(2,1)S(1)}, bf16[32,4096]{1,0:T(8,128)(2,1)S(1)}, u32[]{:S(2)}, u32[]{:S(2)}) collective-permute-start(bf16[32,4096]{1,0:T(8,128)(2,1)S(1)} %pad_maximum_fusion.here_ref), channel_id=1, source_target_pairs={{2,0},{3,1},{0,2},{1,3},{6,4},{7,5},{4,6},{5,7},{10,8},{11,9},{8,1... | collective-permute-start | bytes 786440 | tf_op jit(solution)/shard_map/ppermute | solution.py:164
  117.0 2.8 %collective-permute-start.8 = (bf16[32,4096]{1,0:T(8,128)(2,1)S(1)}, bf16[32,4096]{1,0:T(8,128)(2,1)S(1)}, u32[]{:S(2)}, u32[]{:S(2)}) collective-permute-start(bf16[32,4096]{1,0:T(8,128)(2,1)S(1)} %pad_maximum_fusion.here_ref), channel_id=1, source_target_pairs={{3,0},{0,1},{1,2},{2,3},{7,4},{4,5},{5,6},{6,7},{11,8},{8,9},{9,10... | collective-permute-start | bytes 786440 | tf_op jit(solution)/shard_map/ppermute | solution.py:164
  121.1 3.7 %collective-permute-done.6.one_ref = bf16[32,4096]{1,0:T(8,128)(2,1)S(1)} collective-permute-done((bf16[32,4096]{1,0:T(8,128)(2,1)S(1)}, bf16[32,4096]{1,0:T(8,128)(2,1)S(1)}, u32[]{:S(2)}, u32[]{:S(2)}) %collective-permute-start.6) | collective-permute-done | bytes 262176 | tf_op jit(solution)/shard_map/ppermute | solution.py:164
  124.8 1.6 %collective-permute-done.7.two_ref = bf16[32,4096]{1,0:T(8,128)(2,1)S(1)} collective-permute-done((bf16[32,4096]{1,0:T(8,128)(2,1)S(1)}, bf16[32,4096]{1,0:T(8,128)(2,1)S(1)}, u32[]{:S(2)}, u32[]{:S(2)}) %collective-permute-start.7) | collective-permute-done | bytes 262176 | tf_op jit(solution)/shard_map/ppermute | solution.py:164
  126.4 6.0 %collective-permute-done.8.three_ref = bf16[32,4096]{1,0:T(8,128)(2,1)S(1)} collective-permute-done((bf16[32,4096]{1,0:T(8,128)(2,1)S(1)}, bf16[32,4096]{1,0:T(8,128)(2,1)S(1)}, u32[]{:S(2)}, u32[]{:S(2)}) %collective-permute-start.8) | collective-permute-done | bytes 262176 | tf_op jit(solution)/shard_map/ppermute | solution.py:164
  132.4 1.6 %scores.1 = f32[8,128]{1,0:T(8,128)} custom-call(s32[2]{0:T(128)S(1)} %pad_add_fusion.index_ref, bf16[64,8,128]{2,1,0:T(8,128)(2,1)S(1)} %all-to-all-done.4.docs_ref, bf16[32,4096]{1,0:T(8,128)(2,1)S(1)} %pad_maximum_fusion.here_ref, bf16[32,4096]{1,0:T(8,128)(2,1)S(1)} %collective-permute-done.6.one_ref, ...), custom_call_target="tpu_custom_call" | custom-call | tf_op jit(solution)/shard_map/scores/pallas_call | solution.py:151
  134.0 9.6 %layer.1 = (bf16[128,512]{1,0:T(8,128)(2,1)}, bf16[128,8192]{1,0:T(8,128)(2,1)}) custom-call(s32[8]{0:T(128)} %and_select_fusion.place_ref, bf16[128,8192]{1,0:T(8,128)(2,1)} %hidden_hbm.1, f32[1,8192]{1,0:T(1,128)} %bitcast.42, f32[128,1]{1,0:T(8,128)} %copy.21.scale_ref, bf16[128,512]{1,0:T(8,128)(2,1)} %grad_ref.1, ...), custom_call_target="tpu_custom_call" | custom-call | tf_op jit(solution)/shard_map/layer/pallas_call | solution.py:247
  (52 shorter events, 12.0 us)
Async XLA Ops:
  7.2 14.7 %copy-start = (bf16[128,512]{1,0:T(8,128)(2,1)S(1)}, bf16[128,512]{1,0:T(8,128)(2,1)}, u32[]{:S(2)}) copy-start(bf16[128,512]{1,0:T(8,128)(2,1)} %param.11) | copy-start | bytes 393220
  7.2 31.7 %copy-start.2 = (bf16[128,8192]{1,0:T(8,128)(2,1)S(1)}, bf16[128,8192]{1,0:T(8,128)(2,1)}, u32[]{:S(2)}) copy-start(bf16[128,8192]{1,0:T(8,128)(2,1)} %hidden_hbm.1) | copy-start | bytes 6291460
  8.7 25.0 %all-to-all-start = ((bf16[8,64,128]{2,1,0:T(8,128)(2,1)}), bf16[8,64,128]{2,1,0:T(8,128)(2,1)S(1)}, u32[]{:S(2)}, u32[]{:S(2)}) async-start(bf16[8,64,128]{2,1,0:T(8,128)(2,1)} %broadcast_in_dim.11), calls=%async_computation | async-start | bytes 262144 | tf_op jit(solution)/shard_map/all_to_all | solution.py:20
  21.8 17.5 %collective-permute-start = (bf16[128,128]{1,0:T(8,128)(2,1)S(1)}, bf16[128,128]{1,0:T(8,128)(2,1)S(1)}, u32[]{:S(2)}, u32[]{:S(2)}) collective-permute-start(bf16[128,128]{1,0:T(8,128)(2,1)S(1)} %constant_dynamic-slice_fusion.refs_1_), channel_id=1, source_target_pairs={{116,0},{0,16},{16,32},{32,48},{48,64},{64,80},{80,96},{96,112},{1... | collective-permute-start | bytes 98312 | tf_op jit(solution)/shard_map/ppermute | solution.py:31
  25.2 14.2 %collective-permute-start.1 = (bf16[128,128]{1,0:T(8,128)(2,1)S(1)}, bf16[128,128]{1,0:T(8,128)(2,1)S(1)}, u32[]{:S(2)}, u32[]{:S(2)}) collective-permute-start(bf16[128,128]{1,0:T(8,128)(2,1)S(1)} %constant_dynamic-slice_fusion.refs_1_), channel_id=1, source_target_pairs={{16,0},{32,16},{48,32},{64,48},{80,64},{96,80},{112,96},{4,112},{2... | collective-permute-start | bytes 98312 | tf_op jit(solution)/shard_map/ppermute | solution.py:31
  34.7 12.5 %all-to-all-start.1 = ((bf16[4,592,128]{2,1,0:T(8,128)(2,1)}), bf16[4,592,128]{2,1,0:T(8,128)(2,1)S(1)}, u32[]{:S(2)}, u32[]{:S(2)}) async-start(bf16[4,592,128]{2,1,0:T(8,128)(2,1)} %broadcast_in_dim.13), calls=%async_computation.1 | async-start | bytes 1212416 | tf_op jit(solution)/shard_map/all_to_all | solution.py:20
  38.9 95.2 %all-gather.2.cloned.1.call-start = ((), (), s32[]{:S(2)}) async-start(), calls=%async_computation.5 | async-start | bytes 8650752 | tf_op jit(solution)/shard_map/all_gather | solution.py:208
  39.4 16.3 %collective-permute-start.2 = (bf16[384,128]{1,0:T(8,128)(2,1)S(1)}, bf16[384,128]{1,0:T(8,128)(2,1)}, u32[]{:S(2)}, u32[]{:S(2)}) collective-permute-start(bf16[384,128]{1,0:T(8,128)(2,1)S(1)} %near_three.1.near_ref), channel_id=1, source_target_pairs={{48,0},{64,16},{80,32},{96,48},{112,64},{4,80},{20,96},{36,112},{5... | collective-permute-start | bytes 294920 | tf_op jit(solution)/shard_map/ppermute | solution.py:31
  42.8 12.9 %collective-permute-start.3 = (bf16[384,128]{1,0:T(8,128)(2,1)S(1)}, bf16[384,128]{1,0:T(8,128)(2,1)}, u32[]{:S(2)}, u32[]{:S(2)}) collective-permute-start(bf16[384,128]{1,0:T(8,128)(2,1)S(1)} %near_three.1.near_ref), channel_id=1, source_target_pairs={{84,0},{100,16},{116,32},{0,48},{16,64},{32,80},{48,96},{64,112},{... | collective-permute-start | bytes 294920 | tf_op jit(solution)/shard_map/ppermute | solution.py:31
  47.2 7.1 %collective-permute-start.4 = (bf16[4,592,128]{2,1,0:T(8,128)(2,1)S(1)}, bf16[4,592,128]{2,1,0:T(8,128)(2,1)S(1)}, u32[]{:S(2)}, u32[]{:S(2)}) collective-permute-start(bf16[4,592,128]{2,1,0:T(8,128)(2,1)S(1)} %all-to-all-done.1.own_ref), channel_id=1, source_target_pairs={{0,8},{8,0},{1,9},{9,1},{2,10},{10,2},{3,11},{11,3},{4,12},{12,4},... | collective-permute-start | bytes 1818632 | tf_op jit(solution)/shard_map/ppermute | solution.py:24
  55.1 0.6 copy-start.1
  57.5 10.7 %all-to-all-start.2 = ((f32[8,8,128]{2,1,0:T(8,128)}), f32[8,8,128]{2,1,0:T(8,128)S(1)}, u32[]{:S(2)}, u32[]{:S(2)}) async-start(f32[8,8,128]{2,1,0:T(8,128)} %bitcast.36), calls=%async_computation.2 | async-start | bytes 65536 | tf_op jit(solution)/shard_map/all_to_all | solution.py:213
  68.5 11.3 %copy-start.3 = (bf16[16,4096]{1,0:T(8,128)(2,1)S(1)}, bf16[16,4096]{1,0:T(8,128)(2,1)}, u32[]{:S(2)}) copy-start(bf16[16,4096]{1,0:T(8,128)(2,1)} %param.16) | copy-start | bytes 393220
  68.5 52.1 %copy-start.4 = (s32[8]{0:T(128)S(1)}, s32[8]{0:T(128)}, u32[]{:S(2)}) copy-start(s32[8]{0:T(128)} %constant.46.clone) | copy-start | bytes 100
  70.7 23.9 %all-to-all-start.3 = ((f32[64,1,512]{2,1,0:T(1,128)}), f32[64,1,512]{2,1,0:T(1,128)S(1)}, u32[]{:S(2)}, u32[]{:S(2)}) async-start(f32[64,1,512]{2,1,0:T(1,128)} %reshape.106), calls=%async_computation.3 | async-start | bytes 262144 | tf_op jit(solution)/shard_map/all_to_all | solution.py:230
  79.8 32.7 %collective-permute-start.5 = (bf16[16,4096]{1,0:T(8,128)(2,1)S(1)}, bf16[16,4096]{1,0:T(8,128)(2,1)S(1)}, u32[]{:S(2)}, u32[]{:S(2)}) collective-permute-start(bf16[16,4096]{1,0:T(8,128)(2,1)S(1)} %copy-done.3), channel_id=1, source_target_pairs={{0,4},{4,0},{1,5},{5,1},{2,6},{6,2},{3,7},{7,3},{8,12},{12,8},{9,1... | collective-permute-start | bytes 393224 | tf_op jit(solution)/shard_map/ppermute | solution.py:24
  96.9 35.5 %all-to-all-start.4 = ((bf16[64,8,128]{2,1,0:T(8,128)(2,1)}), bf16[64,8,128]{2,1,0:T(8,128)(2,1)S(1)}, u32[]{:S(2)}, u32[]{:S(2)}) async-start(bf16[64,8,128]{2,1,0:T(8,128)(2,1)} %broadcast_in_dim.14), calls=%async_computation.4 | async-start | bytes 262144 | tf_op jit(solution)/shard_map/all_to_all | solution.py:20
  112.5 12.3 %collective-permute-start.6 = (bf16[32,4096]{1,0:T(8,128)(2,1)S(1)}, bf16[32,4096]{1,0:T(8,128)(2,1)S(1)}, u32[]{:S(2)}, u32[]{:S(2)}) collective-permute-start(bf16[32,4096]{1,0:T(8,128)(2,1)S(1)} %pad_maximum_fusion.here_ref), channel_id=1, source_target_pairs={{1,0},{2,1},{3,2},{0,3},{5,4},{6,5},{7,6},{4,7},{9,8},{10,9},{11,1... | collective-permute-start | bytes 786440 | tf_op jit(solution)/shard_map/ppermute | solution.py:164
  114.4 12.0 %collective-permute-start.7 = (bf16[32,4096]{1,0:T(8,128)(2,1)S(1)}, bf16[32,4096]{1,0:T(8,128)(2,1)S(1)}, u32[]{:S(2)}, u32[]{:S(2)}) collective-permute-start(bf16[32,4096]{1,0:T(8,128)(2,1)S(1)} %pad_maximum_fusion.here_ref), channel_id=1, source_target_pairs={{2,0},{3,1},{0,2},{1,3},{6,4},{7,5},{4,6},{5,7},{10,8},{11,9},{8,1... | collective-permute-start | bytes 786440 | tf_op jit(solution)/shard_map/ppermute | solution.py:164
  117.0 15.5 %collective-permute-start.8 = (bf16[32,4096]{1,0:T(8,128)(2,1)S(1)}, bf16[32,4096]{1,0:T(8,128)(2,1)S(1)}, u32[]{:S(2)}, u32[]{:S(2)}) collective-permute-start(bf16[32,4096]{1,0:T(8,128)(2,1)S(1)} %pad_maximum_fusion.here_ref), channel_id=1, source_target_pairs={{3,0},{0,1},{1,2},{2,3},{7,4},{4,5},{5,6},{6,7},{11,8},{8,9},{9,10... | collective-permute-start | bytes 786440 | tf_op jit(solution)/shard_map/ppermute | solution.py:164
Sparse Core Ops, SparseCore 0:
  57.5 66.1 all-gather.1

commit v9 on v8

--- a/solution.py
+++ b/solution.py
@@ -83,7 +83,7 @@
     width = hidden_ref.shape[1]
     copies = [
         pltpu.make_async_copy(
-            weight_hbm.at[pl.ds((chunk * 4 + part) * depth, depth)],
+            weight_hbm.at[pl.ds((chunk // 2 * 8 + part * 2 + chunk % 2) * depth, depth)],
             held.at[chunk, :, pl.ds(part * BLOCK, BLOCK)],
             arrived.at[chunk * 4 + part],
         )
@@ -205,7 +205,7 @@
     w_z = call(along_z_kernel, struct((8 * BLOCK, BLOCK), jnp.bfloat16), 0, "along_z")(
         near, *after((far_ahead, far_behind), left_t)
     )
-    w_all = lax.all_gather(w_z, ("y", "core", "x"), axis=0, tiled=True)
+    w_all = lax.all_gather(w_z, ("y", "x", "core"), axis=0, tiled=True)
     z_place = (lax.axis_index("zl") + jnp.array(Z_STEPS, jnp.int32)) % 8
 
     q_other = swapped(after(queries, left_t), "zh")
@@ -234,12 +234,6 @@
     q_turns = [from_x(q_here, step) for step in (1, 2, 3)]
     own_docs = jnp.sum(doc_parts, 0).astype(jnp.bfloat16)
     doc_low = spread_to_all(jnp.concatenate([own_docs, own_docs], 1), DP)
-
-    score_index = jnp.stack([lax.axis_index("zh"), lax.axis_index("x")]).astype(jnp.int32)
-    scores = call(score_kernel, struct((8, 8 * queries.shape[0]), jnp.float32), 1, "scores")(
-        score_index, doc_low, q_here, *q_turns
-    )
-    w_all = after(w_all, scores)
 
     vmem = pl.BlockSpec(memory_space=pltpu.VMEM)
     hbm = pl.BlockSpec(memory_space=pltpu.HBM)
@@ -261,6 +255,11 @@
         z_place.astype(jnp.int32), hidden_in, norm_gain.reshape(1, width), inv_rms,
         value_grad, w_all,
     )
+    doc_low, values_out = lax.optimization_barrier((doc_low, values_out))
+    score_index = jnp.stack([lax.axis_index("zh"), lax.axis_index("x")]).astype(jnp.int32)
+    scores = call(score_kernel, struct((8, 8 * queries.shape[0]), jnp.float32), 1, "scores")(
+        score_index, doc_low, q_here, *q_turns
+    )
     return (values_out, hidden_grad, scores)
 
 

time: 151 us -> 146 us (0.967)
  the two profiles are of different devices: /device:TPU:1 before, /device:TPU:257 now
where the time goes in v9:
time: 146 us
  starting transfers between devices  79.1 us (54%)
  waiting for transfers between devices  24.7 us (17%)
  between operations  14.4 us (10%)
  Pallas kernels  13.7 us (9%)
  local copies, waits for them, and re-layouts  6.09 us (4%)
  other arithmetic  5.37 us (4%)
  matrix products  2.29 us (2%)
    all_to_all x3, starting transfers between devices, spread_to_all(): return lax.all_to_all(copies, axes, 0, 0, tiled=True)  25.4 us
    ppermute x4, starting transfers between devices, from_z(): lax.ppermute(value, ('zl', 'zh'), [(place((z + step) % 16), place(z)) for...  15.3 us
    all_to_all x1, starting transfers between devices, shards(): lax.all_to_all(doc_term.reshape(64, 8, rank), ('zl', 'zh', 'x'), 0, 0, ti...  15 us
    all_gather x1, waiting for transfers between devices, shards(): w_all = lax.all_gather(w_z, ('y', 'x', 'core'), axis=0, tiled=True)  14.1 us
    ppermute x3, starting transfers between devices, from_x(): return lax.ppermute(value, 'x', [((x + step) % 4, x) for x in range(4)])  10 us
    pallas_call x1, Pallas kernels, shards(): pl.pallas_call(layer_kernel, out_shape=(struct((rows, kv), jnp.bfloat16),...  9.56 us
    ppermute x2, starting transfers between devices, swapped(): return lax.ppermute(value, axis, [(0, 1), (1, 0)])  7.96 us
    all_to_all x1, waiting for transfers between devices, shards(): lax.all_to_all(doc_term.reshape(64, 8, rank), ('zl', 'zh', 'x'), 0, 0, ti...  5.64 us
  transfers between devices with their start and end apart: 15, of which 4 were waited for; matrix products, arithmetic and copies ran while one was open for 8% of the time, Pallas kernels for 7%

profile of v9, /device:TPU:257, one launch (start us, length us, event | category | flops | bytes accessed | tf_op | source)
XLA Modules:
  0.0 145.6 jit_solution(7999650586241763650)
XLA Ops:
  8.7 4.7 %all-to-all-start = ((bf16[8,64,128]{2,1,0:T(8,128)(2,1)}), bf16[8,64,128]{2,1,0:T(8,128)(2,1)S(1)}, u32[]{:S(2)}, u32[]{:S(2)}) async-start(bf16[8,64,128]{2,1,0:T(8,128)(2,1)} %broadcast_in_dim.13), calls=%async_computation | async-start | bytes 262144 | tf_op jit(solution)/shard_map/all_to_all | solution.py:20
  13.5 3.4 %collective-permute-start.1 = (bf16[128,128]{1,0:T(8,128)(2,1)S(1)}, bf16[128,128]{1,0:T(8,128)(2,1)S(1)}, u32[]{:S(2)}, u32[]{:S(2)}) collective-permute-start(bf16[128,128]{1,0:T(8,128)(2,1)S(1)} %constant_dynamic-slice_fusion.refs_1_), channel_id=1, source_target_pairs={{116,0},{0,16},{16,32},{32,48},{48,64},{64,80},{80,96},{96,112},{1... | collective-permute-start | bytes 98312 | tf_op jit(solution)/shard_map/ppermute | solution.py:31
  16.9 4.9 %collective-permute-start.2 = (bf16[128,128]{1,0:T(8,128)(2,1)S(1)}, bf16[128,128]{1,0:T(8,128)(2,1)S(1)}, u32[]{:S(2)}, u32[]{:S(2)}) collective-permute-start(bf16[128,128]{1,0:T(8,128)(2,1)S(1)} %constant_dynamic-slice_fusion.refs_1_), channel_id=1, source_target_pairs={{16,0},{32,16},{48,32},{64,48},{80,64},{96,80},{112,96},{4,112},{2... | collective-permute-start | bytes 98312 | tf_op jit(solution)/shard_map/ppermute | solution.py:31
  22.4 1.1 convolution_convert_fusion
  24.8 4.2 %all-to-all-start.1 = ((bf16[4,592,128]{2,1,0:T(8,128)(2,1)}), bf16[4,592,128]{2,1,0:T(8,128)(2,1)S(1)}, u32[]{:S(2)}, u32[]{:S(2)}) async-start(bf16[4,592,128]{2,1,0:T(8,128)(2,1)} %broadcast_in_dim.15), calls=%async_computation.1 | async-start | bytes 1212416 | tf_op jit(solution)/shard_map/all_to_all | solution.py:20
  29.5 3.1 %collective-permute-start.3 = (bf16[384,128]{1,0:T(8,128)(2,1)S(1)}, bf16[384,128]{1,0:T(8,128)(2,1)}, u32[]{:S(2)}, u32[]{:S(2)}) collective-permute-start(bf16[384,128]{1,0:T(8,128)(2,1)S(1)} %near_three.1.near_ref), channel_id=1, source_target_pairs={{48,0},{64,16},{80,32},{96,48},{112,64},{4,80},{20,96},{36,112},{5... | collective-permute-start | bytes 294920 | tf_op jit(solution)/shard_map/ppermute | solution.py:31
  32.6 4.0 %collective-permute-start.4 = (bf16[384,128]{1,0:T(8,128)(2,1)S(1)}, bf16[384,128]{1,0:T(8,128)(2,1)}, u32[]{:S(2)}, u32[]{:S(2)}) collective-permute-start(bf16[384,128]{1,0:T(8,128)(2,1)S(1)} %near_three.1.near_ref), channel_id=1, source_target_pairs={{84,0},{100,16},{116,32},{0,48},{16,64},{32,80},{48,96},{64,112},{... | collective-permute-start | bytes 294920 | tf_op jit(solution)/shard_map/ppermute | solution.py:31
  36.6 5.6 %collective-permute-start = (bf16[4,592,128]{2,1,0:T(8,128)(2,1)S(1)}, bf16[4,592,128]{2,1,0:T(8,128)(2,1)S(1)}, u32[]{:S(2)}, u32[]{:S(2)}) collective-permute-start(bf16[4,592,128]{2,1,0:T(8,128)(2,1)S(1)} %all-to-all-done.1.own_ref), channel_id=1, source_target_pairs={{0,8},{8,0},{1,9},{9,1},{2,10},{10,2},{3,11},{11,3},{4,12},{12,4},... | collective-permute-start | bytes 1818632 | tf_op jit(solution)/shard_map/ppermute | solution.py:24
  42.2 2.2 %fusion.2.normed_ref = bf16[128,8192]{1,0:T(8,128)(2,1)S(1)} fusion(bf16[128,8192]{1,0:T(8,128)(2,1)} %hidden_hbm.1, f32[8192]{0:T(1024)} %param.10, f32[128]{0:T(128)S(1)} %get-tuple-element.24), kind=kLoop, calls=%fused_computation.4 | loop fusion | flops 4194304 | bytes 4227584 | tf_op jit(solution)/shard_map/convert_element_type | solution.py:200
  45.8 1.7 %along_z.1 = bf16[1024,128]{1,0:T(8,128)(2,1)} custom-call(bf16[384,128]{1,0:T(8,128)(2,1)S(1)} %near_three.1.near_ref, bf16[384,128]{1,0:T(8,128)(2,1)} %collective-permute-done.3.ahead_ref, bf16[384,128]{1,0:T(8,128)(2,1)} %collective-permute-done.4.behind_ref), custom_call_target="tpu_custom_call" | custom-call | tf_op jit(solution)/shard_map/along_z/pallas_call | solution.py:151
  47.5 5.4 %all-to-all-start.2 = ((f32[8,8,128]{2,1,0:T(8,128)}), f32[8,8,128]{2,1,0:T(8,128)S(1)}, u32[]{:S(2)}, u32[]{:S(2)}) async-start(f32[8,8,128]{2,1,0:T(8,128)} %bitcast.36), calls=%async_computation.2 | async-start | bytes 65536 | tf_op jit(solution)/shard_map/all_to_all | solution.py:213
  53.0 4.6 %all-to-all-done.2 = f32[8,8,128]{2,1,0:T(8,128)S(1)} async-done(((f32[8,8,128]{2,1,0:T(8,128)}), f32[8,8,128]{2,1,0:T(8,128)S(1)}, u32[]{:S(2)}, u32[]{:S(2)}) %all-to-all-start.2) | async-done | bytes 32800 | tf_op jit(solution)/shard_map/all_to_all | solution.py:213
  57.9 1.2 fusion.4
  60.1 15.0 %all-to-all-start.3 = ((f32[64,1,512]{2,1,0:T(1,128)}), f32[64,1,512]{2,1,0:T(1,128)S(1)}, u32[]{:S(2)}, u32[]{:S(2)}) async-start(f32[64,1,512]{2,1,0:T(1,128)} %reshape.103), calls=%async_computation.3 | async-start | bytes 262144 | tf_op jit(solution)/shard_map/all_to_all | solution.py:230
  75.1 2.4 %collective-permute-start.5 = (bf16[16,4096]{1,0:T(8,128)(2,1)S(1)}, bf16[16,4096]{1,0:T(8,128)(2,1)S(1)}, u32[]{:S(2)}, u32[]{:S(2)}) collective-permute-start(bf16[16,4096]{1,0:T(8,128)(2,1)S(1)} %copy-done.3), channel_id=1, source_target_pairs={{0,4},{4,0},{1,5},{5,1},{2,6},{6,2},{3,7},{7,3},{8,12},{12,8},{9,1... | collective-permute-start | bytes 393224 | tf_op jit(solution)/shard_map/ppermute | solution.py:24
  77.4 5.6 %all-to-all-done.3 = f32[64,1,512]{2,1,0:T(1,128)S(1)} async-done(((f32[64,1,512]{2,1,0:T(1,128)}), f32[64,1,512]{2,1,0:T(1,128)S(1)}, u32[]{:S(2)}, u32[]{:S(2)}) %all-to-all-start.3) | async-done | bytes 131104 | tf_op jit(solution)/shard_map/all_to_all | solution.py:230
  83.6 0.9 reduce
  85.5 16.5 %all-to-all-start.4 = ((bf16[64,8,128]{2,1,0:T(8,128)(2,1)}), bf16[64,8,128]{2,1,0:T(8,128)(2,1)S(1)}, u32[]{:S(2)}, u32[]{:S(2)}) async-start(bf16[64,8,128]{2,1,0:T(8,128)(2,1)} %broadcast_in_dim.16), calls=%async_computation.4 | async-start | bytes 262144 | tf_op jit(solution)/shard_map/all_to_all | solution.py:20
  102.0 5.6 %collective-permute-start.6 = (bf16[32,4096]{1,0:T(8,128)(2,1)S(1)}, bf16[32,4096]{1,0:T(8,128)(2,1)S(1)}, u32[]{:S(2)}, u32[]{:S(2)}) collective-permute-start(bf16[32,4096]{1,0:T(8,128)(2,1)S(1)} %pad_maximum_fusion.here_ref), channel_id=1, source_target_pairs={{1,0},{2,1},{3,2},{0,3},{5,4},{6,5},{7,6},{4,7},{9,8},{10,9},{11,1... | collective-permute-start | bytes 786440 | tf_op jit(solution)/shard_map/ppermute | solution.py:164
  107.6 1.9 %collective-permute-start.7 = (bf16[32,4096]{1,0:T(8,128)(2,1)S(1)}, bf16[32,4096]{1,0:T(8,128)(2,1)S(1)}, u32[]{:S(2)}, u32[]{:S(2)}) collective-permute-start(bf16[32,4096]{1,0:T(8,128)(2,1)S(1)} %pad_maximum_fusion.here_ref), channel_id=1, source_target_pairs={{2,0},{3,1},{0,2},{1,3},{6,4},{7,5},{4,6},{5,7},{10,8},{11,9},{8,1... | collective-permute-start | bytes 786440 | tf_op jit(solution)/shard_map/ppermute | solution.py:164
  109.5 2.5 %collective-permute-start.8 = (bf16[32,4096]{1,0:T(8,128)(2,1)S(1)}, bf16[32,4096]{1,0:T(8,128)(2,1)S(1)}, u32[]{:S(2)}, u32[]{:S(2)}) collective-permute-start(bf16[32,4096]{1,0:T(8,128)(2,1)S(1)} %pad_maximum_fusion.here_ref), channel_id=1, source_target_pairs={{3,0},{0,1},{1,2},{2,3},{7,4},{4,5},{5,6},{6,7},{11,8},{8,9},{9,10... | collective-permute-start | bytes 786440 | tf_op jit(solution)/shard_map/ppermute | solution.py:164
  113.4 14.1 %all-gather.2.cloned.1.call-done.weight_hbm = bf16[32768,128]{1,0:T(8,128)(2,1)} async-done(((bf16[1024,128]{1,0:T(8,128)(2,1)}), bf16[32768,128]{1,0:T(8,128)(2,1)}) %all-gather.2.cloned.1.call-update) | async-done | bytes 8388624 | tf_op jit(solution)/shard_map/all_gather | solution.py:208
  127.5 9.6 %layer.1 = (bf16[128,512]{1,0:T(8,128)(2,1)}, bf16[128,8192]{1,0:T(8,128)(2,1)}) custom-call(s32[8]{0:T(128)} %and_select_fusion.place_ref, bf16[128,8192]{1,0:T(8,128)(2,1)} %hidden_hbm.1, f32[1,8192]{1,0:T(1,128)} %bitcast.42, f32[128,1]{1,0:T(8,128)} %copy.21.scale_ref, bf16[128,512]{1,0:T(8,128)(2,1)} %grad_ref.1, ...), custom_call_target="tpu_custom_call" | custom-call | tf_op jit(solution)/shard_map/layer/pallas_call | solution.py:241
  137.1 1.6 %scores.1 = f32[8,128]{1,0:T(8,128)} custom-call(s32[2]{0:T(128)S(1)} %pad_add_fusion.index_ref, bf16[64,8,128]{2,1,0:T(8,128)(2,1)S(1)} %all-to-all-done.4.docs_ref, bf16[32,4096]{1,0:T(8,128)(2,1)S(1)} %pad_maximum_fusion.here_ref, bf16[32,4096]{1,0:T(8,128)(2,1)S(1)} %collective-permute-done.6.one_ref, ...), custom_call_target="tpu_custom_call" | custom-call | tf_op jit(solution)/shard_map/scores/pallas_call | solution.py:151
  (52 shorter events, 9.5 us)
Async XLA Ops:
  7.2 6.3 %copy-start = (bf16[128,512]{1,0:T(8,128)(2,1)S(1)}, bf16[128,512]{1,0:T(8,128)(2,1)}, u32[]{:S(2)}) copy-start(bf16[128,512]{1,0:T(8,128)(2,1)} %param.11) | copy-start | bytes 393220
  7.2 21.8 %copy-start.2 = (bf16[128,8192]{1,0:T(8,128)(2,1)S(1)}, bf16[128,8192]{1,0:T(8,128)(2,1)}, u32[]{:S(2)}) copy-start(bf16[128,8192]{1,0:T(8,128)(2,1)} %hidden_hbm.1) | copy-start | bytes 6291460
  8.7 15.1 %all-to-all-start = ((bf16[8,64,128]{2,1,0:T(8,128)(2,1)}), bf16[8,64,128]{2,1,0:T(8,128)(2,1)S(1)}, u32[]{:S(2)}, u32[]{:S(2)}) async-start(bf16[8,64,128]{2,1,0:T(8,128)(2,1)} %broadcast_in_dim.13), calls=%async_computation | async-start | bytes 262144 | tf_op jit(solution)/shard_map/all_to_all | solution.py:20
  13.5 15.9 %collective-permute-start.1 = (bf16[128,128]{1,0:T(8,128)(2,1)S(1)}, bf16[128,128]{1,0:T(8,128)(2,1)S(1)}, u32[]{:S(2)}, u32[]{:S(2)}) collective-permute-start(bf16[128,128]{1,0:T(8,128)(2,1)S(1)} %constant_dynamic-slice_fusion.refs_1_), channel_id=1, source_target_pairs={{116,0},{0,16},{16,32},{32,48},{48,64},{64,80},{80,96},{96,112},{1... | collective-permute-start | bytes 98312 | tf_op jit(solution)/shard_map/ppermute | solution.py:31
  16.9 12.6 %collective-permute-start.2 = (bf16[128,128]{1,0:T(8,128)(2,1)S(1)}, bf16[128,128]{1,0:T(8,128)(2,1)S(1)}, u32[]{:S(2)}, u32[]{:S(2)}) collective-permute-start(bf16[128,128]{1,0:T(8,128)(2,1)S(1)} %constant_dynamic-slice_fusion.refs_1_), channel_id=1, source_target_pairs={{16,0},{32,16},{48,32},{64,48},{80,64},{96,80},{112,96},{4,112},{2... | collective-permute-start | bytes 98312 | tf_op jit(solution)/shard_map/ppermute | solution.py:31
  24.8 11.8 %all-to-all-start.1 = ((bf16[4,592,128]{2,1,0:T(8,128)(2,1)}), bf16[4,592,128]{2,1,0:T(8,128)(2,1)S(1)}, u32[]{:S(2)}, u32[]{:S(2)}) async-start(bf16[4,592,128]{2,1,0:T(8,128)(2,1)} %broadcast_in_dim.15), calls=%async_computation.1 | async-start | bytes 1212416 | tf_op jit(solution)/shard_map/all_to_all | solution.py:20
  28.9 98.5 %all-gather.2.cloned.1.call-start = ((), (), s32[]{:S(2)}) async-start(), calls=%async_computation.5 | async-start | bytes 8650752 | tf_op jit(solution)/shard_map/all_gather | solution.py:208
  29.5 16.4 %collective-permute-start.3 = (bf16[384,128]{1,0:T(8,128)(2,1)S(1)}, bf16[384,128]{1,0:T(8,128)(2,1)}, u32[]{:S(2)}, u32[]{:S(2)}) collective-permute-start(bf16[384,128]{1,0:T(8,128)(2,1)S(1)} %near_three.1.near_ref), channel_id=1, source_target_pairs={{48,0},{64,16},{80,32},{96,48},{112,64},{4,80},{20,96},{36,112},{5... | collective-permute-start | bytes 294920 | tf_op jit(solution)/shard_map/ppermute | solution.py:31
  32.6 13.3 %collective-permute-start.4 = (bf16[384,128]{1,0:T(8,128)(2,1)S(1)}, bf16[384,128]{1,0:T(8,128)(2,1)}, u32[]{:S(2)}, u32[]{:S(2)}) collective-permute-start(bf16[384,128]{1,0:T(8,128)(2,1)S(1)} %near_three.1.near_ref), channel_id=1, source_target_pairs={{84,0},{100,16},{116,32},{0,48},{16,64},{32,80},{48,96},{64,112},{... | collective-permute-start | bytes 294920 | tf_op jit(solution)/shard_map/ppermute | solution.py:31
  36.6 7.8 %collective-permute-start = (bf16[4,592,128]{2,1,0:T(8,128)(2,1)S(1)}, bf16[4,592,128]{2,1,0:T(8,128)(2,1)S(1)}, u32[]{:S(2)}, u32[]{:S(2)}) collective-permute-start(bf16[4,592,128]{2,1,0:T(8,128)(2,1)S(1)} %all-to-all-done.1.own_ref), channel_id=1, source_target_pairs={{0,8},{8,0},{1,9},{9,1},{2,10},{10,2},{3,11},{11,3},{4,12},{12,4},... | collective-permute-start | bytes 1818632 | tf_op jit(solution)/shard_map/ppermute | solution.py:24
  45.2 0.6 copy-start.1
  47.5 10.1 %all-to-all-start.2 = ((f32[8,8,128]{2,1,0:T(8,128)}), f32[8,8,128]{2,1,0:T(8,128)S(1)}, u32[]{:S(2)}, u32[]{:S(2)}) async-start(f32[8,8,128]{2,1,0:T(8,128)} %bitcast.36), calls=%async_computation.2 | async-start | bytes 65536 | tf_op jit(solution)/shard_map/all_to_all | solution.py:213
  57.9 17.2 %copy-start.3 = (bf16[16,4096]{1,0:T(8,128)(2,1)S(1)}, bf16[16,4096]{1,0:T(8,128)(2,1)}, u32[]{:S(2)}) copy-start(bf16[16,4096]{1,0:T(8,128)(2,1)} %param.16) | copy-start | bytes 393220
  57.9 55.0 %copy-start.4 = (s32[8]{0:T(128)S(1)}, s32[8]{0:T(128)}, u32[]{:S(2)}) copy-start(s32[8]{0:T(128)} %constant.46.clone) | copy-start | bytes 100
  60.1 23.0 %all-to-all-start.3 = ((f32[64,1,512]{2,1,0:T(1,128)}), f32[64,1,512]{2,1,0:T(1,128)S(1)}, u32[]{:S(2)}, u32[]{:S(2)}) async-start(f32[64,1,512]{2,1,0:T(1,128)} %reshape.103), calls=%async_computation.3 | async-start | bytes 262144 | tf_op jit(solution)/shard_map/all_to_all | solution.py:230
  75.1 26.9 %collective-permute-start.5 = (bf16[16,4096]{1,0:T(8,128)(2,1)S(1)}, bf16[16,4096]{1,0:T(8,128)(2,1)S(1)}, u32[]{:S(2)}, u32[]{:S(2)}) collective-permute-start(bf16[16,4096]{1,0:T(8,128)(2,1)S(1)} %copy-done.3), channel_id=1, source_target_pairs={{0,4},{4,0},{1,5},{5,1},{2,6},{6,2},{3,7},{7,3},{8,12},{12,8},{9,1... | collective-permute-start | bytes 393224 | tf_op jit(solution)/shard_map/ppermute | solution.py:24
  85.5 51.6 %all-to-all-start.4 = ((bf16[64,8,128]{2,1,0:T(8,128)(2,1)}), bf16[64,8,128]{2,1,0:T(8,128)(2,1)S(1)}, u32[]{:S(2)}, u32[]{:S(2)}) async-start(bf16[64,8,128]{2,1,0:T(8,128)(2,1)} %broadcast_in_dim.16), calls=%async_computation.4 | async-start | bytes 262144 | tf_op jit(solution)/shard_map/all_to_all | solution.py:20
  102.0 35.1 %collective-permute-start.6 = (bf16[32,4096]{1,0:T(8,128)(2,1)S(1)}, bf16[32,4096]{1,0:T(8,128)(2,1)S(1)}, u32[]{:S(2)}, u32[]{:S(2)}) collective-permute-start(bf16[32,4096]{1,0:T(8,128)(2,1)S(1)} %pad_maximum_fusion.here_ref), channel_id=1, source_target_pairs={{1,0},{2,1},{3,2},{0,3},{5,4},{6,5},{7,6},{4,7},{9,8},{10,9},{11,1... | collective-permute-start | bytes 786440 | tf_op jit(solution)/shard_map/ppermute | solution.py:164
  107.6 29.5 %collective-permute-start.7 = (bf16[32,4096]{1,0:T(8,128)(2,1)S(1)}, bf16[32,4096]{1,0:T(8,128)(2,1)S(1)}, u32[]{:S(2)}, u32[]{:S(2)}) collective-permute-start(bf16[32,4096]{1,0:T(8,128)(2,1)S(1)} %pad_maximum_fusion.here_ref), channel_id=1, source_target_pairs={{2,0},{3,1},{0,2},{1,3},{6,4},{7,5},{4,6},{5,7},{10,8},{11,9},{8,1... | collective-permute-start | bytes 786440 | tf_op jit(solution)/shard_map/ppermute | solution.py:164
  109.5 27.6 %collective-permute-start.8 = (bf16[32,4096]{1,0:T(8,128)(2,1)S(1)}, bf16[32,4096]{1,0:T(8,128)(2,1)S(1)}, u32[]{:S(2)}, u32[]{:S(2)}) collective-permute-start(bf16[32,4096]{1,0:T(8,128)(2,1)S(1)} %pad_maximum_fusion.here_ref), channel_id=1, source_target_pairs={{3,0},{0,1},{1,2},{2,3},{7,4},{4,5},{5,6},{6,7},{11,8},{8,9},{9,10... | collective-permute-start | bytes 786440 | tf_op jit(solution)/shard_map/ppermute | solution.py:164
Sparse Core Ops, SparseCore 0:
  47.6 79.7 all-gather.1

commit v10 on v9

--- a/solution.py
+++ b/solution.py
@@ -77,7 +77,7 @@
 
 def layer_kernel(
     place_ref, hidden_hbm, gain_ref, scale_ref, grad_ref, weight_hbm,
-    values_ref, hidden_grad_ref, held, base, hidden_ref, arrived,
+    values_ref, hidden_grad_hbm, held, base, hidden_ref, formed, arrived, left_for,
 ):
     chunks, depth = held.shape[:2]
     width = hidden_ref.shape[1]
@@ -113,10 +113,20 @@
     values_ref[...] = total.astype(jnp.bfloat16)
     along = jnp.sum(total * grad.astype(jnp.float32), axis=1, keepdims=True)
     pull = inv_rms * inv_rms * along / width
-    for start in range(0, width, 512):
-        where = slice(start, start + 512)
+    sent = []
+    for start in range(0, width, 1024):
+        where = slice(start, start + 1024)
         wide = hidden_ref[:, where].astype(jnp.float32)
-        hidden_grad_ref[:, where] = (base[:, where] - wide * pull).astype(jnp.bfloat16)
+        formed[:, where] = (base[:, where] - wide * pull).astype(jnp.bfloat16)
+        columns = pl.ds(start, 1024)
+        sent.append(
+            pltpu.make_async_copy(
+                formed.at[:, columns], hidden_grad_hbm.at[:, columns], left_for.at[len(sent)]
+            )
+        )
+        sent[-1].start()
+    for copy in sent:
+        copy.wait()
 
 
 def score_kernel(index_ref, docs_ref, here_ref, one_ref, two_ref, three_ref, scores_ref):
@@ -242,12 +252,14 @@
         layer_kernel,
         out_shape=(struct((rows, kv), jnp.bfloat16), struct((rows, width), jnp.bfloat16)),
         in_specs=[pl.BlockSpec(memory_space=pltpu.SMEM), hbm, vmem, vmem, vmem, hbm],
-        out_specs=(vmem, vmem),
+        out_specs=(vmem, hbm),
         scratch_shapes=[
             pltpu.VMEM((chunks, width // chunks, kv), jnp.bfloat16),
             pltpu.VMEM((rows, width), jnp.float32),
             pltpu.VMEM((rows, width), jnp.bfloat16),
+            pltpu.VMEM((rows, width), jnp.bfloat16),
             pltpu.SemaphoreType.DMA((4 * chunks + 1,)),
+            pltpu.SemaphoreType.DMA((width // 1024,)),
         ],
         compiler_params=pltpu.CompilerParams(vmem_limit_bytes=58 * 1024 * 1024),
         name="layer",

time: 146 us -> 147 us (level)
  transfers between devices with their start and end apart: 15 -> 15, of which waited for: 4 -> 4; matrix products, arithmetic and copies ran while one was open for 8% -> 8% of each run, Pallas kernels for 7% -> 8%
where the time goes in v10:
time: 147 us; the launch traced here: 146 us
  starting transfers between devices  79.1 us (54%)
  waiting for transfers between devices  24.7 us (17%)
  Pallas kernels  14.4 us (10%)
  between operations  14.4 us (10%)
  local copies, waits for them, and re-layouts  6.09 us (4%)
  other arithmetic  5.37 us (4%)
  matrix products  2.29 us (2%)
    all_to_all x3, starting transfers between devices, spread_to_all(): return lax.all_to_all(copies, axes, 0, 0, tiled=True)  25.4 us
    ppermute x4, starting transfers between devices, from_z(): lax.ppermute(value, ('zl', 'zh'), [(place((z + step) % 16), place(z)) for...  15.3 us
    all_to_all x1, starting transfers between devices, shards(): lax.all_to_all(doc_term.reshape(64, 8, rank), ('zl', 'zh', 'x'), 0, 0, ti...  15 us
    all_gather x1, waiting for transfers between devices, shards(): w_all = lax.all_gather(w_z, ('y', 'x', 'core'), axis=0, tiled=True)  14.1 us
    pallas_call x1, Pallas kernels, shards(): pl.pallas_call(layer_kernel, out_shape=(struct((rows, kv), jnp.bfloat16),...  10.3 us
    ppermute x3, starting transfers between devices, from_x(): return lax.ppermute(value, 'x', [((x + step) % 4, x) for x in range(4)])  10 us
    ppermute x2, starting transfers between devices, swapped(): return lax.ppermute(value, axis, [(0, 1), (1, 0)])  7.96 us
    all_to_all x1, waiting for transfers between devices, shards(): lax.all_to_all(doc_term.reshape(64, 8, rank), ('zl', 'zh', 'x'), 0, 0, ti...  5.64 us
  transfers between devices with their start and end apart: 15, of which 4 were waited for; matrix products, arithmetic and copies ran while one was open for 8% of the time, Pallas kernels for 8%

profile of v10, /device:TPU:257, one launch (start us, length us, event | category | flops | bytes accessed | tf_op | source)
XLA Modules:
  0.0 146.3 jit_solution(13444656385114632229)
XLA Ops:
  8.7 4.7 %all-to-all-start = ((bf16[8,64,128]{2,1,0:T(8,128)(2,1)}), bf16[8,64,128]{2,1,0:T(8,128)(2,1)S(1)}, u32[]{:S(2)}, u32[]{:S(2)}) async-start(bf16[8,64,128]{2,1,0:T(8,128)(2,1)} %broadcast_in_dim.13), calls=%async_computation | async-start | bytes 262144 | tf_op jit(solution)/shard_map/all_to_all | solution.py:20
  13.5 3.4 %collective-permute-start.1 = (bf16[128,128]{1,0:T(8,128)(2,1)S(1)}, bf16[128,128]{1,0:T(8,128)(2,1)S(1)}, u32[]{:S(2)}, u32[]{:S(2)}) collective-permute-start(bf16[128,128]{1,0:T(8,128)(2,1)S(1)} %constant_dynamic-slice_fusion.refs_1_), channel_id=1, source_target_pairs={{116,0},{0,16},{16,32},{32,48},{48,64},{64,80},{80,96},{96,112},{1... | collective-permute-start | bytes 98312 | tf_op jit(solution)/shard_map/ppermute | solution.py:31
  16.9 4.9 %collective-permute-start.2 = (bf16[128,128]{1,0:T(8,128)(2,1)S(1)}, bf16[128,128]{1,0:T(8,128)(2,1)S(1)}, u32[]{:S(2)}, u32[]{:S(2)}) collective-permute-start(bf16[128,128]{1,0:T(8,128)(2,1)S(1)} %constant_dynamic-slice_fusion.refs_1_), channel_id=1, source_target_pairs={{16,0},{32,16},{48,32},{64,48},{80,64},{96,80},{112,96},{4,112},{2... | collective-permute-start | bytes 98312 | tf_op jit(solution)/shard_map/ppermute | solution.py:31
  22.4 1.1 convolution_convert_fusion
  24.8 4.2 %all-to-all-start.1 = ((bf16[4,592,128]{2,1,0:T(8,128)(2,1)}), bf16[4,592,128]{2,1,0:T(8,128)(2,1)S(1)}, u32[]{:S(2)}, u32[]{:S(2)}) async-start(bf16[4,592,128]{2,1,0:T(8,128)(2,1)} %broadcast_in_dim.15), calls=%async_computation.1 | async-start | bytes 1212416 | tf_op jit(solution)/shard_map/all_to_all | solution.py:20
  29.5 3.1 %collective-permute-start.3 = (bf16[384,128]{1,0:T(8,128)(2,1)S(1)}, bf16[384,128]{1,0:T(8,128)(2,1)}, u32[]{:S(2)}, u32[]{:S(2)}) collective-permute-start(bf16[384,128]{1,0:T(8,128)(2,1)S(1)} %near_three.1.near_ref), channel_id=1, source_target_pairs={{48,0},{64,16},{80,32},{96,48},{112,64},{4,80},{20,96},{36,112},{5... | collective-permute-start | bytes 294920 | tf_op jit(solution)/shard_map/ppermute | solution.py:31
  32.6 4.0 %collective-permute-start.4 = (bf16[384,128]{1,0:T(8,128)(2,1)S(1)}, bf16[384,128]{1,0:T(8,128)(2,1)}, u32[]{:S(2)}, u32[]{:S(2)}) collective-permute-start(bf16[384,128]{1,0:T(8,128)(2,1)S(1)} %near_three.1.near_ref), channel_id=1, source_target_pairs={{84,0},{100,16},{116,32},{0,48},{16,64},{32,80},{48,96},{64,112},{... | collective-permute-start | bytes 294920 | tf_op jit(solution)/shard_map/ppermute | solution.py:31
  36.6 5.6 %collective-permute-start = (bf16[4,592,128]{2,1,0:T(8,128)(2,1)S(1)}, bf16[4,592,128]{2,1,0:T(8,128)(2,1)S(1)}, u32[]{:S(2)}, u32[]{:S(2)}) collective-permute-start(bf16[4,592,128]{2,1,0:T(8,128)(2,1)S(1)} %all-to-all-done.1.own_ref), channel_id=1, source_target_pairs={{0,8},{8,0},{1,9},{9,1},{2,10},{10,2},{3,11},{11,3},{4,12},{12,4},... | collective-permute-start | bytes 1818632 | tf_op jit(solution)/shard_map/ppermute | solution.py:24
  42.2 2.2 %fusion.2.normed_ref = bf16[128,8192]{1,0:T(8,128)(2,1)S(1)} fusion(bf16[128,8192]{1,0:T(8,128)(2,1)} %hidden_hbm.1, f32[8192]{0:T(1024)} %param.10, f32[128]{0:T(128)S(1)} %get-tuple-element.24), kind=kLoop, calls=%fused_computation.4 | loop fusion | flops 4194304 | bytes 4227584 | tf_op jit(solution)/shard_map/convert_element_type | solution.py:210
  45.8 1.7 %along_z.1 = bf16[1024,128]{1,0:T(8,128)(2,1)} custom-call(bf16[384,128]{1,0:T(8,128)(2,1)S(1)} %near_three.1.near_ref, bf16[384,128]{1,0:T(8,128)(2,1)} %collective-permute-done.3.ahead_ref, bf16[384,128]{1,0:T(8,128)(2,1)} %collective-permute-done.4.behind_ref), custom_call_target="tpu_custom_call" | custom-call | tf_op jit(solution)/shard_map/along_z/pallas_call | solution.py:161
  47.5 5.4 %all-to-all-start.2 = ((f32[8,8,128]{2,1,0:T(8,128)}), f32[8,8,128]{2,1,0:T(8,128)S(1)}, u32[]{:S(2)}, u32[]{:S(2)}) async-start(f32[8,8,128]{2,1,0:T(8,128)} %bitcast.36), calls=%async_computation.2 | async-start | bytes 65536 | tf_op jit(solution)/shard_map/all_to_all | solution.py:223
  53.0 4.6 %all-to-all-done.2 = f32[8,8,128]{2,1,0:T(8,128)S(1)} async-done(((f32[8,8,128]{2,1,0:T(8,128)}), f32[8,8,128]{2,1,0:T(8,128)S(1)}, u32[]{:S(2)}, u32[]{:S(2)}) %all-to-all-start.2) | async-done | bytes 32800 | tf_op jit(solution)/shard_map/all_to_all | solution.py:223
  57.9 1.2 fusion.4
  60.1 15.0 %all-to-all-start.3 = ((f32[64,1,512]{2,1,0:T(1,128)}), f32[64,1,512]{2,1,0:T(1,128)S(1)}, u32[]{:S(2)}, u32[]{:S(2)}) async-start(f32[64,1,512]{2,1,0:T(1,128)} %reshape.103), calls=%async_computation.3 | async-start | bytes 262144 | tf_op jit(solution)/shard_map/all_to_all | solution.py:240
  75.1 2.4 %collective-permute-start.5 = (bf16[16,4096]{1,0:T(8,128)(2,1)S(1)}, bf16[16,4096]{1,0:T(8,128)(2,1)S(1)}, u32[]{:S(2)}, u32[]{:S(2)}) collective-permute-start(bf16[16,4096]{1,0:T(8,128)(2,1)S(1)} %copy-done.3), channel_id=1, source_target_pairs={{0,4},{4,0},{1,5},{5,1},{2,6},{6,2},{3,7},{7,3},{8,12},{12,8},{9,1... | collective-permute-start | bytes 393224 | tf_op jit(solution)/shard_map/ppermute | solution.py:24
  77.4 5.6 %all-to-all-done.3 = f32[64,1,512]{2,1,0:T(1,128)S(1)} async-done(((f32[64,1,512]{2,1,0:T(1,128)}), f32[64,1,512]{2,1,0:T(1,128)S(1)}, u32[]{:S(2)}, u32[]{:S(2)}) %all-to-all-start.3) | async-done | bytes 131104 | tf_op jit(solution)/shard_map/all_to_all | solution.py:240
  83.6 0.9 reduce
  85.5 16.5 %all-to-all-start.4 = ((bf16[64,8,128]{2,1,0:T(8,128)(2,1)}), bf16[64,8,128]{2,1,0:T(8,128)(2,1)S(1)}, u32[]{:S(2)}, u32[]{:S(2)}) async-start(bf16[64,8,128]{2,1,0:T(8,128)(2,1)} %broadcast_in_dim.16), calls=%async_computation.4 | async-start | bytes 262144 | tf_op jit(solution)/shard_map/all_to_all | solution.py:20
  102.0 5.6 %collective-permute-start.6 = (bf16[32,4096]{1,0:T(8,128)(2,1)S(1)}, bf16[32,4096]{1,0:T(8,128)(2,1)S(1)}, u32[]{:S(2)}, u32[]{:S(2)}) collective-permute-start(bf16[32,4096]{1,0:T(8,128)(2,1)S(1)} %pad_maximum_fusion.here_ref), channel_id=1, source_target_pairs={{1,0},{2,1},{3,2},{0,3},{5,4},{6,5},{7,6},{4,7},{9,8},{10,9},{11,1... | collective-permute-start | bytes 786440 | tf_op jit(solution)/shard_map/ppermute | solution.py:174
  107.6 1.9 %collective-permute-start.7 = (bf16[32,4096]{1,0:T(8,128)(2,1)S(1)}, bf16[32,4096]{1,0:T(8,128)(2,1)S(1)}, u32[]{:S(2)}, u32[]{:S(2)}) collective-permute-start(bf16[32,4096]{1,0:T(8,128)(2,1)S(1)} %pad_maximum_fusion.here_ref), channel_id=1, source_target_pairs={{2,0},{3,1},{0,2},{1,3},{6,4},{7,5},{4,6},{5,7},{10,8},{11,9},{8,1... | collective-permute-start | bytes 786440 | tf_op jit(solution)/shard_map/ppermute | solution.py:174
  109.5 2.5 %collective-permute-start.8 = (bf16[32,4096]{1,0:T(8,128)(2,1)S(1)}, bf16[32,4096]{1,0:T(8,128)(2,1)S(1)}, u32[]{:S(2)}, u32[]{:S(2)}) collective-permute-start(bf16[32,4096]{1,0:T(8,128)(2,1)S(1)} %pad_maximum_fusion.here_ref), channel_id=1, source_target_pairs={{3,0},{0,1},{1,2},{2,3},{7,4},{4,5},{5,6},{6,7},{11,8},{8,9},{9,10... | collective-permute-start | bytes 786440 | tf_op jit(solution)/shard_map/ppermute | solution.py:174
  113.4 14.1 %all-gather.2.cloned.1.call-done.weight_hbm = bf16[32768,128]{1,0:T(8,128)(2,1)} async-done(((bf16[1024,128]{1,0:T(8,128)(2,1)}), bf16[32768,128]{1,0:T(8,128)(2,1)}) %all-gather.2.cloned.1.call-update) | async-done | bytes 8388624 | tf_op jit(solution)/shard_map/all_gather | solution.py:218
  127.5 10.3 %layer.1 = (bf16[128,512]{1,0:T(8,128)(2,1)}, bf16[128,8192]{1,0:T(8,128)(2,1)}) custom-call(s32[8]{0:T(128)} %and_select_fusion.place_ref, bf16[128,8192]{1,0:T(8,128)(2,1)} %hidden_hbm.1, f32[1,8192]{1,0:T(1,128)} %bitcast.42, f32[128,1]{1,0:T(8,128)} %copy.21.scale_ref, bf16[128,512]{1,0:T(8,128)(2,1)} %grad_ref.1, ...), custom_call_target="tpu_custom_call" | custom-call | tf_op jit(solution)/shard_map/layer/pallas_call | solution.py:251
  137.8 1.6 %scores.1 = f32[8,128]{1,0:T(8,128)} custom-call(s32[2]{0:T(128)S(1)} %pad_add_fusion.index_ref, bf16[64,8,128]{2,1,0:T(8,128)(2,1)S(1)} %all-to-all-done.4.docs_ref, bf16[32,4096]{1,0:T(8,128)(2,1)S(1)} %pad_maximum_fusion.here_ref, bf16[32,4096]{1,0:T(8,128)(2,1)S(1)} %collective-permute-done.6.one_ref, ...), custom_call_target="tpu_custom_call" | custom-call | tf_op jit(solution)/shard_map/scores/pallas_call | solution.py:161
  (52 shorter events, 9.5 us)
Async XLA Ops:
  7.2 6.3 %copy-start = (bf16[128,512]{1,0:T(8,128)(2,1)S(1)}, bf16[128,512]{1,0:T(8,128)(2,1)}, u32[]{:S(2)}) copy-start(bf16[128,512]{1,0:T(8,128)(2,1)} %param.11) | copy-start | bytes 393220
  7.2 21.8 %copy-start.2 = (bf16[128,8192]{1,0:T(8,128)(2,1)S(1)}, bf16[128,8192]{1,0:T(8,128)(2,1)}, u32[]{:S(2)}) copy-start(bf16[128,8192]{1,0:T(8,128)(2,1)} %hidden_hbm.1) | copy-start | bytes 6291460
  8.7 15.1 %all-to-all-start = ((bf16[8,64,128]{2,1,0:T(8,128)(2,1)}), bf16[8,64,128]{2,1,0:T(8,128)(2,1)S(1)}, u32[]{:S(2)}, u32[]{:S(2)}) async-start(bf16[8,64,128]{2,1,0:T(8,128)(2,1)} %broadcast_in_dim.13), calls=%async_computation | async-start | bytes 262144 | tf_op jit(solution)/shard_map/all_to_all | solution.py:20
  13.5 15.9 %collective-permute-start.1 = (bf16[128,128]{1,0:T(8,128)(2,1)S(1)}, bf16[128,128]{1,0:T(8,128)(2,1)S(1)}, u32[]{:S(2)}, u32[]{:S(2)}) collective-permute-start(bf16[128,128]{1,0:T(8,128)(2,1)S(1)} %constant_dynamic-slice_fusion.refs_1_), channel_id=1, source_target_pairs={{116,0},{0,16},{16,32},{32,48},{48,64},{64,80},{80,96},{96,112},{1... | collective-permute-start | bytes 98312 | tf_op jit(solution)/shard_map/ppermute | solution.py:31
  16.9 12.6 %collective-permute-start.2 = (bf16[128,128]{1,0:T(8,128)(2,1)S(1)}, bf16[128,128]{1,0:T(8,128)(2,1)S(1)}, u32[]{:S(2)}, u32[]{:S(2)}) collective-permute-start(bf16[128,128]{1,0:T(8,128)(2,1)S(1)} %constant_dynamic-slice_fusion.refs_1_), channel_id=1, source_target_pairs={{16,0},{32,16},{48,32},{64,48},{80,64},{96,80},{112,96},{4,112},{2... | collective-permute-start | bytes 98312 | tf_op jit(solution)/shard_map/ppermute | solution.py:31
  24.8 11.8 %all-to-all-start.1 = ((bf16[4,592,128]{2,1,0:T(8,128)(2,1)}), bf16[4,592,128]{2,1,0:T(8,128)(2,1)S(1)}, u32[]{:S(2)}, u32[]{:S(2)}) async-start(bf16[4,592,128]{2,1,0:T(8,128)(2,1)} %broadcast_in_dim.15), calls=%async_computation.1 | async-start | bytes 1212416 | tf_op jit(solution)/shard_map/all_to_all | solution.py:20
  28.9 98.5 %all-gather.2.cloned.1.call-start = ((), (), s32[]{:S(2)}) async-start(), calls=%async_computation.5 | async-start | bytes 8650752 | tf_op jit(solution)/shard_map/all_gather | solution.py:218
  29.5 16.4 %collective-permute-start.3 = (bf16[384,128]{1,0:T(8,128)(2,1)S(1)}, bf16[384,128]{1,0:T(8,128)(2,1)}, u32[]{:S(2)}, u32[]{:S(2)}) collective-permute-start(bf16[384,128]{1,0:T(8,128)(2,1)S(1)} %near_three.1.near_ref), channel_id=1, source_target_pairs={{48,0},{64,16},{80,32},{96,48},{112,64},{4,80},{20,96},{36,112},{5... | collective-permute-start | bytes 294920 | tf_op jit(solution)/shard_map/ppermute | solution.py:31
  32.6 13.3 %collective-permute-start.4 = (bf16[384,128]{1,0:T(8,128)(2,1)S(1)}, bf16[384,128]{1,0:T(8,128)(2,1)}, u32[]{:S(2)}, u32[]{:S(2)}) collective-permute-start(bf16[384,128]{1,0:T(8,128)(2,1)S(1)} %near_three.1.near_ref), channel_id=1, source_target_pairs={{84,0},{100,16},{116,32},{0,48},{16,64},{32,80},{48,96},{64,112},{... | collective-permute-start | bytes 294920 | tf_op jit(solution)/shard_map/ppermute | solution.py:31
  36.6 7.8 %collective-permute-start = (bf16[4,592,128]{2,1,0:T(8,128)(2,1)S(1)}, bf16[4,592,128]{2,1,0:T(8,128)(2,1)S(1)}, u32[]{:S(2)}, u32[]{:S(2)}) collective-permute-start(bf16[4,592,128]{2,1,0:T(8,128)(2,1)S(1)} %all-to-all-done.1.own_ref), channel_id=1, source_target_pairs={{0,8},{8,0},{1,9},{9,1},{2,10},{10,2},{3,11},{11,3},{4,12},{12,4},... | collective-permute-start | bytes 1818632 | tf_op jit(solution)/shard_map/ppermute | solution.py:24
  45.2 0.6 copy-start.1
  47.5 10.1 %all-to-all-start.2 = ((f32[8,8,128]{2,1,0:T(8,128)}), f32[8,8,128]{2,1,0:T(8,128)S(1)}, u32[]{:S(2)}, u32[]{:S(2)}) async-start(f32[8,8,128]{2,1,0:T(8,128)} %bitcast.36), calls=%async_computation.2 | async-start | bytes 65536 | tf_op jit(solution)/shard_map/all_to_all | solution.py:223
  57.9 17.2 %copy-start.3 = (bf16[16,4096]{1,0:T(8,128)(2,1)S(1)}, bf16[16,4096]{1,0:T(8,128)(2,1)}, u32[]{:S(2)}) copy-start(bf16[16,4096]{1,0:T(8,128)(2,1)} %param.16) | copy-start | bytes 393220
  57.9 55.0 %copy-start.4 = (s32[8]{0:T(128)S(1)}, s32[8]{0:T(128)}, u32[]{:S(2)}) copy-start(s32[8]{0:T(128)} %constant.46.clone) | copy-start | bytes 100
  60.1 23.0 %all-to-all-start.3 = ((f32[64,1,512]{2,1,0:T(1,128)}), f32[64,1,512]{2,1,0:T(1,128)S(1)}, u32[]{:S(2)}, u32[]{:S(2)}) async-start(f32[64,1,512]{2,1,0:T(1,128)} %reshape.103), calls=%async_computation.3 | async-start | bytes 262144 | tf_op jit(solution)/shard_map/all_to_all | solution.py:240
  75.1 26.9 %collective-permute-start.5 = (bf16[16,4096]{1,0:T(8,128)(2,1)S(1)}, bf16[16,4096]{1,0:T(8,128)(2,1)S(1)}, u32[]{:S(2)}, u32[]{:S(2)}) collective-permute-start(bf16[16,4096]{1,0:T(8,128)(2,1)S(1)} %copy-done.3), channel_id=1, source_target_pairs={{0,4},{4,0},{1,5},{5,1},{2,6},{6,2},{3,7},{7,3},{8,12},{12,8},{9,1... | collective-permute-start | bytes 393224 | tf_op jit(solution)/shard_map/ppermute | solution.py:24
  85.5 52.3 %all-to-all-start.4 = ((bf16[64,8,128]{2,1,0:T(8,128)(2,1)}), bf16[64,8,128]{2,1,0:T(8,128)(2,1)S(1)}, u32[]{:S(2)}, u32[]{:S(2)}) async-start(bf16[64,8,128]{2,1,0:T(8,128)(2,1)} %broadcast_in_dim.16), calls=%async_computation.4 | async-start | bytes 262144 | tf_op jit(solution)/shard_map/all_to_all | solution.py:20
  102.0 35.8 %collective-permute-start.6 = (bf16[32,4096]{1,0:T(8,128)(2,1)S(1)}, bf16[32,4096]{1,0:T(8,128)(2,1)S(1)}, u32[]{:S(2)}, u32[]{:S(2)}) collective-permute-start(bf16[32,4096]{1,0:T(8,128)(2,1)S(1)} %pad_maximum_fusion.here_ref), channel_id=1, source_target_pairs={{1,0},{2,1},{3,2},{0,3},{5,4},{6,5},{7,6},{4,7},{9,8},{10,9},{11,1... | collective-permute-start | bytes 786440 | tf_op jit(solution)/shard_map/ppermute | solution.py:174
  107.6 30.2 %collective-permute-start.7 = (bf16[32,4096]{1,0:T(8,128)(2,1)S(1)}, bf16[32,4096]{1,0:T(8,128)(2,1)S(1)}, u32[]{:S(2)}, u32[]{:S(2)}) collective-permute-start(bf16[32,4096]{1,0:T(8,128)(2,1)S(1)} %pad_maximum_fusion.here_ref), channel_id=1, source_target_pairs={{2,0},{3,1},{0,2},{1,3},{6,4},{7,5},{4,6},{5,7},{10,8},{11,9},{8,1... | collective-permute-start | bytes 786440 | tf_op jit(solution)/shard_map/ppermute | solution.py:174
  109.5 28.3 %collective-permute-start.8 = (bf16[32,4096]{1,0:T(8,128)(2,1)S(1)}, bf16[32,4096]{1,0:T(8,128)(2,1)S(1)}, u32[]{:S(2)}, u32[]{:S(2)}) collective-permute-start(bf16[32,4096]{1,0:T(8,128)(2,1)S(1)} %pad_maximum_fusion.here_ref), channel_id=1, source_target_pairs={{3,0},{0,1},{1,2},{2,3},{7,4},{4,5},{5,6},{6,7},{11,8},{8,9},{9,10... | collective-permute-start | bytes 786440 | tf_op jit(solution)/shard_map/ppermute | solution.py:174
Sparse Core Ops, SparseCore 0:
  47.6 79.7 all-gather.1
